TPU v7x, 32 devices: a whole 2x2x4 slice. The times are simulated.
32 devices in a mesh: wide: 8 (over y, x, core), narrow: 4 (over z).
Axes of the slice: x: 2, y: 2, z: 4, core: 2. Of those that a mesh axis runs over, the one named last changes fastest.
Arguments:
- tokens: bfloat16 [16384, 1024], P(('wide', 'narrow')), may hold values from -6 to 6
- w_query: bfloat16 [1024, 1024], P(('wide', 'narrow')), may hold values from -0.0234375 to 0.0234375
- w_key: bfloat16 [1024, 1024], P(('wide', 'narrow')), may hold values from -0.1875 to 0.1875
- w_value: bfloat16 [1024, 1024], P(('wide', 'narrow')), may hold values from -0.1875 to 0.1875
- w_output: bfloat16 [1024, 1024], P(('wide', 'narrow')), may hold values from -1.5 to 1.5
- w_gate: bfloat16 [1024, 2816], P(('wide', 'narrow')), may hold values from -0.1875 to 0.1875
- w_up: bfloat16 [1024, 2816], P(('wide', 'narrow')), may hold values from -0.1875 to 0.1875
- w_down: bfloat16 [2816, 1024], P(('wide', 'narrow')), may hold values from -0.109375 to 0.109375
- gain_attn: bfloat16 [1024], P(('wide', 'narrow')), may hold values from 0.5 to 1.5
- gain_ffn: bfloat16 [1024], P(('wide', 'narrow')), may hold values from 0.5 to 1.5
- rel_table: bfloat16 [512], P(('wide', 'narrow')), may hold values from -4 to 4
- lay_table: bfloat16 [512], P(('wide', 'narrow')), may hold values from -4 to 4
- ocr_counts: int32 [32], P(('wide', 'narrow')), may hold values from 50 to 316, as said below
- rel_bucket: int32 [16384, 512], P(('wide', 'narrow')), may hold values from 0 to 31
- lay_bucket: int32 [16384, 512], P(('wide', 'narrow')), may hold values from 0 to 31
- cotangent: bfloat16 [16384, 1024], P(('wide', 'narrow')), may hold values from -6 to 6
Outputs:
- output: bfloat16 [16384, 1024], P(('wide', 'narrow'))
- grad_tokens: float32 [16384, 1024], P(('wide', 'narrow'))
- grad_query: float32 [1024, 1024], P(('wide', 'narrow'))
- grad_key: float32 [1024, 1024], P(('wide', 'narrow'))
- grad_value: float32 [1024, 1024], P(('wide', 'narrow'))
- grad_output: float32 [1024, 1024], P(('wide', 'narrow'))
- grad_gate: float32 [1024, 2816], P(('wide', 'narrow'))
- grad_up: float32 [1024, 2816], P(('wide', 'narrow'))
- grad_down: float32 [2816, 1024], P(('wide', 'narrow'))
- grad_gain_attn: float32 [1024], P(('wide', 'narrow'))
- grad_gain_ffn: float32 [1024], P(('wide', 'narrow'))
- grad_rel: float32 [512], P(('wide', 'narrow'))
- grad_lay: float32 [512], P(('wide', 'narrow'))
Inputs may be any that keep to these rules, and one draw needn't show every extreme that they name: `ocr_counts`: one page in every draw holds exactly 316 OCR tokens.
All inputs are finite; a program needn't handle non-finite values.
Results may differ from a plain program's by a relative error of at most 0.035.
Values may be sent and summed in bfloat16 or wider, within the bound.
A program may use at most 320 MiB of HBM per device.

v0:
```python
import jax
import jax.numpy as jnp
from jax import lax
from jax.sharding import PartitionSpec as P

H = 16
HD = 64
NB = 32
IMG = 196


RMS_EPSILON = 1e-06
MASK_SCORE = -1000000000.0
HEAD_GROUP = 4


def rms_scale(values, gain):
    return (
        values * lax.rsqrt(jnp.mean(values * values, axis=-1, keepdims=True) + RMS_EPSILON) * gain
    )


def gated_product(gate_act, up_proj):
    return jax.nn.gelu(gate_act, approximate=True) * up_proj


def product(left, right):
    return jnp.dot(left, right, preferred_element_type=jnp.float32)


def contract_rows(left, right):
    return lax.dot_general(
        left, right, (((0,), (0,)), ((), ())), preferred_element_type=jnp.float32
    )


def contract_cols(left, right):
    return lax.dot_general(
        left, right, (((1,), (1,)), ((), ())), preferred_element_type=jnp.float32
    )


def split_heads(matrix):
    return jnp.moveaxis(matrix.reshape(matrix.shape[0], H // HEAD_GROUP, HEAD_GROUP, HD), 1, 0)


def join_heads(stacked):
    return jnp.moveaxis(stacked, 0, 1).reshape(stacked.shape[1], H * HD)


def group_tables(table_all):
    return jnp.moveaxis(table_all.reshape(2 * NB, H // HEAD_GROUP, HEAD_GROUP), 1, 0)


def group_scores(query_group, key_group, table_group, onehot, valid):
    scores = jnp.einsum("ihd,jhd->hij", query_group, key_group, preferred_element_type=jnp.float32)
    scores = scores + jnp.einsum(
        "ijb,bh->hij", onehot, table_group, preferred_element_type=jnp.float32
    )
    return jnp.where(valid[None, None, :], scores, MASK_SCORE)


def gather_weights(
    w_query,
    w_key,
    w_value,
    w_output,
    w_gate,
    w_up,
    w_down,
    gain_attn,
    gain_ffn,
    rel_table,
    lay_table,
):
    return (
        lax.all_gather(w_query, ("wide", "narrow"), axis=0, tiled=True),
        lax.all_gather(w_key, ("wide", "narrow"), axis=0, tiled=True),
        lax.all_gather(w_value, ("wide", "narrow"), axis=0, tiled=True),
        lax.all_gather(w_output, ("wide", "narrow"), axis=0, tiled=True),
        lax.all_gather(w_gate, ("wide", "narrow"), axis=0, tiled=True),
        lax.all_gather(w_up, ("wide", "narrow"), axis=0, tiled=True),
        lax.all_gather(w_down, ("wide", "narrow"), axis=0, tiled=True),
        lax.all_gather(gain_attn, ("wide", "narrow"), axis=0, tiled=True),
        lax.all_gather(gain_ffn, ("wide", "narrow"), axis=0, tiled=True),
        lax.all_gather(rel_table, ("wide", "narrow"), axis=0, tiled=True),
        lax.all_gather(lay_table, ("wide", "narrow"), axis=0, tiled=True),
    )


def table_pair(full_rel, full_lay):
    return jnp.concatenate([full_rel.reshape(NB, H), full_lay.reshape(NB, H)], axis=0)


def forward_pass(tokens_f, weights, onehot, valid):
    (
        full_query,
        full_key,
        full_value,
        full_output,
        full_gate,
        full_up,
        full_down,
        full_gain_attn,
        full_gain_ffn,
        full_rel,
        full_lay,
    ) = weights
    normed_attn = rms_scale(tokens_f, full_gain_attn.astype(jnp.float32)).astype(jnp.bfloat16)
    queries = product(normed_attn, full_query).astype(jnp.bfloat16)
    keys_all = product(normed_attn, full_key).astype(jnp.bfloat16)
    values_all = product(normed_attn, full_value).astype(jnp.bfloat16)

    def forward_one_group(operands):
        query_group, key_group, value_group, table_group = operands
        scores = group_scores(query_group, key_group, table_group, onehot, valid)
        peak = jnp.max(scores, axis=-1, keepdims=True)
        expo = jnp.exp(scores - peak)
        total = jnp.sum(expo, axis=-1, keepdims=True)
        probs_low = (expo / total).astype(jnp.bfloat16)
        attended_group = jnp.einsum(
            "hij,jhd->ihd", probs_low, value_group, preferred_element_type=jnp.float32
        )
        return (attended_group.astype(jnp.bfloat16), (peak + jnp.log(total))[..., 0])

    stacked, log_totals = lax.map(
        forward_one_group,
        (
            split_heads(queries),
            split_heads(keys_all),
            split_heads(values_all),
            group_tables(table_pair(full_rel, full_lay)),
        ),
    )
    attended = join_heads(stacked)
    hidden_one = tokens_f + product(attended, full_output)
    normed_ffn = rms_scale(hidden_one, full_gain_ffn.astype(jnp.float32)).astype(jnp.bfloat16)
    gate_act = product(normed_ffn, full_gate)
    up_proj = product(normed_ffn, full_up)
    mixed = gated_product(gate_act, up_proj).astype(jnp.bfloat16)
    result = hidden_one + product(mixed, full_down)
    return (
        result,
        (
            normed_attn,
            queries,
            keys_all,
            values_all,
            log_totals,
            attended,
            hidden_one,
            normed_ffn,
            gate_act,
            up_proj,
            mixed,
        ),
    )


def attention_backward(
    queries, keys_all, values_all, log_totals, grad_attended, table_all, onehot, valid
):

    def attention_one_group(operands):
        query_group, key_group, value_group, table_group, lse_group, grad_group = operands
        scores = group_scores(query_group, key_group, table_group, onehot, valid)
        probs = jnp.exp(scores - lse_group[..., None])
        probs_low = probs.astype(jnp.bfloat16)
        grad_values = jnp.einsum(
            "hij,ihd->jhd", probs_low, grad_group, preferred_element_type=jnp.float32
        )
        grad_probs = jnp.einsum(
            "ihd,jhd->hij", grad_group, value_group, preferred_element_type=jnp.float32
        )
        grad_scores = (
            probs * (grad_probs - jnp.sum(probs * grad_probs, axis=-1, keepdims=True))
        ).astype(jnp.bfloat16)
        grad_queries = jnp.einsum(
            "hij,jhd->ihd", grad_scores, key_group, preferred_element_type=jnp.float32
        )
        grad_keys = jnp.einsum(
            "hij,ihd->jhd", grad_scores, query_group, preferred_element_type=jnp.float32
        )
        grad_table = jnp.einsum(
            "hij,ijb->bh", grad_scores, onehot, preferred_element_type=jnp.float32
        )
        return (
            grad_queries.astype(jnp.bfloat16),
            grad_keys.astype(jnp.bfloat16),
            grad_values.astype(jnp.bfloat16),
            grad_table,
        )

    grad_q_all, grad_k_all, grad_v_all, grad_tables = lax.map(
        attention_one_group,
        (
            split_heads(queries),
            split_heads(keys_all),
            split_heads(values_all),
            group_tables(table_all),
            log_totals,
            split_heads(grad_attended),
        ),
    )
    grad_table_all = jnp.moveaxis(grad_tables, 0, 1).reshape(2 * NB, H)
    return (join_heads(grad_q_all), join_heads(grad_k_all), join_heads(grad_v_all), grad_table_all)


def local(
    tokens,
    w_query,
    w_key,
    w_value,
    w_output,
    w_gate,
    w_up,
    w_down,
    gain_attn,
    gain_ffn,
    rel_table,
    lay_table,
    ocr_counts,
    rel_bucket,
    lay_bucket,
    cotangent,
):
    slot = tokens.shape[0]
    valid = jnp.arange(slot) < ocr_counts[0] + IMG
    buckets = jnp.arange(NB)
    onehot = jnp.concatenate(
        [
            (rel_bucket[:, :, None] == buckets).astype(jnp.bfloat16),
            (lay_bucket[:, :, None] == buckets).astype(jnp.bfloat16),
        ],
        axis=2,
    )
    tokens_f = tokens.astype(jnp.float32)
    weights = gather_weights(
        w_query,
        w_key,
        w_value,
        w_output,
        w_gate,
        w_up,
        w_down,
        gain_attn,
        gain_ffn,
        rel_table,
        lay_table,
    )
    result, saved = forward_pass(tokens_f, weights, onehot, valid)
    output = jnp.where(valid[:, None], result, 0.0).astype(jnp.bfloat16)
    weights = gather_weights(
        w_query,
        w_key,
        w_value,
        w_output,
        w_gate,
        w_up,
        w_down,
        gain_attn,
        gain_ffn,
        rel_table,
        lay_table,
    )
    result_again, saved = forward_pass(tokens_f, weights, onehot, valid)
    (
        full_query,
        full_key,
        full_value,
        full_output,
        full_gate,
        full_up,
        full_down,
        full_gain_attn,
        full_gain_ffn,
        full_rel,
        full_lay,
    ) = weights
    (
        normed_attn,
        queries,
        keys_all,
        values_all,
        log_totals,
        attended,
        hidden_one,
        normed_ffn,
        gate_act,
        up_proj,
        mixed,
    ) = saved
    grad_result = jnp.where(valid[:, None], cotangent.astype(jnp.float32), 0.0)
    grad_low = grad_result.astype(jnp.bfloat16)
    grad_down = contract_rows(mixed, grad_low)
    grad_mixed = contract_cols(grad_low, full_down)
    gated_value, gated_pull = jax.vjp(gated_product, gate_act, up_proj)
    grad_gate_act, grad_up_proj = gated_pull(grad_mixed)
    gate_low = grad_gate_act.astype(jnp.bfloat16)
    up_low = grad_up_proj.astype(jnp.bfloat16)
    grad_gate = contract_rows(normed_ffn, gate_low)
    grad_up = contract_rows(normed_ffn, up_low)
    grad_normed_ffn = contract_cols(gate_low, full_gate) + contract_cols(up_low, full_up)
    norm_value, norm_pull = jax.vjp(rms_scale, hidden_one, full_gain_ffn.astype(jnp.float32))
    grad_hidden_part, grad_gain_ffn = norm_pull(grad_normed_ffn)
    grad_hidden = grad_result + grad_hidden_part
    branch_low = grad_hidden.astype(jnp.bfloat16)
    grad_output = contract_rows(attended, branch_low)
    grad_attended = contract_cols(branch_low, full_output).astype(jnp.bfloat16)
    grad_queries, grad_keys, grad_values, grad_table_all = attention_backward(
        queries,
        keys_all,
        values_all,
        log_totals,
        grad_attended,
        table_pair(full_rel, full_lay),
        onehot,
        valid,
    )
    grad_rel = grad_table_all[:NB].reshape(NB * H)
    grad_lay = grad_table_all[NB:].reshape(NB * H)
    grad_query = contract_rows(normed_attn, grad_queries)
    grad_key = contract_rows(normed_attn, grad_keys)
    grad_value = contract_rows(normed_attn, grad_values)
    grad_normed_attn = (
        contract_cols(grad_queries, full_query)
        + contract_cols(grad_keys, full_key)
        + contract_cols(grad_values, full_value)
    )
    input_value, input_pull = jax.vjp(rms_scale, tokens_f, full_gain_attn.astype(jnp.float32))
    grad_input_part, grad_gain_attn = input_pull(grad_normed_attn)
    grad_tokens = grad_hidden + grad_input_part
    owned = (
        lax.psum_scatter(grad_query, ("wide", "narrow"), scatter_dimension=0, tiled=True),
        lax.psum_scatter(grad_key, ("wide", "narrow"), scatter_dimension=0, tiled=True),
        lax.psum_scatter(grad_value, ("wide", "narrow"), scatter_dimension=0, tiled=True),
        lax.psum_scatter(grad_output, ("wide", "narrow"), scatter_dimension=0, tiled=True),
        lax.psum_scatter(grad_gate, ("wide", "narrow"), scatter_dimension=0, tiled=True),
        lax.psum_scatter(grad_up, ("wide", "narrow"), scatter_dimension=0, tiled=True),
        lax.psum_scatter(grad_down, ("wide", "narrow"), scatter_dimension=0, tiled=True),
        lax.psum_scatter(grad_gain_attn, ("wide", "narrow"), scatter_dimension=0, tiled=True),
        lax.psum_scatter(grad_gain_ffn, ("wide", "narrow"), scatter_dimension=0, tiled=True),
        lax.psum_scatter(grad_rel, ("wide", "narrow"), scatter_dimension=0, tiled=True),
        lax.psum_scatter(grad_lay, ("wide", "narrow"), scatter_dimension=0, tiled=True),
    )
    return (
        output,
        grad_tokens,
        owned[0],
        owned[1],
        owned[2],
        owned[3],
        owned[4],
        owned[5],
        owned[6],
        owned[7],
        owned[8],
        owned[9],
        owned[10],
    )


def solution(mesh):
    placed = (
        P(("wide", "narrow"), None),
        P(("wide", "narrow"), None),
        P(("wide", "narrow"), None),
        P(("wide", "narrow"), None),
        P(("wide", "narrow"), None),
        P(("wide", "narrow"), None),
        P(("wide", "narrow"), None),
        P(("wide", "narrow"), None),
        P(("wide", "narrow")),
        P(("wide", "narrow")),
        P(("wide", "narrow")),
        P(("wide", "narrow")),
        P(("wide", "narrow")),
        P(("wide", "narrow"), None),
        P(("wide", "narrow"), None),
        P(("wide", "narrow"), None),
    )
    return jax.shard_map(
        local,
        mesh=mesh,
        in_specs=placed,
        out_specs=(
            P(("wide", "narrow"), None),
            P(("wide", "narrow"), None),
            P(("wide", "narrow"), None),
            P(("wide", "narrow"), None),
            P(("wide", "narrow"), None),
            P(("wide", "narrow"), None),
            P(("wide", "narrow"), None),
            P(("wide", "narrow"), None),
            P(("wide", "narrow"), None),
            P(("wide", "narrow")),
            P(("wide", "narrow")),
            P(("wide", "narrow")),
            P(("wide", "narrow")),
        ),
        check_vma=False,
    )
```

profile of v0, /device:TPU:0, one launch (start us, length us, event | category | flops | bytes accessed | tf_op | source)
XLA Modules:
  0.0 2067.6 jit_solution(8038425684361716998)
XLA Ops:
  15.4 42.2 %all-reduce.9 = (bf16[1024]{0:T(1024)(128)(2,1)S(1)}, bf16[512]{0:T(512)(128)(2,1)S(1)}, bf16[512]{0:T(512)(128)(2,1)S(1)}, bf16[1024]{0:T(1024)(128)(2,1)S(1)}) all-reduce(bf16[1024]{0:T(1024)(128)(2,1)S(1)} %dynamic-update-slice, bf16[512]{0:T(512)(128)(2,1)S(1)} %dynamic-update-slice.2, ...), channel_id=1, replica_groups=mesh['wide'=8,'narrow'=4] {'wide','narrow'}, use_global_device_ids=true, to_apply=%add | all-reduce | flops 3072 | bytes 12288
  72.5 16.3 add_convert_fusion
  93.1 35.4 %all-gather.10.cloned.1.call-done = bf16[1024,1024]{1,0:T(8,128)(2,1)} async-done(((bf16[32,1024]{1,0:T(8,128)(2,1)}), bf16[1024,1024]{1,0:T(8,128)(2,1)}) %all-gather.10.cloned.1.call-update) | async-done | bytes 2097168 | tf_op jit(solution)/shard_map/all_gather | solution.py:77
  132.0 54.9 %all-gather.12.cloned.1.call-done = bf16[1024,1024]{1,0:T(8,128)(2,1)} async-done(((bf16[32,1024]{1,0:T(8,128)(2,1)}), bf16[1024,1024]{1,0:T(8,128)(2,1)}) %all-gather.12.cloned.1.call-update) | async-done | bytes 2097168 | tf_op jit(solution)/shard_map/all_gather | solution.py:78
  193.3 107.8 %while.42 = (s32[]{:T(128)}, bf16[4,512,4,64]{1,3,2,0:T(8,128)(2,1)}, f32[4,4,512]{2,1,0:T(4,128)S(1)}, bf16[4,512,4,64]{1,3,2,0:T(8,128)(2,1)}, bf16[4,512,4,64...) while((s32[]{:T(128)}, ...), condition=%wide.region_9.10_spmd.clone, body=%wide.region_6.9_spmd.clone.sunk | while | flops 411171328 | bytes 64032888 | solution.py:126
  219.9 15.3 fusion.242
  246.9 15.1 fusion.242
  273.6 15.0 fusion.242
  321.4 61.5 %all-gather.18.cloned.1.call-done = bf16[1024,2816]{1,0:T(8,128)(2,1)} async-done(((bf16[32,2816]{1,0:T(8,128)(2,1)}), bf16[1024,2816]{1,0:T(8,128)(2,1)}) %all-gather.18.cloned.1.call-update) | async-done | bytes 5767184 | tf_op jit(solution)/shard_map/all_gather | solution.py:82
  390.6 61.5 %all-gather.20.cloned.1.call-done = bf16[2816,1024]{1,0:T(8,128)(2,1)} async-done(((bf16[88,1024]{1,0:T(8,128)(2,1)}), bf16[2816,1024]{1,0:T(8,128)(2,1)}) %all-gather.20.cloned.1.call-update) | async-done | bytes 5767184 | tf_op jit(solution)/shard_map/all_gather | solution.py:83
  484.9 221.5 %while.43 = (s32[]{:T(128)}, bf16[4,512,4,64]{1,3,2,0:T(8,128)(2,1)}, bf16[4,512,4,64]{1,3,2,0:T(8,128)(2,1)}, bf16[4,512,4,64]{1,3,2,0:T(8,128)(2,1)}, f32[4,64...) while((s32[]{:T(128)}, ...), condition=%wide.region_14.15_spmd.clone, body=%wide.region_12.14_spmd.clone.sunk | while | flops 949352960 | bytes 157861184 | solution.py:194
  524.8 15.6 fusion.263
  580.1 15.6 fusion.263
  635.4 15.6 fusion.263
  690.7 15.6 fusion.263
  761.7 139.0 %while.41 = (s32[]{:T(128)}, bf16[4,512,4,64]{1,3,2,0:T(8,128)(2,1)}, bf16[4,512,4,64]{1,3,2,0:T(8,128)(2,1)}, bf16[4,512,4,64]{1,3,2,0:T(8,128)(2,1)S(1)}, bf16...) while((s32[]{:T(128)}, ...), condition=%wide.region_4.5_spmd.clone, body=%wide.region_1.4_spmd.clone.sunk | while | flops 546442752 | bytes 68703856 | solution.py:126
  762.1 15.0 fusion.236
  914.0 41.2 %all-reduce.8 = (f32[1024]{0:T(1024)S(1)}, f32[1024]{0:T(1024)S(1)}, f32[512]{0:T(512)S(1)}, f32[512]{0:T(512)S(1)}) all-reduce(f32[1024]{0:T(1024)S(1)} %get-tuple-element.281, f32[1024]{0:T(1024)S(1)} %copy-done.29, f32[512]{0:T(512)S(1)} %reshape.179, ...), channel_id=9, replica_groups=mesh['wide'=8,'narrow'=4] {'wide','narrow'}, use_global_device_ids=true, to_apply=%region_24.25.clone | all-reduce | flops 3072 | bytes 24576
  984.0 22.9 %reduce-scatter.10.cloned.1.call-done = f32[32,1024]{1,0:T(8,128)} async-done(((f32[1024,1024]{1,0:T(8,128)}), f32[32,1024]{1,0:T(8,128)}) %reduce-scatter.10.cloned.1.call-update) | async-done | bytes 131088 | tf_op jit(solution)/shard_map/reduce_scatter | solution.py:335
  1007.0 149.6 %reduce-scatter.12.cloned.1.call-done = f32[32,1024]{1,0:T(8,128)} async-done(((f32[1024,1024]{1,0:T(8,128)}), f32[32,1024]{1,0:T(8,128)}) %reduce-scatter.12.cloned.1.call-update) | async-done | bytes 131088 | tf_op jit(solution)/shard_map/reduce_scatter | solution.py:336
  1156.6 149.7 %reduce-scatter.14.cloned.1.call-done = f32[32,1024]{1,0:T(8,128)} async-done(((f32[1024,1024]{1,0:T(8,128)}), f32[32,1024]{1,0:T(8,128)}) %reduce-scatter.14.cloned.1.call-update) | async-done | bytes 131088 | tf_op jit(solution)/shard_map/reduce_scatter | solution.py:337
  1306.3 252.0 %reduce-scatter.16.cloned.1.call-done = f32[32,2816]{1,0:T(8,128)} async-done(((f32[1024,2816]{1,0:T(8,128)}), f32[32,2816]{1,0:T(8,128)}) %reduce-scatter.16.cloned.1.call-update) | async-done | bytes 360464 | tf_op jit(solution)/shard_map/reduce_scatter | solution.py:338
  1558.3 251.3 %reduce-scatter.18.cloned.1.call-done = f32[32,2816]{1,0:T(8,128)} async-done(((f32[1024,2816]{1,0:T(8,128)}), f32[32,2816]{1,0:T(8,128)}) %reduce-scatter.18.cloned.1.call-update) | async-done | bytes 360464 | tf_op jit(solution)/shard_map/reduce_scatter | solution.py:339
  1809.6 251.2 %reduce-scatter.20.cloned.1.call-done = f32[88,1024]{1,0:T(8,128)} async-done(((f32[2816,1024]{1,0:T(8,128)}), f32[88,1024]{1,0:T(8,128)}) %reduce-scatter.20.cloned.1.call-update) | async-done | bytes 360464 | tf_op jit(solution)/shard_map/reduce_scatter | solution.py:340
  (295 shorter events, 538.3 us)
Async XLA Ops:
  7.2 81.7 %all-gather.8.cloned.1.call-start = ((), (), s32[]{:S(2)}) async-start(), calls=%async_computation.7 | async-start | bytes 2162688 | tf_op jit(solution)/shard_map/all_gather | solution.py:79
  7.9 120.6 %all-gather.10.cloned.1.call-start = ((), (), s32[]{:S(2)}) async-start(), calls=%async_computation.8 | async-start | bytes 2162688 | tf_op jit(solution)/shard_map/all_gather | solution.py:77
  8.7 178.2 %all-gather.12.cloned.1.call-start = ((), (), s32[]{:S(2)}) async-start(), calls=%async_computation.9 | async-start | bytes 2162688 | tf_op jit(solution)/shard_map/all_gather | solution.py:78
  9.4 291.7 %all-gather.14.cloned.1.call-start = ((), (), s32[]{:S(2)}) async-start(), calls=%async_computation.10 | async-start | bytes 2162688 | tf_op jit(solution)/shard_map/all_gather | solution.py:80
  10.0 303.9 %all-gather.16.cloned.1.call-start = ((), (), s32[]{:S(2)}) async-start(), calls=%async_computation.11 | async-start | bytes 5947392 | tf_op jit(solution)/shard_map/all_gather | solution.py:81
  10.6 372.3 %all-gather.18.cloned.1.call-start = ((), (), s32[]{:S(2)}) async-start(), calls=%async_computation.12 | async-start | bytes 5947392 | tf_op jit(solution)/shard_map/all_gather | solution.py:82
  11.1 440.9 %all-gather.20.cloned.1.call-start = ((), (), s32[]{:S(2)}) async-start(), calls=%async_computation.13 | async-start | bytes 5947392 | tf_op jit(solution)/shard_map/all_gather | solution.py:83
  11.9 972.2 %reduce-scatter.8.cloned.1.call-start = ((), (), s32[]{:S(2)}) async-start(), calls=%async_computation.14 | async-start | bytes 4325376 | tf_op jit(solution)/shard_map/reduce_scatter | solution.py:334
  57.6 129.2 %copy-start.18 = (f32[1024]{0:T(1024)}, f32[1024]{0:T(1024)S(1)}, u32[]{:S(2)}) copy-start(f32[1024]{0:T(1024)S(1)} %convert_element_type.107) | copy-start | bytes 12292
  59.1 127.7 %copy-start.26 = (f32[512]{0:T(512)}, f32[512]{0:T(512)S(1)}, u32[]{:S(2)}) copy-start(f32[512]{0:T(512)S(1)} %fusion.114) | copy-start | bytes 6148
  60.3 415.5 %copy-start.30 = (pred[512]{0:T(512)(128)(4,1)}, pred[512]{0:T(512)(128)(4,1)S(1)}, u32[]{:S(2)}) copy-start(pred[512]{0:T(512)(128)(4,1)S(1)} %iota_compare_fusion.5) | copy-start | bytes 1540
  60.3 415.5 %copy-start.21 = (f32[1024]{0:T(1024)}, f32[1024]{0:T(1024)S(1)}, u32[]{:S(2)}) copy-start(f32[1024]{0:T(1024)S(1)} %convert_element_type.112) | copy-start | bytes 12292
  306.0 76.9 %copy-start.14 = (bf16[512,1024]{1,0:T(8,128)(2,1)}, bf16[512,1024]{1,0:T(8,128)(2,1)S(1)}, u32[]{:S(2)}) copy-start(bf16[512,1024]{1,0:T(8,128)(2,1)S(1)} %multiply_convert_fusion.4) | copy-start | bytes 3145732
  484.9 221.5 %copy-start.19 = (f32[1024]{0:T(1024)S(1)}, f32[1024]{0:T(1024)}, u32[]{:S(2)}) copy-start(f32[1024]{0:T(1024)} %copy-done.18) | copy-start | bytes 12292
  484.9 221.5 %copy-start.27 = (f32[512]{0:T(512)S(1)}, f32[512]{0:T(512)}, u32[]{:S(2)}) copy-start(f32[512]{0:T(512)} %copy-done.26) | copy-start | bytes 6148
  540.4 24.3 %copy-start.1 = (bf16[4,512,4,64]{1,3,2,0:T(8,128)(2,1)}, bf16[4,512,4,64]{1,3,2,0:T(8,128)(2,1)S(1)}, u32[]{:S(2)}) copy-start(bf16[4,512,4,64]{1,3,2,0:T(8,128)(2,1)S(1)} %get-tuple-element.648) | copy-start | bytes 3145732 | tf_op jit(solution)/shard_map/while
  711.3 295.7 %reduce-scatter.10.cloned.1.call-start = ((), (), s32[]{:S(2)}) async-start(), calls=%async_computation.15 | async-start | bytes 4325376 | tf_op jit(solution)/shard_map/reduce_scatter | solution.py:335
  717.2 439.4 %reduce-scatter.12.cloned.1.call-start = ((), (), s32[]{:S(2)}) async-start(), calls=%async_computation.16 | async-start | bytes 4325376 | tf_op jit(solution)/shard_map/reduce_scatter | solution.py:336
  722.2 584.1 %reduce-scatter.14.cloned.1.call-start = ((), (), s32[]{:S(2)}) async-start(), calls=%async_computation.17 | async-start | bytes 4325376 | tf_op jit(solution)/shard_map/reduce_scatter | solution.py:337
  727.5 830.8 %reduce-scatter.16.cloned.1.call-start = ((), (), s32[]{:S(2)}) async-start(), calls=%async_computation.18 | async-start | bytes 11894784 | tf_op jit(solution)/shard_map/reduce_scatter | solution.py:338
  737.1 1072.5 %reduce-scatter.18.cloned.1.call-start = ((), (), s32[]{:S(2)}) async-start(), calls=%async_computation.19 | async-start | bytes 11894784 | tf_op jit(solution)/shard_map/reduce_scatter | solution.py:339
  746.7 1314.1 %reduce-scatter.20.cloned.1.call-start = ((), (), s32[]{:S(2)}) async-start(), calls=%async_computation.20 | async-start | bytes 11894784 | tf_op jit(solution)/shard_map/reduce_scatter | solution.py:340
  910.9 46.6 %copy-start.25 = (f32[512]{0:T(512)S(1)}, f32[512]{0:T(512)}, u32[]{:S(2)}) copy-start(f32[512]{0:T(512)} %copy-done.24) | copy-start | bytes 6148
  914.0 47.6 %copy-start.22 = (f32[1024]{0:T(1024)S(1)}, f32[1024]{0:T(1024)}, u32[]{:S(2)}) copy-start(f32[1024]{0:T(1024)} %copy-done.21) | copy-start | bytes 12292
  (41 other events, 387.3 us)
Sparse Core Ops, SparseCore 0:
  10.9 59.1 all-gather.7
  73.1 55.4 all-gather.9
  131.5 55.3 all-gather.11
  189.6 55.3 all-gather.13
  247.7 66.1 all-gather.15
  316.6 66.2 all-gather.17
  385.7 66.2 all-gather.19
  711.5 146.5 reduce-scatter.7
  860.9 146.0 reduce-scatter.9
  1009.7 146.8 reduce-scatter.11
  1159.5 146.8 reduce-scatter.13
  1309.1 249.1 reduce-scatter.15
  1561.2 248.4 reduce-scatter.17
  1812.4 248.4 reduce-scatter.19
where the time goes:
time: 2080 us; the launch traced here: 2070 us
  waiting for transfers between devices  1300 us (62%)
  matrix products  524 us (25%)
  local copies, waits for them, and re-layouts  98.1 us (5%)
  blocking collectives  83.4 us (4%)
  other arithmetic  42.1 us (2%)
    reduce_scatter x1, waiting for transfers between devices, local(): lax.psum_scatter(grad_gate, ('wide', 'narrow'), scatter_dimension=0, tile...  252 us
    reduce_scatter x1, waiting for transfers between devices, local(): lax.psum_scatter(grad_up, ('wide', 'narrow'), scatter_dimension=0, tiled=...  251 us
    reduce_scatter x1, waiting for transfers between devices, local(): lax.psum_scatter(grad_down, ('wide', 'narrow'), scatter_dimension=0, tile...  251 us
    dot_general x12, matrix products, group_scores(): jnp.einsum('ijb,bh->hij', onehot, table_group, preferred_element_type=jnp...  181 us
    reduce_scatter x1, waiting for transfers between devices, local(): lax.psum_scatter(grad_output, ('wide', 'narrow'), scatter_dimension=0, ti...  150 us
    reduce_scatter x1, waiting for transfers between devices, local(): lax.psum_scatter(grad_value, ('wide', 'narrow'), scatter_dimension=0, til...  150 us
    unnamed x2, blocking collectives  83.4 us
    dot_general x12, local copies, waits for them, and re-layouts, group_scores(): jnp.einsum('ijb,bh->hij', onehot, table_group, preferred_element_type=jnp...  63.5 us
  transfers between devices with their start and end apart: 14, of which 11 were waited for; matrix products, arithmetic and copies ran while one was open for 19% of the time, Pallas kernels for 0%

commit v1 on v0

--- a/solution.py
+++ b/solution.py
@@ -1,12 +1,18 @@
+import functools
+
 import jax
 import jax.numpy as jnp
 from jax import lax
+from jax.experimental import pallas as pl
+from jax.experimental.pallas import tpu as pltpu
 from jax.sharding import PartitionSpec as P
 
 H = 16
 HD = 64
 NB = 32
 IMG = 196
+RING = 6
+SCATTER_COPIES = 10
 
 
 RMS_EPSILON = 1e-06
@@ -206,7 +212,582 @@
     return (join_heads(grad_q_all), join_heads(grad_k_all), join_heads(grad_v_all), grad_table_all)
 
 
+MESH_ID = pl.DeviceIdType.MESH
+BF = jnp.bfloat16
+F32 = jnp.float32
+X_BIT = 2
+Y_BIT = 4
+PARTS = ((X_BIT, Y_BIT), (Y_BIT, X_BIT))
+
+
+class Links:
+    def __init__(self, nn, send_sem, recv_sem):
+        self.nn = nn
+        self.w = lax.axis_index("wide")
+        self.z = lax.axis_index("narrow")
+        self.send_sem = send_sem
+        self.recv_sem = recv_sem
+        self.used = 0
+        self.sent = []
+
+    def fresh(self):
+        self.used += 1
+        return self.used - 1
+
+    def wide(self, bit):
+        return (jnp.bitwise_xor(self.w, bit), self.z)
+
+    def along(self, step):
+        return (self.w, lax.rem(self.z + step, self.nn))
+
+    def copy(self, src, dst, number, device):
+        return pltpu.make_async_remote_copy(
+            src_ref=src,
+            dst_ref=dst,
+            send_sem=self.send_sem.at[number],
+            recv_sem=self.recv_sem.at[number],
+            device_id=device,
+            device_id_type=MESH_ID,
+        )
+
+    def send(self, src, dst, number, device):
+        copy = self.copy(src, dst, number, device)
+        copy.start()
+        self.sent.append(copy)
+
+    def greet(self):
+        barrier = pltpu.get_barrier_semaphore()
+        others = [self.wide(bit) for bit in (1, X_BIT, Y_BIT)]
+        others += [self.along(step) for step in range(1, self.nn)]
+        for other in others:
+            pl.semaphore_signal(barrier, inc=1, device_id=other, device_id_type=MESH_ID)
+        pl.semaphore_wait(barrier, len(others))
+
+    def finish(self):
+        for copy in self.sent:
+            copy.wait_send()
+
+
+class Gather:
+    def __init__(self, links, shard, full, rows, parts, local_sem, line=None, merged=None):
+        self.links, self.shard, self.full, self.rows, self.parts = links, shard, full, rows, parts
+        self.local_sem, self.line, self.merged = local_sem, line, merged
+        nn = links.nn
+        self.block = rows * nn
+        self.line_ids = [links.fresh() for _ in range(1, nn)]
+        self.part_ids = {
+            (p, mask): links.fresh()
+            for p in range(len(parts))
+            for mask in (X_BIT, Y_BIT, X_BIT | Y_BIT)
+        }
+        self.core_ids = {mask: links.fresh() for mask in (0, X_BIT, Y_BIT, X_BIT | Y_BIT)}
+
+    def place(self, w, z):
+        if self.line is not None:
+            return self.line.at[z]
+        return self.full.at[pl.ds((w * self.links.nn + z) * self.rows, self.rows)]
+
+    def span(self, mask, part=None):
+        rows = pl.ds(jnp.bitwise_xor(self.links.w, mask) * self.block, self.block)
+        if part is None:
+            return self.full.at[rows]
+        low, size = self.parts[part][:2]
+        return self.full.at[rows, pl.ds(low, size)]
+
+    def own(self):
+        return pltpu.make_async_copy(
+            self.shard, self.place(self.links.w, self.links.z), self.local_sem
+        )
+
+    def start(self):
+        k = self.links
+        self.own().start()
+        for step in range(1, k.nn):
+            k.send(self.shard, self.place(k.w, k.z), self.line_ids[step - 1], k.along(step))
+
+    def spread(self):
+        k = self.links
+        self.own().wait()
+        for step in range(1, k.nn):
+            came = lax.rem(k.z - step + k.nn, k.nn)
+            k.copy(
+                self.shard, self.place(k.w, came), self.line_ids[step - 1], k.along(step)
+            ).wait_recv()
+        if self.line is not None:
+            whole = jnp.concatenate(
+                [self.line[z, : self.rows].astype(F32) for z in range(k.nn)], axis=0
+            )
+            self.merged[...] = whole.astype(BF)
+            move = pltpu.make_async_copy(self.merged, self.span(0), self.local_sem)
+            move.start()
+            move.wait()
+        for p, part in enumerate(self.parts):
+            for bit in part[2]:
+                k.send(self.span(0, p), self.span(0, p), self.part_ids[p, bit], k.wide(bit))
+        k.send(self.span(0), self.span(0), self.core_ids[0], k.wide(1))
+
+    def arrive(self, p, mask):
+        k = self.links
+        k.copy(
+            self.span(mask, p), self.span(mask, p), self.part_ids[p, mask], k.wide(X_BIT)
+        ).wait_recv()
+
+    def forward(self):
+        k = self.links
+        for p, part in enumerate(self.parts):
+            first, second = part[2]
+            self.arrive(p, first)
+            both = first | second
+            k.send(self.span(first, p), self.span(first, p), self.part_ids[p, both], k.wide(second))
+        for p, part in enumerate(self.parts):
+            self.arrive(p, part[2][1])
+        for mask in (X_BIT, Y_BIT):
+            k.send(self.span(mask), self.span(mask), self.core_ids[mask], k.wide(1))
+
+    def last(self):
+        k = self.links
+        both = X_BIT | Y_BIT
+        for p in range(len(self.parts)):
+            self.arrive(p, both)
+        k.send(self.span(both), self.span(both), self.core_ids[both], k.wide(1))
+
+    def done(self):
+        k = self.links
+        for mask, number in self.core_ids.items():
+            place = self.span(mask | 1)
+            k.copy(place, place, number, k.wide(1)).wait_recv()
+
+
+def halves(columns):
+    low = columns // 256 * 128
+    return ((0, low, PARTS[0]), (low, columns - low, PARTS[1]))
+
+
+def gather_kernel(nn, shapes, *refs):
+    count = len(shapes)
+    shards, fulls = refs[:count], refs[count : 2 * count]
+    line, merged, send_sem, recv_sem, local_sem = refs[2 * count :]
+    links = Links(nn, send_sem, recv_sem)
+    links.greet()
+    gathers = []
+    for index, (rows, columns) in enumerate(shapes):
+        odd = rows % 16 != 0 and columns > 128
+        gathers.append(
+            Gather(
+                links,
+                shards[index],
+                fulls[index],
+                rows,
+                halves(columns) if columns > 128 else ((0, columns, PARTS[0]),),
+                local_sem.at[index],
+                line if odd else None,
+                merged if odd else None,
+            )
+        )
+    gathers[0].start()
+    gathers[1].start()
+    for index in range(count + 3):
+        if index < count:
+            gathers[index].spread()
+            if index + 2 < count:
+                gathers[index + 2].start()
+        if 0 <= index - 1 < count:
+            gathers[index - 1].forward()
+        if 0 <= index - 2 < count:
+            gathers[index - 2].last()
+        if 0 <= index - 3 < count:
+            gathers[index - 3].done()
+    links.finish()
+
+
+def gather_all(nw, nn, shards, odd_rows):
+    devices = nw * nn
+    shapes = []
+    for index, shard in enumerate(shards):
+        rows = odd_rows if index == len(shards) - 1 else shard.shape[0]
+        shapes.append((rows, shard.shape[1]))
+    copies = len(shards) * (nn - 1 + 6 + 4)
+    return pl.pallas_call(
+        functools.partial(gather_kernel, nn, shapes),
+        out_shape=[
+            jax.ShapeDtypeStruct((rows * devices, columns), shard.dtype)
+            for (rows, columns), shard in zip(shapes, shards)
+        ],
+        in_specs=[pl.BlockSpec(memory_space=pl.ANY)] * len(shards),
+        out_specs=[pl.BlockSpec(memory_space=pl.ANY)] * len(shards),
+        scratch_shapes=[
+            pltpu.VMEM((nn,) + shards[-1].shape, BF),
+            pltpu.VMEM((nn * odd_rows, shards[-1].shape[1]), BF),
+            pltpu.SemaphoreType.DMA((copies,)),
+            pltpu.SemaphoreType.DMA((copies,)),
+            pltpu.SemaphoreType.DMA((len(shards),)),
+        ],
+        compiler_params=pltpu.CompilerParams(collective_id=0, has_side_effects=True),
+    )(*shards)
+
+
+class Scatter:
+    def __init__(self, links, chunks, rows, columns, grads, came, slots, base):
+        self.links, self.chunks, self.rows, self.columns = links, chunks, rows, columns
+        self.grads, self.came = grads, came
+        (self.held, self.other, self.round, self.out_line, self.in_line, self.load_sem) = slots
+        self.base = base
+        self.block = rows * links.nn
+        self.parts = halves(columns)
+        self.core = lax.rem(links.w, 2)
+        self.ring = self.held.shape[0]
+
+    def number(self, chunk, kind):
+        return self.base + chunk * SCATTER_COPIES + kind
+
+    def core_copy(self, chunk):
+        return self.links.copy(
+            self.grads.at[chunk, :, 1 - self.core],
+            self.came.at[chunk],
+            self.number(chunk, 0),
+            self.links.wide(1),
+        )
+
+    def trade(self, chunk):
+        self.core_copy(chunk).start()
+
+    def loads(self, chunk):
+        slot, turn = lax.rem(chunk, self.ring), lax.rem(chunk, 2)
+        return (
+            pltpu.make_async_copy(
+                self.grads.at[chunk, :, self.core], self.held.at[slot], self.load_sem.at[turn, 0]
+            ),
+            pltpu.make_async_copy(
+                self.came.at[chunk], self.other.at[turn], self.load_sem.at[turn, 1]
+            ),
+        )
+
+    def fetch(self, chunk):
+        self.core_copy(chunk).wait_recv()
+        for load in self.loads(chunk):
+            load.start()
+
+    def square(self, mask):
+        return jnp.bitwise_xor(self.links.w, mask) // 2
+
+    def hop(self, chunk, p, mask):
+        slot = lax.rem(chunk, self.ring)
+        low, size, order = self.parts[p]
+        bit = order[1] if mask & order[1] else order[0]
+        kind = 1 + p * 3 + (X_BIT, Y_BIT, X_BIT | Y_BIT).index(mask)
+        return self.links.copy(
+            self.held.at[slot, self.square(mask), :, pl.ds(low, size)],
+            self.round.at[slot, kind - 1, :, pl.ds(0, size)],
+            self.number(chunk, kind),
+            self.links.wide(bit),
+        )
+
+    def landed(self, chunk, p, mask):
+        return self.round.at[
+            lax.rem(chunk, self.ring), p * 3 + (X_BIT, Y_BIT, X_BIT | Y_BIT).index(mask)
+        ]
+
+    def add_core(self, chunk):
+        for load in self.loads(chunk):
+            load.wait()
+        slot, turn = lax.rem(chunk, self.ring), lax.rem(chunk, 2)
+
+        def one(square, carry):
+            self.held[slot, square] = (
+                self.held[slot, square].astype(F32) + self.other[turn, square].astype(F32)
+            ).astype(BF)
+            return carry
+
+        lax.fori_loop(0, self.held.shape[1], one, 0)
+        for p, part in enumerate(self.parts):
+            self.hop(chunk, p, X_BIT | Y_BIT).start()
+        for p, part in enumerate(self.parts):
+            self.hop(chunk, p, part[2][1]).start()
+
+    def add_corner(self, chunk):
+        slot = lax.rem(chunk, self.ring)
+        for p, (low, size, order) in enumerate(self.parts):
+            self.hop(chunk, p, X_BIT | Y_BIT).wait_recv()
+            square = self.square(order[0])
+            came = self.landed(chunk, p, X_BIT | Y_BIT)
+            self.held[slot, square, :, low : low + size] = (
+                self.held[slot, square, :, low : low + size].astype(F32)
+                + came[:, :size].astype(F32)
+            ).astype(BF)
+        for p, part in enumerate(self.parts):
+            self.hop(chunk, p, part[2][0]).start()
+
+    def line_copy(self, chunk, step):
+        k = self.links
+        slot = lax.rem(chunk, self.ring)
+        return k.copy(
+            self.out_line.at[slot, lax.rem(k.z + step, k.nn)],
+            self.in_line.at[slot, step - 1],
+            self.number(chunk, 6 + step),
+            k.along(step),
+        )
+
+    def add_square(self, chunk):
+        slot = lax.rem(chunk, self.ring)
+        home = self.square(0)
+        for p, (low, size, order) in enumerate(self.parts):
+            total = self.held[slot, home, :, low : low + size].astype(F32)
+            for mask in order:
+                self.hop(chunk, p, mask).wait_recv()
+                total = total + self.landed(chunk, p, mask)[:, :size].astype(F32)
+            for z in range(self.links.nn):
+                self.out_line[slot, z, : self.rows, low : low + size] = total[
+                    z * self.rows : (z + 1) * self.rows
+                ].astype(BF)
+        for step in range(1, self.links.nn):
+            self.line_copy(chunk, step).start()
+
+    def total(self, chunk):
+        slot = lax.rem(chunk, self.ring)
+        total = self.out_line[slot, self.links.z, : self.rows].astype(F32)
+        for step in range(1, self.links.nn):
+            self.line_copy(chunk, step).wait_recv()
+            total = total + self.in_line[slot, step - 1, : self.rows].astype(F32)
+        return total
+
+    def wait_sent(self, chunk):
+        self.core_copy(chunk).wait_send()
+        for p, part in enumerate(self.parts):
+            for mask in (X_BIT, Y_BIT, X_BIT | Y_BIT):
+                self.hop(chunk, p, mask).wait_send()
+        for step in range(1, self.links.nn):
+            self.line_copy(chunk, step).wait_send()
+
+
+def scatter_kernel(nn, few, many, few_ref, many_ref, small_ref, few_out, many_out, small_out, few_came, many_came, *refs):
+    few_slots, many_slots = refs[:6], refs[6:12]
+    small_came, small_round, small_line, small_mine, send_sem, recv_sem = refs[12:]
+    links = Links(nn, send_sem, recv_sem)
+    links.greet()
+    sets = []
+    base = 0
+    for (chunks, rows, columns), grads, came, slots in (
+        (few, few_ref, few_came, few_slots),
+        (many, many_ref, many_came, many_slots),
+    ):
+        sets.append(Scatter(links, chunks, rows, columns, grads, came, slots, base))
+        base += chunks * SCATTER_COPIES
+    links.used = base
+
+    def run(scatter, out):
+        chunks = scatter.chunks
+
+        def each(chunk, carry):
+            scatter.trade(chunk)
+            return carry
+
+        lax.fori_loop(0, chunks, each, 0)
+
+        def step(index, carry):
+            for lag, action in enumerate(
+                (scatter.fetch, scatter.add_core, scatter.add_corner, scatter.add_square)
+            ):
+                chunk = index - lag
+
+                @pl.when(jnp.logical_and(chunk >= 0, chunk < chunks))
+                def _(chunk=chunk, action=action):
+                    action(chunk)
+
+            chunk = index - 4
+
+            @pl.when(chunk >= 0)
+            def _(chunk=chunk):
+                out[chunk] = scatter.total(chunk)
+                scatter.wait_sent(chunk)
+
+            return carry
+
+        lax.fori_loop(0, chunks + 4, step, 0)
+
+    run(sets[0], few_out)
+    run(sets[1], many_out)
+    scatter_small(links, small_ref, small_out, small_came, small_round, small_line, small_mine)
+    links.finish()
+
+
+def scatter_small(links, grads, out, came, round_in, line_in, mine):
+    core = lax.rem(links.w, 2)
+    home = links.w // 2
+    number = links.fresh()
+    links.send(grads.at[:, 1 - core], came, number, links.wide(1))
+    links.sent[-1].wait_recv()
+    mine[...] = grads[:, core] + came[...]
+    masks = (X_BIT, Y_BIT, X_BIT | Y_BIT)
+    copies = []
+    for index, mask in enumerate(masks):
+        number = links.fresh()
+        links.send(
+            mine.at[jnp.bitwise_xor(links.w, mask) // 2], round_in.at[index], number, links.wide(mask)
+        )
+        copies.append(links.sent[-1])
+    for copy in copies:
+        copy.wait()
+    del links.sent[-3:]
+    mine[home] = mine[home] + round_in[0] + round_in[1] + round_in[2]
+    copies = []
+    for step in range(1, links.nn):
+        number = links.fresh()
+        links.send(
+            mine.at[home, pl.ds(lax.rem(links.z + step, links.nn) * 8, 8)],
+            line_in.at[step - 1],
+            number,
+            links.along(step),
+        )
+        copies.append(links.sent[-1])
+    total = mine[home, pl.ds(pl.multiple_of(links.z * 8, 8), 8)]
+    for step in range(1, links.nn):
+        copies[step - 1].wait_recv()
+        total = total + line_in[step - 1]
+    out[...] = total
+
+
+def padded(rows):
+    return (rows + 15) // 16 * 16
+
+
+def scatter_slots(squares, nn, rows, columns):
+    half = columns // 2
+    return [
+        pltpu.VMEM((RING, squares, nn * rows, columns), BF),
+        pltpu.VMEM((2, squares, nn * rows, columns), BF),
+        pltpu.VMEM((RING, 6, nn * rows, half), BF),
+        pltpu.VMEM((RING, nn, padded(rows), columns), BF),
+        pltpu.VMEM((RING, nn - 1, padded(rows), columns), BF),
+        pltpu.SemaphoreType.DMA((2, 2)),
+    ]
+
+
+def scatter_all(nw, nn, few_grads, many_grads, small):
+    squares = nw // 2
+
+    def facts(grads):
+        return (grads.shape[0], grads.shape[1] // (nw * nn), grads.shape[2])
+
+    few, many = facts(few_grads), facts(many_grads)
+    outs = []
+    for chunks, rows, columns in (few, many):
+        outs.append(jax.ShapeDtypeStruct((chunks, rows, columns), F32))
+    outs.append(jax.ShapeDtypeStruct((8, 128), F32))
+    for chunks, rows, columns in (few, many):
+        outs.append(jax.ShapeDtypeStruct((chunks, squares, nn * rows, columns), BF))
+    copies = (few[0] + many[0]) * SCATTER_COPIES + 16
+    vmem = pl.BlockSpec(memory_space=pltpu.VMEM)
+    hbm = pl.BlockSpec(memory_space=pl.ANY)
+    given = [
+        grads.reshape(grads.shape[0], squares, 2, -1, grads.shape[2])
+        for grads in (few_grads, many_grads)
+    ]
+    return pl.pallas_call(
+        functools.partial(scatter_kernel, nn, few, many),
+        out_shape=outs,
+        in_specs=[hbm, hbm, vmem],
+        out_specs=[vmem, vmem, vmem, hbm, hbm],
+        scratch_shapes=scatter_slots(squares, nn, few[1], few[2])
+        + scatter_slots(squares, nn, many[1], many[2])
+        + [
+            pltpu.VMEM((squares, nn * 8, 128), F32),
+            pltpu.VMEM((3, nn * 8, 128), F32),
+            pltpu.VMEM((nn - 1, 8, 128), F32),
+            pltpu.VMEM((squares, nn * 8, 128), F32),
+            pltpu.SemaphoreType.DMA((copies,)),
+            pltpu.SemaphoreType.DMA((copies,)),
+        ],
+        compiler_params=pltpu.CompilerParams(
+            collective_id=1, has_side_effects=True, vmem_limit_bytes=60 * 2**20
+        ),
+    )(*given, small.reshape(squares, 2, nn * 8, 128))[:3]
+
+def gather_fast(
+    nw,
+    nn,
+    w_query,
+    w_key,
+    w_value,
+    w_output,
+    w_gate,
+    w_up,
+    w_down,
+    gain_attn,
+    gain_ffn,
+    rel_table,
+    lay_table,
+):
+    small = jnp.concatenate([gain_attn, gain_ffn, rel_table, lay_table]).astype(F32)
+    small = jnp.zeros((8, 128), F32).at[0, : small.shape[0]].set(small)
+    down = jnp.pad(w_down, ((0, padded(w_down.shape[0]) - w_down.shape[0]), (0, 0)))
+    full = gather_all(
+        nw,
+        nn,
+        [small, w_query, w_key, w_value, w_output, w_gate, w_up, down],
+        w_down.shape[0],
+    )
+    rows = full[0].reshape(nw * nn, 8, 128)[:, 0]
+    cuts, at = [], 0
+    for part in (gain_attn, gain_ffn, rel_table, lay_table):
+        size = part.shape[0]
+        cuts.append(rows[:, at : at + size].reshape(-1).astype(BF))
+        at += size
+    return tuple(full[1:]) + tuple(cuts)
+
+
+def scatter_fast(
+    nw,
+    nn,
+    grad_query,
+    grad_key,
+    grad_value,
+    grad_output,
+    grad_gate,
+    grad_up,
+    grad_down,
+    grad_gain_attn,
+    grad_gain_ffn,
+    grad_rel,
+    grad_lay,
+):
+    devices = nw * nn
+
+    def columns(grad, width):
+        return jnp.moveaxis(
+            grad.astype(BF).reshape(grad.shape[0], grad.shape[1] // width, width), 1, 0
+        )
+
+    few = columns(grad_down, 256)
+    pairs = jnp.concatenate([columns(grad_gate, 256), columns(grad_up, 256)], axis=2)
+    many = jnp.concatenate(
+        [pairs] + [columns(grad, 512) for grad in (grad_output, grad_query, grad_key, grad_value)]
+    )
+    parts = [
+        part.reshape(devices, -1) for part in (grad_gain_attn, grad_gain_ffn, grad_rel, grad_lay)
+    ]
+    small = jnp.concatenate(parts, axis=1)
+    small = jnp.zeros((devices, 8, 128), F32).at[:, 0, : small.shape[1]].set(small)
+    few_sum, many_sum, small_sum = scatter_all(nw, nn, few, many, small)
+
+    def join(stack):
+        return jnp.moveaxis(stack, 0, 1).reshape(stack.shape[1], -1)
+
+    tiles = pairs.shape[0]
+    owned = []
+    for index in range(4):
+        at = tiles + 2 * index
+        owned.append(join(many_sum[at : at + 2]))
+    gate, up = join(many_sum[:tiles, :, :256]), join(many_sum[:tiles, :, 256:])
+    at, cuts = 0, []
+    for part in parts:
+        cuts.append(small_sum[0, at : at + part.shape[1]])
+        at += part.shape[1]
+    return (owned[1], owned[2], owned[3], owned[0], gate, up, join(few_sum)) + tuple(cuts)
+
+
 def local(
+    nw,
+    nn,
     tokens,
     w_query,
     w_key,
@@ -235,35 +816,39 @@
         axis=2,
     )
     tokens_f = tokens.astype(jnp.float32)
-    weights = gather_weights(
-        w_query,
-        w_key,
-        w_value,
-        w_output,
-        w_gate,
-        w_up,
-        w_down,
-        gain_attn,
-        gain_ffn,
-        rel_table,
-        lay_table,
-    )
+    fast = nw == 8 and w_query.shape[0] % 16 == 0
+    if fast:
+        weights = gather_fast(
+            nw,
+            nn,
+            w_query,
+            w_key,
+            w_value,
+            w_output,
+            w_gate,
+            w_up,
+            w_down,
+            gain_attn,
+            gain_ffn,
+            rel_table,
+            lay_table,
+        )
+    else:
+        weights = gather_weights(
+            w_query,
+            w_key,
+            w_value,
+            w_output,
+            w_gate,
+            w_up,
+            w_down,
+            gain_attn,
+            gain_ffn,
+            rel_table,
+            lay_table,
+        )
     result, saved = forward_pass(tokens_f, weights, onehot, valid)
     output = jnp.where(valid[:, None], result, 0.0).astype(jnp.bfloat16)
-    weights = gather_weights(
-        w_query,
-        w_key,
-        w_value,
-        w_output,
-        w_gate,
-        w_up,
-        w_down,
-        gain_attn,
-        gain_ffn,
-        rel_table,
-        lay_table,
-    )
-    result_again, saved = forward_pass(tokens_f, weights, onehot, valid)
     (
         full_query,
         full_key,
@@ -330,6 +915,23 @@
     input_value, input_pull = jax.vjp(rms_scale, tokens_f, full_gain_attn.astype(jnp.float32))
     grad_input_part, grad_gain_attn = input_pull(grad_normed_attn)
     grad_tokens = grad_hidden + grad_input_part
+    if fast:
+        owned = scatter_fast(
+            nw,
+            nn,
+            grad_query,
+            grad_key,
+            grad_value,
+            grad_output,
+            grad_gate,
+            grad_up,
+            grad_down,
+            grad_gain_attn,
+            grad_gain_ffn,
+            grad_rel,
+            grad_lay,
+        )
+        return (output, grad_tokens) + owned
     owned = (
         lax.psum_scatter(grad_query, ("wide", "narrow"), scatter_dimension=0, tiled=True),
         lax.psum_scatter(grad_key, ("wide", "narrow"), scatter_dimension=0, tiled=True),
@@ -380,7 +982,7 @@
         P(("wide", "narrow"), None),
     )
     return jax.shard_map(
-        local,
+        functools.partial(local, mesh.shape["wide"], mesh.shape["narrow"]),
         mesh=mesh,
         in_specs=placed,
         out_specs=(

time: 2080 us -> 859 us (0.41)
  waiting for transfers between devices: 1300 us -> 0 us
  Pallas kernels: 0 us -> 278 us
  matrix products: 524 us -> 368 us
  blocking collectives: 83.4 us -> 0 us
  local copies, waits for them, and re-layouts: 98.1 us -> 148 us
    reduce_scatter x7 -> x0, waiting for transfers between devices: 1080 us -> none  [the longest x1 252 us: local(): lax.psum_scatter(grad_gate, ('wide', 'narrow'), scatter_dimension=0, tile...]
    pallas_call x0 -> x2, Pallas kernels: none -> 278 us  [the longest x1 156 us: scatter_all(): pl.pallas_call(functools.partial(scatter_kernel, nn, few, many), out_shap...]
    all_gather x7 -> x0, waiting for transfers between devices: 221 us -> none  [the longest x1 61.5 us: gather_weights(): lax.all_gather(w_up, ('wide', 'narrow'), axis=0, tiled=True)]
    unnamed x2 -> x0, blocking collectives: 83.4 us -> none
    dot_general x12 -> x8, matrix products: 181 us -> 120 us  [group_scores(): jnp.einsum('ijb,bh->hij', onehot, table_group, preferred_element_type=jnp...]
    concatenate x4 -> x2, local copies, waits for them, and re-layouts: 0.47 us -> 29.2 us  [scatter_fast(): jnp.concatenate([pairs] + [columns(grad, 512) for grad in (grad_output, g...]
    dot_general x7, matrix products: 51.8 us -> 30.1 us  [contract_rows(): lax.dot_general(left, right, (((0,), (0,)), ((), ())), preferred_element_...]
    dot_general x12 -> x8, local copies, waits for them, and re-layouts: 63.5 us -> 42 us  [group_scores(): jnp.einsum('ijb,bh->hij', onehot, table_group, preferred_element_type=jnp...]
  transfers between devices with their start and end apart: 14 -> 0, of which waited for: 11 -> 0; matrix products, arithmetic and copies ran while one was open for 19% -> 0% of each run, Pallas kernels for 0% -> 0%
where the time goes in v1:
time: 859 us; the launch traced here: 853 us
  matrix products  368 us (43%)
  Pallas kernels  278 us (32%)
  local copies, waits for them, and re-layouts  148 us (17%)
  other arithmetic  55.5 us (6%)
    pallas_call x1, Pallas kernels, scatter_all(): pl.pallas_call(functools.partial(scatter_kernel, nn, few, many), out_shap...  156 us
    pallas_call x1, Pallas kernels, gather_all(): pl.pallas_call(functools.partial(gather_kernel, nn, shapes), out_shape=[j...  122 us
    dot_general x8, matrix products, group_scores(): jnp.einsum('ijb,bh->hij', onehot, table_group, preferred_element_type=jnp...  120 us
    dot_general x4, matrix products, attention_one_group(): jnp.einsum('hij,ijb->bh', grad_scores, onehot, preferred_element_type=jnp...  59.5 us
    dot_general x8, local copies, waits for them, and re-layouts, group_scores(): jnp.einsum('ijb,bh->hij', onehot, table_group, preferred_element_type=jnp...  42 us
    dot_general x7, matrix products, product(): return jnp.dot(left, right, preferred_element_type=jnp.float32)  38.1 us
    dot_general x7, matrix products, contract_cols(): lax.dot_general(left, right, (((1,), (1,)), ((), ())), preferred_element_...  36.5 us
    dot_general x8, matrix products, group_scores(): jnp.einsum('ihd,jhd->hij', query_group, key_group, preferred_element_type...  33.4 us

profile of v1, /device:TPU:0, one launch (start us, length us, event | category | flops | bytes accessed | tf_op | source)
XLA Modules:
  0.0 853.1 jit_solution(5059623018659361109)
XLA Ops:
  3.6 121.9 %shard_map.255 = (f32[256,128]{1,0:T(8,128)}, bf16[1024,1024]{1,0:T(8,128)(2,1)}, bf16[1024,1024]{1,0:T(8,128)(2,1)}, bf16[1024,1024]{1,0:T(8,128)(2,1)}, bf16[1...) custom-call(f32[8,128]{1,0:T(8,128)} %fusion.89.refs_0_, ...), custom_call_target="tpu_custom_call" | custom-call | tf_op jit(solution)/shard_map/pallas_call | solution.py:410
  144.6 12.0 %iota_compare_fusion.2 = (pred[512,512,32]{1,2,0:T(8,128)(4,1)}, pred[512,512,32]{1,2,0:T(8,128)(4,1)}) fusion(s32[512,512]{1,0:T(8,128)} %param.38, s32[512,512]{1,0:T(8,128)} %param.37), kind=kLoop, calls=%fused_computation.65 | loop fusion | flops 16777216 | bytes 18874368 | tf_op jit(solution)/shard_map/eq | solution.py:814
  156.6 15.9 %add_convert_fusion = bf16[512,512,64]{1,2,0:T(8,128)(2,1)} fusion(pred[512,512,32]{1,2,0:T(8,128)(4,1)} %get-tuple-element.308, pred[512,512,32]{1,2,0:T(8,128)(4,1)} %get-tuple-element.309), kind=kLoop, calls=%fused_computation.64 | loop fusion | flops 33554432 | bytes 50331648 | tf_op jit(solution)/shard_map/concatenate | solution.py:811
  174.3 106.3 %while.32 = (s32[]{:T(128)}, bf16[4,512,4,64]{1,3,2,0:T(8,128)(2,1)}, f32[4,4,512]{2,1,0:T(4,128)S(1)}, bf16[4,512,4,64]{1,3,2,0:T(8,128)(2,1)}, bf16[4,512,4,64...) while((s32[]{:T(128)}, ...), condition=%wide.region_4.5_spmd.clone, body=%wide.region_1.4_spmd.clone.sunk | while | flops 411171328 | bytes 64032880 | solution.py:132
  174.3 15.0 %fusion.177 = f32[4,512,512]{2,0,1:T(4,128)} fusion(bf16[512,512,64]{1,2,0:T(8,128)(2,1)} %get-tuple-element.479, bf16[4,64,4]{1,2,0:T(4,128)(2,1)S(1)} %get-tuple-element.478, s32[]{:T(128)} %get-tuple-element.462), kind=kOutput, calls=%fused_computation.22.clone.1 | convolution fusion | flops 134217728 | bytes 37749764 | tf_op jit(solution)/shard_map/while/body/eval_jaxpr/ijb,bh->hij/dot_general | solution.py:63
  200.9 15.0 %fusion.177 = f32[4,512,512]{2,0,1:T(4,128)} fusion(bf16[512,512,64]{1,2,0:T(8,128)(2,1)} %get-tuple-element.479, bf16[4,64,4]{1,2,0:T(4,128)(2,1)S(1)} %get-tuple-element.478, s32[]{:T(128)} %get-tuple-element.462), kind=kOutput, calls=%fused_computation.22.clone.1 | convolution fusion | flops 134217728 | bytes 37749764 | tf_op jit(solution)/shard_map/while/body/eval_jaxpr/ijb,bh->hij/dot_general | solution.py:63
  227.4 15.0 %fusion.177 = f32[4,512,512]{2,0,1:T(4,128)} fusion(bf16[512,512,64]{1,2,0:T(8,128)(2,1)} %get-tuple-element.479, bf16[4,64,4]{1,2,0:T(4,128)(2,1)S(1)} %get-tuple-element.478, s32[]{:T(128)} %get-tuple-element.462), kind=kOutput, calls=%fused_computation.22.clone.1 | convolution fusion | flops 134217728 | bytes 37749764 | tf_op jit(solution)/shard_map/while/body/eval_jaxpr/ijb,bh->hij/dot_general | solution.py:63
  254.0 15.0 %fusion.177 = f32[4,512,512]{2,0,1:T(4,128)} fusion(bf16[512,512,64]{1,2,0:T(8,128)(2,1)} %get-tuple-element.479, bf16[4,64,4]{1,2,0:T(4,128)(2,1)S(1)} %get-tuple-element.478, s32[]{:T(128)} %get-tuple-element.462), kind=kOutput, calls=%fused_computation.22.clone.1 | convolution fusion | flops 134217728 | bytes 37749764 | tf_op jit(solution)/shard_map/while/body/eval_jaxpr/ijb,bh->hij/dot_general | solution.py:63
  302.9 11.7 %multiply_convert_fusion.1 = (bf16[512,2816]{1,0:T(8,128)(2,1)S(1)}, bf16[512,2816]{1,0:T(8,128)(2,1)}, bf16[512,2816]{1,0:T(8,128)(2,1)}) fusion(f32[512,2816]{1,0:T(8,128)} %fusion.106, f32[512,2816]{1,0:T(8,128)} %fusion.107, bf16[2816,1024]{1,0:T(8,128)(2,1)S(1)} %bitcast.306, bf16[512,1024]{1,0:T(8,128)(2,1)S(1)} %copy-done.22, ...), kind=kOutput, calls=%fused_computation.77 | convolution fusion | flops 2991849472 | bytes 27001344 | tf_op jit(solution)/shard_map/dot_general | solution.py:44
  337.1 228.1 %while.33 = (s32[]{:T(128)}, bf16[4,512,4,64]{1,3,2,0:T(8,128)(2,1)}, bf16[4,512,4,64]{1,3,2,0:T(8,128)(2,1)}, bf16[4,512,4,64]{1,3,2,0:T(8,128)(2,1)}, f32[4,64...) while((s32[]{:T(128)}, ...), condition=%wide.region_9.10_spmd.clone, body=%wide.region_7.9_spmd.clone.sunk | while | flops 949352960 | bytes 191415680 | solution.py:200
  341.4 15.0 %fusion.194 = f32[4,512,512]{2,0,1:T(4,128)} fusion(bf16[512,512,64]{1,2,0:T(8,128)(2,1)} %get-tuple-element.518, bf16[4,64,4]{1,2,0:T(4,128)(2,1)S(1)} %get-tuple-element.517, s32[]{:T(128)} %get-tuple-element.496), kind=kOutput, calls=%fused_computation.63.clone.1 | convolution fusion | flops 134217728 | bytes 37749764 | tf_op jit(solution)/shard_map/while/body/eval_jaxpr/ijb,bh->hij/dot_general | solution.py:63
  373.2 14.9 %fusion.198 = f32[4,64,4]{1,2,0:T(4,128)S(1)} fusion(f32[4,64,4]{1,2,0:T(4,128)S(1)} %get-tuple-element.500, s32[]{:T(128)} %get-tuple-element.496, bf16[4,512,512]{2,0,1:T(4,128)(2,1)} %copy.122, bf16[512,512,64]{1,2,0:T(8,128)(2,1)} %get-tuple-element.518), kind=kOutput, calls=%fused_computation.38.clone.1 | convolution fusion | flops 134217728 | bytes 35653636 | tf_op jit(solution)/shard_map/while/body/eval_jaxpr/hij,ijb->bh/dot_general | solution.py:190
  398.3 15.0 %fusion.194 = f32[4,512,512]{2,0,1:T(4,128)} fusion(bf16[512,512,64]{1,2,0:T(8,128)(2,1)} %get-tuple-element.518, bf16[4,64,4]{1,2,0:T(4,128)(2,1)S(1)} %get-tuple-element.517, s32[]{:T(128)} %get-tuple-element.496), kind=kOutput, calls=%fused_computation.63.clone.1 | convolution fusion | flops 134217728 | bytes 37749764 | tf_op jit(solution)/shard_map/while/body/eval_jaxpr/ijb,bh->hij/dot_general | solution.py:63
  430.0 14.9 %fusion.198 = f32[4,64,4]{1,2,0:T(4,128)S(1)} fusion(f32[4,64,4]{1,2,0:T(4,128)S(1)} %get-tuple-element.500, s32[]{:T(128)} %get-tuple-element.496, bf16[4,512,512]{2,0,1:T(4,128)(2,1)} %copy.122, bf16[512,512,64]{1,2,0:T(8,128)(2,1)} %get-tuple-element.518), kind=kOutput, calls=%fused_computation.38.clone.1 | convolution fusion | flops 134217728 | bytes 35653636 | tf_op jit(solution)/shard_map/while/body/eval_jaxpr/hij,ijb->bh/dot_general | solution.py:190
  455.1 15.0 %fusion.194 = f32[4,512,512]{2,0,1:T(4,128)} fusion(bf16[512,512,64]{1,2,0:T(8,128)(2,1)} %get-tuple-element.518, bf16[4,64,4]{1,2,0:T(4,128)(2,1)S(1)} %get-tuple-element.517, s32[]{:T(128)} %get-tuple-element.496), kind=kOutput, calls=%fused_computation.63.clone.1 | convolution fusion | flops 134217728 | bytes 37749764 | tf_op jit(solution)/shard_map/while/body/eval_jaxpr/ijb,bh->hij/dot_general | solution.py:63
  486.9 14.9 %fusion.198 = f32[4,64,4]{1,2,0:T(4,128)S(1)} fusion(f32[4,64,4]{1,2,0:T(4,128)S(1)} %get-tuple-element.500, s32[]{:T(128)} %get-tuple-element.496, bf16[4,512,512]{2,0,1:T(4,128)(2,1)} %copy.122, bf16[512,512,64]{1,2,0:T(8,128)(2,1)} %get-tuple-element.518), kind=kOutput, calls=%fused_computation.38.clone.1 | convolution fusion | flops 134217728 | bytes 35653636 | tf_op jit(solution)/shard_map/while/body/eval_jaxpr/hij,ijb->bh/dot_general | solution.py:190
  512.0 15.0 %fusion.194 = f32[4,512,512]{2,0,1:T(4,128)} fusion(bf16[512,512,64]{1,2,0:T(8,128)(2,1)} %get-tuple-element.518, bf16[4,64,4]{1,2,0:T(4,128)(2,1)S(1)} %get-tuple-element.517, s32[]{:T(128)} %get-tuple-element.496), kind=kOutput, calls=%fused_computation.63.clone.1 | convolution fusion | flops 134217728 | bytes 37749764 | tf_op jit(solution)/shard_map/while/body/eval_jaxpr/ijb,bh->hij/dot_general | solution.py:63
  543.7 14.9 %fusion.198 = f32[4,64,4]{1,2,0:T(4,128)S(1)} fusion(f32[4,64,4]{1,2,0:T(4,128)S(1)} %get-tuple-element.500, s32[]{:T(128)} %get-tuple-element.496, bf16[4,512,512]{2,0,1:T(4,128)(2,1)} %copy.122, bf16[512,512,64]{1,2,0:T(8,128)(2,1)} %get-tuple-element.518), kind=kOutput, calls=%fused_computation.38.clone.1 | convolution fusion | flops 134217728 | bytes 35653636 | tf_op jit(solution)/shard_map/while/body/eval_jaxpr/hij,ijb->bh/dot_general | solution.py:190
  585.2 8.3 copy.93
  601.3 8.3 copy.94
  609.6 13.0 %maximum_dynamic-update-slice_fusion = bf16[19,1024,512]{1,2,0:T(8,128)(2,1)} fusion(bf16[11,1024,256]{1,2,0:T(8,128)(2,1)} %bitcast.272, bf16[11,1024,256]{1,2,0:T(8,128)(2,1)} %bitcast.271), kind=kLoop, calls=%fused_computation.67 | loop fusion | flops 23068672 | bytes 23068672
  633.9 27.7 %copy.95 = bf16[19,1024,512]{2,1,0:T(8,128)(2,1)} copy(bf16[19,1024,512]{1,2,0:T(8,128)(2,1)} %constant_dynamic-update-slice_fusion) | data formatting | bytes 39845888 | tf_op jit(solution)/shard_map/concatenate | solution.py:762
  669.5 8.3 copy.92
  677.8 156.4 %shard_map.256 = (f32[4,88,256]{2,1,0:T(8,128)}, f32[19,32,512]{2,1,0:T(8,128)}, f32[8,128]{1,0:T(8,128)}, bf16[4,4,352,256]{3,2,1,0:T(8,128)(2,1)}, bf16[19,4,128,512]{3,2,1,0:T(8,128)(2,1)}) custom-call(bf16[4,4,2,352,256]{4,3,2,1,0:T(8,128)(2,1)} %bitcast.270, bf16[19,4,2,128,512]{4,3,2,1,0:T(8,128)(2,1)} %bitcast.267, f32[4,2,32,128]{3,2,1,0:T(8,128)} %bitcast.284), custom_call_target="tpu_custom_call" | custom-call | tf_op jit(solution)/shard_map/pallas_call | solution.py:685
  (259 shorter events, 287.5 us)
Async XLA Ops:
  126.6 11.5 %copy-start.24 = (f32[1024]{0:T(1024)}, f32[1024]{0:T(1024)S(1)}, u32[]{:S(2)}) copy-start(f32[1024]{0:T(1024)S(1)} %reshape.355) | copy-start | bytes 12292
  128.7 9.4 %copy-start.28 = (f32[512]{0:T(512)}, f32[512]{0:T(512)S(1)}, u32[]{:S(2)}) copy-start(f32[512]{0:T(512)S(1)} %fusion.93) | copy-start | bytes 6148
  287.0 7.9 copy-start.17
  287.1 15.8 %slice-start = ((s8[5767168]{0:T(1024)(128)(4,1)}), s8[4194304]{0:T(1024)(128)(4,1)S(1)}, s32[]{:S(2)}) async-start(s8[5767168]{0:T(1024)(128)(4,1)} %bitcast.305), calls=%async_computation | async-start | bytes 8388608
  295.0 7.9 copy-start.22
  295.0 7.9 slice-start.1
  302.9 25.1 %copy-start.32 = (pred[512]{0:T(512)(128)(4,1)}, pred[512]{0:T(512)(128)(4,1)S(1)}, u32[]{:S(2)}) copy-start(pred[512]{0:T(512)(128)(4,1)S(1)} %iota_compare_fusion.6) | copy-start | bytes 1540
  337.5 18.9 %copy-start.9 = (bf16[4,512,4,64]{1,3,2,0:T(8,128)(2,1)}, bf16[4,512,4,64]{1,3,2,0:T(8,128)(2,1)S(1)}, u32[]{:S(2)}) copy-start(bf16[4,512,4,64]{1,3,2,0:T(8,128)(2,1)S(1)} %get-tuple-element.520) | copy-start | bytes 3145732 | tf_op jit(solution)/shard_map/while
  337.5 24.1 %copy-start.3 = (bf16[4,512,4,64]{1,3,2,0:T(8,128)(2,1)}, bf16[4,512,4,64]{1,3,2,0:T(8,128)(2,1)S(1)}, u32[]{:S(2)}) copy-start(bf16[4,512,4,64]{1,3,2,0:T(8,128)(2,1)S(1)} %get-tuple-element.516) | copy-start | bytes 3145732 | tf_op jit(solution)/shard_map/while
  361.6 7.2 copy-start.2
  394.4 18.9 %copy-start.9 = (bf16[4,512,4,64]{1,3,2,0:T(8,128)(2,1)}, bf16[4,512,4,64]{1,3,2,0:T(8,128)(2,1)S(1)}, u32[]{:S(2)}) copy-start(bf16[4,512,4,64]{1,3,2,0:T(8,128)(2,1)S(1)} %get-tuple-element.520) | copy-start | bytes 3145732 | tf_op jit(solution)/shard_map/while
  394.4 24.1 %copy-start.3 = (bf16[4,512,4,64]{1,3,2,0:T(8,128)(2,1)}, bf16[4,512,4,64]{1,3,2,0:T(8,128)(2,1)S(1)}, u32[]{:S(2)}) copy-start(bf16[4,512,4,64]{1,3,2,0:T(8,128)(2,1)S(1)} %get-tuple-element.516) | copy-start | bytes 3145732 | tf_op jit(solution)/shard_map/while
  418.5 7.2 copy-start.2
  451.2 18.9 %copy-start.9 = (bf16[4,512,4,64]{1,3,2,0:T(8,128)(2,1)}, bf16[4,512,4,64]{1,3,2,0:T(8,128)(2,1)S(1)}, u32[]{:S(2)}) copy-start(bf16[4,512,4,64]{1,3,2,0:T(8,128)(2,1)S(1)} %get-tuple-element.520) | copy-start | bytes 3145732 | tf_op jit(solution)/shard_map/while
  451.2 24.1 %copy-start.3 = (bf16[4,512,4,64]{1,3,2,0:T(8,128)(2,1)}, bf16[4,512,4,64]{1,3,2,0:T(8,128)(2,1)S(1)}, u32[]{:S(2)}) copy-start(bf16[4,512,4,64]{1,3,2,0:T(8,128)(2,1)S(1)} %get-tuple-element.516) | copy-start | bytes 3145732 | tf_op jit(solution)/shard_map/while
  475.4 7.2 copy-start.2
  508.1 18.9 %copy-start.9 = (bf16[4,512,4,64]{1,3,2,0:T(8,128)(2,1)}, bf16[4,512,4,64]{1,3,2,0:T(8,128)(2,1)S(1)}, u32[]{:S(2)}) copy-start(bf16[4,512,4,64]{1,3,2,0:T(8,128)(2,1)S(1)} %get-tuple-element.520) | copy-start | bytes 3145732 | tf_op jit(solution)/shard_map/while
  508.1 24.1 %copy-start.3 = (bf16[4,512,4,64]{1,3,2,0:T(8,128)(2,1)}, bf16[4,512,4,64]{1,3,2,0:T(8,128)(2,1)S(1)}, u32[]{:S(2)}) copy-start(bf16[4,512,4,64]{1,3,2,0:T(8,128)(2,1)S(1)} %get-tuple-element.516) | copy-start | bytes 3145732 | tf_op jit(solution)/shard_map/while
  532.2 7.2 copy-start.2
  609.6 13.0 %copy-start.15 = (bf16[1024,1024]{0,1:T(8,128)(2,1)S(1)}, bf16[1024,1024]{0,1:T(8,128)(2,1)}, u32[]{:S(2)}) copy-start(bf16[1024,1024]{0,1:T(8,128)(2,1)} %convolution_convert_fusion.8) | copy-start | bytes 6291460
  633.9 27.7 %copy-start.33 = (pred[512]{0:T(512)(128)(4,1)S(1)}, pred[512]{0:T(512)(128)(4,1)}, u32[]{:S(2)}) copy-start(pred[512]{0:T(512)(128)(4,1)} %copy-done.32) | copy-start | bytes 1540
  834.3 7.4 copy-start.31
  834.3 8.6 %copy-start.27 = (f32[512]{0:T(512)S(1)}, f32[512]{0:T(512)}, u32[]{:S(2)}) copy-start(f32[512]{0:T(512)} %copy-done.26) | copy-start | bytes 6148
  834.3 8.6 %copy-start.13 = (f32[512,1024]{1,0:T(8,128)S(1)}, f32[512,1024]{1,0:T(8,128)}, u32[]{:S(2)}) copy-start(f32[512,1024]{1,0:T(8,128)} %get-tuple-element.307) | copy-start | bytes 6291460
  (37 other events, 113.3 us)

commit v2 on v1

--- a/solution.py
+++ b/solution.py
@@ -13,6 +13,10 @@
 IMG = 196
 RING = 6
 SCATTER_COPIES = 10
+TILE = 256
+QB = 8
+GELU_SCALE = 0.7978845608028654
+GELU_CUBE = 0.044715
 
 
 RMS_EPSILON = 1e-06
@@ -363,67 +367,395 @@
     return ((0, low, PARTS[0]), (low, columns - low, PARTS[1]))
 
 
-def gather_kernel(nn, shapes, *refs):
+def dot(left, right):
+    return jnp.dot(left, right, preferred_element_type=F32)
+
+
+def dot_nt(left, right):
+    return lax.dot_general(left, right, (((1,), (1,)), ((), ())), preferred_element_type=F32)
+
+
+def dot_tn(left, right):
+    return lax.dot_general(left, right, (((0,), (0,)), ((), ())), preferred_element_type=F32)
+
+
+def iota(shape, dimension):
+    return lax.broadcasted_iota(jnp.int32, shape, dimension)
+
+
+def ones_where(mask):
+    return jnp.where(mask, 1.0, 0.0).astype(BF)
+
+
+def unpack_row(rows, first, each, total):
+    devices = rows.shape[0]
+    pick = ones_where(iota((128, total), 0) == first + lax.rem(iota((128, total), 1), each))
+    spread = dot(rows.astype(BF), pick)
+    mine = iota((devices, total), 1) // each == iota((devices, total), 0)
+    return jnp.sum(jnp.where(mine, spread, 0.0), axis=0, keepdims=True)
+
+
+def table_block(rows, first):
+    pick_shape = (H * QB, 128)
+    total = None
+    for index in range(2):
+        lane = first + H * index + iota(pick_shape, 0) // QB
+        pick = ones_where(iota(pick_shape, 1) == lane)
+        table = dot_nt(pick, rows.astype(BF)).astype(BF)
+        wide = (NB, QB * 2 * NB)
+        spread = dot(table, ones_where(lax.rem(iota(wide, 1), 2 * NB) == iota(wide, 0) + NB * index))
+        total = spread if total is None else total + spread
+    shape = (H * QB, QB * 2 * NB)
+    mine = lax.rem(iota(shape, 0), QB) == iota(shape, 1) // (2 * NB)
+    return jnp.where(mine, total, 0.0).astype(BF)
+
+
+def bucket_ones(rel, lay, onehot, block):
+    width = rel.shape[1]
+    rows = iota((NB, width), 0)
+    for query in range(QB):
+        for index, bucket in enumerate((rel, lay)):
+            row = bucket[pl.ds(block * QB + query, 1), :]
+            low = (query * 2 + index) * NB
+            onehot[low : low + NB, :] = ones_where(jnp.broadcast_to(row, (NB, width)) == rows)
+
+
+def forward_kernel(nn, shapes, *refs):
     count = len(shapes)
-    shards, fulls = refs[:count], refs[count : 2 * count]
-    line, merged, send_sem, recv_sem, local_sem = refs[2 * count :]
+    occupied, tokens, rel_hbm, lay_hbm = refs[:4]
+    shards = refs[4 : 4 + count]
+    refs = refs[4 + count :]
+    fulls, refs = refs[:count], refs[count:]
+    saved, refs = refs[:10], refs[10:]
+    (out_h, na_h, q_h, k_h, v_h, att_h, hid_h, nf_h, mix_h, probs_h) = saved
+    (slope_h, act_h), refs = refs[:2], refs[2:]
+    (
+        line,
+        merged,
+        x,
+        rel,
+        lay,
+        small,
+        lhs,
+        onehot,
+        bias,
+        na,
+        q,
+        k,
+        v,
+        att,
+        hid,
+        nf,
+        mix,
+        slope,
+        act,
+        probs,
+        w_one,
+        w_wide,
+        w_down,
+        gains,
+        send_sem,
+        recv_sem,
+        gather_sem,
+        local_sem,
+        ring_sem,
+    ) = refs
+    slots, width = x.shape
     links = Links(nn, send_sem, recv_sem)
+    numbers = iter(range(64))
+
+    def move(src, dst):
+        copy = pltpu.make_async_copy(src, dst, local_sem.at[next(numbers)])
+        copy.start()
+        return copy
+
+    arriving = [move(tokens, x), move(rel_hbm, rel), move(lay_hbm, lay)]
     links.greet()
-    gathers = []
+    g = []
     for index, (rows, columns) in enumerate(shapes):
         odd = rows % 16 != 0 and columns > 128
-        gathers.append(
+        g.append(
             Gather(
                 links,
                 shards[index],
                 fulls[index],
                 rows,
                 halves(columns) if columns > 128 else ((0, columns, PARTS[0]),),
-                local_sem.at[index],
+                gather_sem.at[index],
                 line if odd else None,
                 merged if odd else None,
             )
         )
-    gathers[0].start()
-    gathers[1].start()
-    for index in range(count + 3):
-        if index < count:
-            gathers[index].spread()
-            if index + 2 < count:
-                gathers[index + 2].start()
-        if 0 <= index - 1 < count:
-            gathers[index - 1].forward()
-        if 0 <= index - 2 < count:
-            gathers[index - 2].last()
-        if 0 <= index - 3 < count:
-            gathers[index - 3].done()
+    SMALL, Q, K, V, O, GATE, UP, DOWN = range(8)
+    g[SMALL].start()
+    g[Q].start()
+    g[K].start()
+    g[SMALL].spread()
+    g[SMALL].forward()
+    g[SMALL].last()
+    g[SMALL].done()
+    small_in = move(fulls[SMALL], small)
+    g[Q].spread()
+    g[V].start()
+    leaving = []
+    for copy in arriving:
+        copy.wait()
+    small_in.wait()
+    rows = small.reshape(small.shape[0] // 8, 8, 128)[:, 0, :]
+    each = width // rows.shape[0]
+    gains[0:1, :] = unpack_row(rows, 0, each, width)
+    gains[1:2, :] = unpack_row(rows, each, each, width)
+    lhs[...] = table_block(rows, 2 * each)
+
+    def normalise(index, carry):
+        at = pl.ds(pl.multiple_of(index * 64, 64), 64)
+        values = x[at, :].astype(F32)
+        scale = lax.rsqrt(jnp.mean(values * values, axis=-1, keepdims=True) + RMS_EPSILON)
+        na[at, :] = (values * scale * gains[0:1, :]).astype(BF)
+        return carry
+
+    lax.fori_loop(0, slots // 64, normalise, 0)
+    leaving.append(move(na, na_h))
+    valid = iota((1, slots), 1) < occupied[0] + IMG
+
+    def bias_block(block, carry):
+        bucket_ones(rel, lay, onehot, block)
+        found = jnp.where(valid, dot(lhs[...], onehot[...]), MASK_SCORE)
+        bias[:, pl.ds(pl.multiple_of(block * QB, QB), QB), :] = found.reshape(H, QB, slots)
+        return carry
+
+    blocks = slots // QB
+    lax.fori_loop(0, blocks // 4, bias_block, 0)
+    g[K].spread()
+    g[O].start()
+    g[Q].forward()
+    lax.fori_loop(blocks // 4, blocks // 2, bias_block, 0)
+    g[V].spread()
+    g[GATE].start()
+    g[K].forward()
+    g[Q].last()
+    lax.fori_loop(blocks // 2, 3 * blocks // 4, bias_block, 0)
+    g[O].spread()
+    g[V].forward()
+    g[K].last()
+    g[Q].done()
+    fetch = move(fulls[Q], w_one.at[0])
+    lax.fori_loop(3 * blocks // 4, blocks, bias_block, 0)
+    fetch.wait()
+
+    def project(slot, target):
+        def one(tile, carry):
+            at = pl.ds(pl.multiple_of(tile * TILE, TILE), TILE)
+            target[:, at] = dot(na[...], w_one[slot, :, at]).astype(BF)
+            return carry
+
+        lax.fori_loop(0, width // TILE, one, 0)
+
+    project(0, q)
+    leaving.append(move(q, q_h))
+    g[GATE].spread()
+    g[UP].start()
+    g[O].forward()
+    g[V].last()
+    g[K].done()
+    fetch = move(fulls[K], w_one.at[1])
+    fetch.wait()
+    project(1, k)
+    leaving.append(move(k, k_h))
+    g[O].last()
+    g[V].done()
+    fetch = move(fulls[V], w_one.at[0])
+    fetch.wait()
+    project(0, v)
+    leaving.append(move(v, v_h))
+
+    def probs_out(pair):
+        turn = lax.rem(pair, 2)
+        return pltpu.make_async_copy(probs.at[turn], probs_h.at[pl.ds(pair * 2, 2)], ring_sem.at[turn])
+
+    def attend(pair, carry):
+        @pl.when(pair >= 2)
+        def _():
+            probs_out(pair - 2).wait()
+
+        at = pl.ds(pl.multiple_of(pair * 128, 128), 128)
+        low = iota((slots, 128), 1) < HD
+        queries = q[:, at]
+        keys = k[:, at]
+        found = []
+        for side in range(2):
+            mine = jnp.where(low if side == 0 else jnp.logical_not(low), queries, 0)
+            scores = dot_nt(mine, keys) + bias[pair * 2 + side]
+            peak = jnp.max(scores, axis=-1, keepdims=True)
+            expo = jnp.exp(scores - peak)
+            total = jnp.sum(expo, axis=-1, keepdims=True)
+            share = (expo * (1.0 / total)).astype(BF)
+            probs[lax.rem(pair, 2), side] = share
+            found.append(dot(share, v[:, at]))
+        att[:, at] = jnp.where(low, found[0], found[1]).astype(BF)
+        probs_out(pair).start()
+        return carry
+
+    pairs = H // 2
+    lax.fori_loop(0, 2, attend, 0)
+    g[UP].spread()
+    g[DOWN].start()
+    g[GATE].forward()
+    g[O].done()
+    fetch_o = move(fulls[O], w_one.at[1])
+    lax.fori_loop(2, 5, attend, 0)
+    g[GATE].last()
+    lax.fori_loop(5, pairs, attend, 0)
+    leaving.append(move(att, att_h))
+    g[DOWN].spread()
+    g[UP].forward()
+    g[GATE].done()
+    fetch_gate = move(fulls[GATE], w_wide.at[0])
+    fetch_o.wait()
+
+    def output_tile(tile, carry):
+        at = pl.ds(pl.multiple_of(tile * TILE, TILE), TILE)
+        hid[:, at] = x[:, at].astype(F32) + dot(att[...], w_one[1, :, at])
+        return carry
+
+    lax.fori_loop(0, width // TILE, output_tile, 0)
+    leaving.append(move(hid, hid_h))
+
+    def normalise_two(index, carry):
+        at = pl.ds(pl.multiple_of(index * 64, 64), 64)
+        values = hid[at, :]
+        scale = lax.rsqrt(jnp.mean(values * values, axis=-1, keepdims=True) + RMS_EPSILON)
+        nf[at, :] = (values * scale * gains[1:2, :]).astype(BF)
+        return carry
+
+    lax.fori_loop(0, slots // 64, normalise_two, 0)
+    leaving.append(move(nf, nf_h))
+    g[UP].last()
+    g[DOWN].forward()
+    g[UP].done()
+    fetch_up = move(fulls[UP], w_wide.at[1])
+    fetch_gate.wait()
+    fetch_up.wait()
+
+    def ffn_out(tile):
+        turn = lax.rem(tile, 2)
+        at = pl.ds(pl.multiple_of(tile * TILE, TILE), TILE)
+        return (
+            pltpu.make_async_copy(slope.at[turn], slope_h.at[:, at], ring_sem.at[2 + turn]),
+            pltpu.make_async_copy(act.at[turn], act_h.at[:, at], ring_sem.at[4 + turn]),
+        )
+
+    def ffn_tile(tile, carry):
+        @pl.when(tile >= 2)
+        def _():
+            for copy in ffn_out(tile - 2):
+                copy.wait()
+
+        at = pl.ds(pl.multiple_of(tile * TILE, TILE), TILE)
+        turn = lax.rem(tile, 2)
+        gate = dot(nf[...], w_wide[0, :, at])
+        up = dot(nf[...], w_wide[1, :, at])
+        square = gate * gate
+        inner = GELU_SCALE * gate * (1.0 + GELU_CUBE * square)
+        bend = jnp.tanh(inner)
+        half = 0.5 * (1.0 + bend)
+        active = gate * half
+        rise = half + 0.5 * gate * (1.0 - bend * bend) * GELU_SCALE * (1.0 + 3.0 * GELU_CUBE * square)
+        mix[:, at] = (active * up).astype(BF)
+        act[turn] = active.astype(BF)
+        slope[turn] = (up * rise).astype(BF)
+        for copy in ffn_out(tile):
+            copy.start()
+        return carry
+
+    tiles = mix.shape[1] // TILE
+    lax.fori_loop(0, tiles // 2, ffn_tile, 0)
+    g[DOWN].last()
+    lax.fori_loop(tiles // 2, tiles, ffn_tile, 0)
+    leaving.append(move(mix, mix_h))
+    g[DOWN].done()
+    move(fulls[DOWN], w_down).wait()
+    valid_rows = iota((slots, 1), 0) < occupied[0] + IMG
+
+    def down_tile(tile, carry):
+        at = pl.ds(pl.multiple_of(tile * TILE, TILE), TILE)
+        result = hid[:, at] + dot(mix[...], w_down[:, at])
+        na[:, at] = jnp.where(valid_rows, result, 0.0).astype(BF)
+        return carry
+
+    leaving[0].wait()
+    lax.fori_loop(0, width // TILE, down_tile, 0)
+    move(na, out_h).wait()
+    for copy in leaving[1:]:
+        copy.wait()
+    for pair in (pairs - 2, pairs - 1):
+        probs_out(pair).wait()
+    for tile in (tiles - 2, tiles - 1):
+        for copy in ffn_out(tile):
+            copy.wait()
     links.finish()
 
 
-def gather_all(nw, nn, shards, odd_rows):
+def forward_all(nw, nn, counts, tokens, rel, lay, shards, odd_rows):
     devices = nw * nn
     shapes = []
     for index, shard in enumerate(shards):
         rows = odd_rows if index == len(shards) - 1 else shard.shape[0]
         shapes.append((rows, shard.shape[1]))
     copies = len(shards) * (nn - 1 + 6 + 4)
+    slots, width = tokens.shape
+    ffn = shapes[5][1]
+    low = jax.ShapeDtypeStruct((slots, width), BF)
+    wide = jax.ShapeDtypeStruct((slots, ffn), BF)
+    full = jax.ShapeDtypeStruct((slots, width), F32)
+    out_shape = [
+        jax.ShapeDtypeStruct((rows * devices, columns), shard.dtype)
+        for (rows, columns), shard in zip(shapes, shards)
+    ]
+    out_shape += [low] * 6 + [full, low, wide]
+    out_shape += [jax.ShapeDtypeStruct((H, slots, slots), BF), wide, wide]
+    hbm = pl.BlockSpec(memory_space=pl.ANY)
+    page = pltpu.VMEM((slots, width), BF)
     return pl.pallas_call(
-        functools.partial(gather_kernel, nn, shapes),
-        out_shape=[
-            jax.ShapeDtypeStruct((rows * devices, columns), shard.dtype)
-            for (rows, columns), shard in zip(shapes, shards)
-        ],
-        in_specs=[pl.BlockSpec(memory_space=pl.ANY)] * len(shards),
-        out_specs=[pl.BlockSpec(memory_space=pl.ANY)] * len(shards),
+        functools.partial(forward_kernel, nn, shapes),
+        out_shape=out_shape,
+        in_specs=[pl.BlockSpec(memory_space=pltpu.SMEM)] + [hbm] * (3 + len(shards)),
+        out_specs=[hbm] * len(out_shape),
         scratch_shapes=[
             pltpu.VMEM((nn,) + shards[-1].shape, BF),
             pltpu.VMEM((nn * odd_rows, shards[-1].shape[1]), BF),
+            page,
+            pltpu.VMEM((slots, slots), jnp.int32),
+            pltpu.VMEM((slots, slots), jnp.int32),
+            pltpu.VMEM((devices * 8, 128), F32),
+            pltpu.VMEM((H * QB, QB * 2 * NB), BF),
+            pltpu.VMEM((QB * 2 * NB, slots), BF),
+            pltpu.VMEM((H, slots, slots), F32),
+            page,
+            page,
+            page,
+            page,
+            page,
+            pltpu.VMEM((slots, width), F32),
+            page,
+            pltpu.VMEM((slots, ffn), BF),
+            pltpu.VMEM((2, slots, TILE), BF),
+            pltpu.VMEM((2, slots, TILE), BF),
+            pltpu.VMEM((2, 2, slots, slots), BF),
+            pltpu.VMEM((2, width, width), BF),
+            pltpu.VMEM((2, width, ffn), BF),
+            pltpu.VMEM((ffn, width), BF),
+            pltpu.VMEM((8, width), F32),
             pltpu.SemaphoreType.DMA((copies,)),
             pltpu.SemaphoreType.DMA((copies,)),
             pltpu.SemaphoreType.DMA((len(shards),)),
+            pltpu.SemaphoreType.DMA((64,)),
+            pltpu.SemaphoreType.DMA((6,)),
         ],
-        compiler_params=pltpu.CompilerParams(collective_id=0, has_side_effects=True),
-    )(*shards)
+        compiler_params=pltpu.CompilerParams(
+            collective_id=0, has_side_effects=True, vmem_limit_bytes=63 * 2**20
+        ),
+    )(counts, tokens, rel, lay, *shards)
 
 
 class Scatter:
@@ -702,9 +1034,10 @@
         ),
     )(*given, small.reshape(squares, 2, nn * 8, 128))[:3]
 
-def gather_fast(
+def local_fast(
     nw,
     nn,
+    tokens,
     w_query,
     w_key,
     w_value,
@@ -716,23 +1049,132 @@
     gain_ffn,
     rel_table,
     lay_table,
+    ocr_counts,
+    rel_bucket,
+    lay_bucket,
+    cotangent,
 ):
     small = jnp.concatenate([gain_attn, gain_ffn, rel_table, lay_table]).astype(F32)
-    small = jnp.zeros((8, 128), F32).at[0, : small.shape[0]].set(small)
+    small = jnp.pad(small[None], ((0, 7), (0, 128 - small.shape[0])))
     down = jnp.pad(w_down, ((0, padded(w_down.shape[0]) - w_down.shape[0]), (0, 0)))
-    full = gather_all(
+    (
+        full_small,
+        full_query,
+        full_key,
+        full_value,
+        full_output,
+        full_gate,
+        full_up,
+        full_down,
+        output,
+        normed_attn,
+        queries,
+        keys_all,
+        values_all,
+        attended,
+        hidden_one,
+        normed_ffn,
+        mixed,
+        probs,
+        slope,
+        active,
+    ) = forward_all(
         nw,
         nn,
+        ocr_counts,
+        tokens,
+        rel_bucket,
+        lay_bucket,
         [small, w_query, w_key, w_value, w_output, w_gate, w_up, down],
         w_down.shape[0],
     )
-    rows = full[0].reshape(nw * nn, 8, 128)[:, 0]
-    cuts, at = [], 0
-    for part in (gain_attn, gain_ffn, rel_table, lay_table):
-        size = part.shape[0]
-        cuts.append(rows[:, at : at + size].reshape(-1).astype(BF))
-        at += size
-    return tuple(full[1:]) + tuple(cuts)
+    rows = full_small.reshape(nw * nn, 8, 128)[:, 0]
+    each = gain_attn.shape[0]
+    full_gain_attn = rows[:, :each].reshape(-1)
+    full_gain_ffn = rows[:, each : 2 * each].reshape(-1)
+    slot = tokens.shape[0]
+    valid = jnp.arange(slot) < ocr_counts[0] + IMG
+    buckets = jnp.arange(NB)
+    onehot = jnp.concatenate(
+        [
+            (rel_bucket[:, :, None] == buckets).astype(jnp.bfloat16),
+            (lay_bucket[:, :, None] == buckets).astype(jnp.bfloat16),
+        ],
+        axis=2,
+    )
+    tokens_f = tokens.astype(F32)
+    grad_result = jnp.where(valid[:, None], cotangent.astype(jnp.float32), 0.0)
+    grad_low = grad_result.astype(jnp.bfloat16)
+    grad_down = contract_rows(mixed, grad_low)
+    grad_mixed = contract_cols(grad_low, full_down)
+    gate_low = (grad_mixed * slope.astype(F32)).astype(BF)
+    up_low = (grad_mixed * active.astype(F32)).astype(BF)
+    grad_gate = contract_rows(normed_ffn, gate_low)
+    grad_up = contract_rows(normed_ffn, up_low)
+    grad_normed_ffn = contract_cols(gate_low, full_gate) + contract_cols(up_low, full_up)
+    norm_value, norm_pull = jax.vjp(rms_scale, hidden_one, full_gain_ffn)
+    grad_hidden_part, grad_gain_ffn = norm_pull(grad_normed_ffn)
+    grad_hidden = grad_result + grad_hidden_part
+    branch_low = grad_hidden.astype(jnp.bfloat16)
+    grad_output = contract_rows(attended, branch_low)
+    grad_attended = contract_cols(branch_low, full_output).astype(jnp.bfloat16)
+
+    def one_group(operands):
+        query_group, key_group, value_group, grad_group, probs_low = operands
+        part = functools.partial(jnp.einsum, preferred_element_type=F32)
+        grad_values = part("hij,ihd->jhd", probs_low, grad_group)
+        grad_probs = part("ihd,jhd->hij", grad_group, value_group)
+        share = probs_low.astype(F32)
+        grad_scores = (
+            share * (grad_probs - jnp.sum(share * grad_probs, axis=-1, keepdims=True))
+        ).astype(BF)
+        return (
+            part("hij,jhd->ihd", grad_scores, key_group).astype(BF),
+            part("hij,ihd->jhd", grad_scores, query_group).astype(BF),
+            grad_values.astype(BF),
+            part("hij,ijb->bh", grad_scores, onehot),
+        )
+
+    grad_q, grad_k, grad_v, grad_tables = lax.map(
+        one_group,
+        (
+            split_heads(queries),
+            split_heads(keys_all),
+            split_heads(values_all),
+            split_heads(grad_attended),
+            probs.reshape(H // HEAD_GROUP, HEAD_GROUP, slot, slot),
+        ),
+    )
+    grad_table_all = jnp.moveaxis(grad_tables, 0, 1).reshape(2 * NB, H)
+    grad_queries, grad_keys, grad_values = join_heads(grad_q), join_heads(grad_k), join_heads(grad_v)
+    grad_rel = grad_table_all[:NB].reshape(NB * H)
+    grad_lay = grad_table_all[NB:].reshape(NB * H)
+    grad_query = contract_rows(normed_attn, grad_queries)
+    grad_key = contract_rows(normed_attn, grad_keys)
+    grad_value = contract_rows(normed_attn, grad_values)
+    grad_normed_attn = (
+        contract_cols(grad_queries, full_query)
+        + contract_cols(grad_keys, full_key)
+        + contract_cols(grad_values, full_value)
+    )
+    input_value, input_pull = jax.vjp(rms_scale, tokens_f, full_gain_attn)
+    grad_input_part, grad_gain_attn = input_pull(grad_normed_attn)
+    grad_tokens = grad_hidden + grad_input_part
+    return (output, grad_tokens) + scatter_fast(
+        nw,
+        nn,
+        grad_query,
+        grad_key,
+        grad_value,
+        grad_output,
+        grad_gate,
+        grad_up,
+        grad_down,
+        grad_gain_attn,
+        grad_gain_ffn,
+        grad_rel,
+        grad_lay,
+    )
 
 
 def scatter_fast(
@@ -786,8 +1228,6 @@
 
 
 def local(
-    nw,
-    nn,
     tokens,
     w_query,
     w_key,
@@ -816,37 +1256,19 @@
         axis=2,
     )
     tokens_f = tokens.astype(jnp.float32)
-    fast = nw == 8 and w_query.shape[0] % 16 == 0
-    if fast:
-        weights = gather_fast(
-            nw,
-            nn,
-            w_query,
-            w_key,
-            w_value,
-            w_output,
-            w_gate,
-            w_up,
-            w_down,
-            gain_attn,
-            gain_ffn,
-            rel_table,
-            lay_table,
-        )
-    else:
-        weights = gather_weights(
-            w_query,
-            w_key,
-            w_value,
-            w_output,
-            w_gate,
-            w_up,
-            w_down,
-            gain_attn,
-            gain_ffn,
-            rel_table,
-            lay_table,
-        )
+    weights = gather_weights(
+        w_query,
+        w_key,
+        w_value,
+        w_output,
+        w_gate,
+        w_up,
+        w_down,
+        gain_attn,
+        gain_ffn,
+        rel_table,
+        lay_table,
+    )
     result, saved = forward_pass(tokens_f, weights, onehot, valid)
     output = jnp.where(valid[:, None], result, 0.0).astype(jnp.bfloat16)
     (
@@ -915,23 +1337,6 @@
     input_value, input_pull = jax.vjp(rms_scale, tokens_f, full_gain_attn.astype(jnp.float32))
     grad_input_part, grad_gain_attn = input_pull(grad_normed_attn)
     grad_tokens = grad_hidden + grad_input_part
-    if fast:
-        owned = scatter_fast(
-            nw,
-            nn,
-            grad_query,
-            grad_key,
-            grad_value,
-            grad_output,
-            grad_gate,
-            grad_up,
-            grad_down,
-            grad_gain_attn,
-            grad_gain_ffn,
-            grad_rel,
-            grad_lay,
-        )
-        return (output, grad_tokens) + owned
     owned = (
         lax.psum_scatter(grad_query, ("wide", "narrow"), scatter_dimension=0, tiled=True),
         lax.psum_scatter(grad_key, ("wide", "narrow"), scatter_dimension=0, tiled=True),
@@ -963,6 +1368,13 @@
 
 
 def solution(mesh):
+    nw, nn = mesh.shape["wide"], mesh.shape["narrow"]
+
+    def body(*args):
+        if nw == 8 and nw * nn == NB and args[1].shape[0] % 16 == 0:
+            return local_fast(nw, nn, *args)
+        return local(*args)
+
     placed = (
         P(("wide", "narrow"), None),
         P(("wide", "narrow"), None),
@@ -982,7 +1394,7 @@
         P(("wide", "narrow"), None),
     )
     return jax.shard_map(
-        functools.partial(local, mesh.shape["wide"], mesh.shape["narrow"]),
+        body,
         mesh=mesh,
         in_specs=placed,
         out_specs=(

time: 859 us -> 665 us (0.77)
  matrix products: 368 us -> 165 us
  local copies, waits for them, and re-layouts: 148 us -> 118 us
  Pallas kernels: 278 us -> 303 us
  other arithmetic: 55.5 us -> 66.7 us
    dot_general x47 -> x20, matrix products: 302 us -> 96.4 us  [the longest x4 59.5 us: one_group(): part('hij,ijb->bh', grad_scores, onehot)]
    dot_general x8 -> x0, local copies, waits for them, and re-layouts: 42 us -> none  [group_scores(): jnp.einsum('ijb,bh->hij', onehot, table_group, preferred_element_type=jnp...]
    pallas_call x1, Pallas kernels: 122 us -> 158 us  [forward_all(): pl.pallas_call(functools.partial(forward_kernel, nn, shapes), out_shape=o...]
    dynamic_slice x0 -> x8, local copies, waits for them, and re-layouts: none -> 23.6 us  [local_fast(): lax.map(one_group, (split_heads(queries), split_heads(keys_all), split_he...]
    pallas_call x1, Pallas kernels: 156 us -> 145 us  [scatter_all(): pl.pallas_call(functools.partial(scatter_kernel, nn, few, many), out_shap...]
    eq x1, other arithmetic: 12 us -> 23.3 us  [local_fast(): lay_bucket[:, :, None] == buckets]
    convert_element_type x10 -> x5, local copies, waits for them, and re-layouts: 18.6 us -> 13 us  [the longest x4 12.5 us: one_group(): grad_scores = (share * (grad_probs - jnp.sum(share * grad_probs, axis=-1,...]
where the time goes in v2:
time: 665 us; the launch traced here: 655 us
  Pallas kernels  303 us (46%)
  matrix products  165 us (25%)
  local copies, waits for them, and re-layouts  118 us (18%)
  other arithmetic  66.7 us (10%)
    pallas_call x1, Pallas kernels, forward_all(): pl.pallas_call(functools.partial(forward_kernel, nn, shapes), out_shape=o...  158 us
    pallas_call x1, Pallas kernels, scatter_all(): pl.pallas_call(functools.partial(scatter_kernel, nn, few, many), out_shap...  145 us
    dot_general x4, matrix products, one_group(): part('hij,ijb->bh', grad_scores, onehot)  59.5 us
    dot_general x7, matrix products, contract_cols(): lax.dot_general(left, right, (((1,), (1,)), ((), ())), preferred_element_...  34.9 us
    dot_general x7, matrix products, contract_rows(): lax.dot_general(left, right, (((0,), (0,)), ((), ())), preferred_element_...  34.1 us
    concatenate x2, local copies, waits for them, and re-layouts, scatter_fast(): jnp.concatenate([pairs] + [columns(grad, 512) for grad in (grad_output, g...  29.2 us
    dynamic_slice x8, local copies, waits for them, and re-layouts, local_fast(): lax.map(one_group, (split_heads(queries), split_heads(keys_all), split_he...  23.6 us
    eq x1, other arithmetic, local_fast(): lay_bucket[:, :, None] == buckets  23.3 us

profile of v2, /device:TPU:0, one launch (start us, length us, event | category | flops | bytes accessed | tf_op | source)
XLA Modules:
  0.0 655.3 jit_solution(13214376463761849659)
XLA Ops:
  4.3 158.2 %shard_map.255 = (f32[256,128]{1,0:T(8,128)}, bf16[1024,1024]{1,0:T(8,128)(2,1)}, bf16[1024,1024]{1,0:T(8,128)(2,1)}, bf16[1024,1024]{1,0:T(8,128)(2,1)}, bf16[1...) custom-call(s32[1]{0:T(128)S(6)} %copy.109.refs_0_, ...), custom_call_target="tpu_custom_call" | custom-call | tf_op jit(solution)/shard_map/pallas_call | solution.py:719
  162.6 6.3 fusion.43
  168.9 4.5 fusion.62
  175.2 9.3 %multiply_reduce_fusion = (f32[1024]{0:T(1024)S(1)}, f32[512]{0:T(512)S(1)}, f32[512,1024]{1,0:T(8,128)S(1)}) fusion(f32[512,1024]{1,0:T(8,128)S(1)} %copy-done.2, f32[512]{0:T(512)S(1)} %fusion.58, f32[1024]{0:T(1024)S(1)} %mul.112, f32[512,1024]{1,0:T(8,128)} %fusion.62, bf16[1024,2816]{1,0:T(8,128)(2,1)} %get-tuple-element.113, ...), kind=kOutput, calls=%fused_computation.54 | convolution fusion | flops 2960783872 | bytes 20721664 | tf_op jit(solution)/shard_map/dot_general | solution.py:48
  195.4 23.3 %iota_compare_fusion = (pred[512,512,32]{1,2,0:T(8,128)(4,1)}, pred[512,512,32]{1,2,0:T(8,128)(4,1)}) fusion(s32[512,512]{1,0:T(8,128)S(1)} %copy-done.7, s32[512,512]{1,0:T(8,128)S(1)} %copy-done.6), kind=kLoop, calls=%fused_computation.34 | loop fusion | flops 16777216 | bytes 18874368 | tf_op jit(solution)/shard_map/eq | solution.py:1101
  218.7 15.9 %add_convert_fusion = bf16[512,512,64]{1,2,0:T(8,128)(2,1)} fusion(pred[512,512,32]{1,2,0:T(8,128)(4,1)} %get-tuple-element.201, pred[512,512,32]{1,2,0:T(8,128)(4,1)} %get-tuple-element.202), kind=kLoop, calls=%fused_computation.33 | loop fusion | flops 33554432 | bytes 50331648 | tf_op jit(solution)/shard_map/concatenate | solution.py:1098
  234.7 142.6 %while.17 = (s32[]{:T(128)}, bf16[4,512,4,64]{1,3,2,0:T(8,128)(2,1)}, bf16[4,512,4,64]{1,3,2,0:T(8,128)(2,1)}, bf16[4,512,4,64]{1,3,2,0:T(8,128)(2,1)}, f32[4,64...) while((s32[]{:T(128)}, ...), condition=%wide.region_4.5_spmd, body=%wide.region_2.4_spmd.sunk | while | flops 678819840 | bytes 79714968 | solution.py:1138
  245.1 3.1 copy.83
  248.2 14.9 %fusion.118 = f32[4,64,4]{1,2,0:T(4,128)S(1)} fusion(f32[4,64,4]{1,2,0:T(4,128)S(1)} %get-tuple-element.290, s32[]{:T(128)} %get-tuple-element.286, bf16[4,512,512]{2,0,1:T(4,128)(2,1)} %copy.83, bf16[512,512,64]{1,2,0:T(8,128)(2,1)} %get-tuple-element.308), kind=kOutput, calls=%fused_computation.16.clone.1 | convolution fusion | flops 134217728 | bytes 35653636 | tf_op jit(solution)/shard_map/while/body/eval_jaxpr/hij,ijb->bh/dot_general | solution.py:1135
  283.8 14.9 %fusion.118 = f32[4,64,4]{1,2,0:T(4,128)S(1)} fusion(f32[4,64,4]{1,2,0:T(4,128)S(1)} %get-tuple-element.290, s32[]{:T(128)} %get-tuple-element.286, bf16[4,512,512]{2,0,1:T(4,128)(2,1)} %copy.83, bf16[512,512,64]{1,2,0:T(8,128)(2,1)} %get-tuple-element.308), kind=kOutput, calls=%fused_computation.16.clone.1 | convolution fusion | flops 134217728 | bytes 35653636 | tf_op jit(solution)/shard_map/while/body/eval_jaxpr/hij,ijb->bh/dot_general | solution.py:1135
  319.5 14.9 %fusion.118 = f32[4,64,4]{1,2,0:T(4,128)S(1)} fusion(f32[4,64,4]{1,2,0:T(4,128)S(1)} %get-tuple-element.290, s32[]{:T(128)} %get-tuple-element.286, bf16[4,512,512]{2,0,1:T(4,128)(2,1)} %copy.83, bf16[512,512,64]{1,2,0:T(8,128)(2,1)} %get-tuple-element.308), kind=kOutput, calls=%fused_computation.16.clone.1 | convolution fusion | flops 134217728 | bytes 35653636 | tf_op jit(solution)/shard_map/while/body/eval_jaxpr/hij,ijb->bh/dot_general | solution.py:1135
  355.1 14.9 %fusion.118 = f32[4,64,4]{1,2,0:T(4,128)S(1)} fusion(f32[4,64,4]{1,2,0:T(4,128)S(1)} %get-tuple-element.290, s32[]{:T(128)} %get-tuple-element.286, bf16[4,512,512]{2,0,1:T(4,128)(2,1)} %copy.83, bf16[512,512,64]{1,2,0:T(8,128)(2,1)} %get-tuple-element.308), kind=kOutput, calls=%fused_computation.16.clone.1 | convolution fusion | flops 134217728 | bytes 35653636 | tf_op jit(solution)/shard_map/while/body/eval_jaxpr/hij,ijb->bh/dot_general | solution.py:1135
  377.3 4.7 fusion.66
  385.0 6.3 fusion.38
  392.4 4.0 convolution_convert_fusion.8
  396.4 7.7 %convolution_convert_fusion.3 = bf16[1024,2816]{1,0:T(8,128)(2,1)} fusion(bf16[512,1024]{1,0:T(8,128)(2,1)S(1)} %copy-done.22, f32[512,2816]{1,0:T(8,128)} %copy-done.26, bf16[512,2816]{1,0:T(8,128)(2,1)S(1)} %copy-done.18), kind=kOutput, calls=%fused_computation.40 | convolution fusion | flops 2959998976 | bytes 15466496 | tf_op jit(solution)/shard_map/dot_general | solution.py:42
  404.1 8.3 %copy.57 = bf16[1024,2816]{0,1:T(8,128)(2,1)} copy(bf16[1024,2816]{1,0:T(8,128)(2,1)} %convolution_convert_fusion.3) | data formatting | bytes 11534336 | tf_op jit(solution)/shard_map/convert_element_type | solution.py:1199
  412.4 9.5 %convolution_convert_fusion.2 = bf16[1024,2816]{1,0:T(8,128)(2,1)} fusion(bf16[512,1024]{1,0:T(8,128)(2,1)} %get-tuple-element.128, f32[512,2816]{1,0:T(8,128)} %copy-done.26, bf16[512,2816]{1,0:T(8,128)(2,1)} %get-tuple-element.112), kind=kOutput, calls=%fused_computation.39 | convolution fusion | flops 2959998976 | bytes 15466496 | tf_op jit(solution)/shard_map/dot_general | solution.py:42
  421.9 8.2 %copy.58 = bf16[1024,2816]{0,1:T(8,128)(2,1)} copy(bf16[1024,2816]{1,0:T(8,128)(2,1)} %convolution_convert_fusion.2) | data formatting | bytes 11534336 | tf_op jit(solution)/shard_map/convert_element_type | solution.py:1199
  430.2 13.0 %maximum_dynamic-update-slice_fusion = bf16[19,1024,512]{1,2,0:T(8,128)(2,1)} fusion(bf16[11,1024,256]{1,2,0:T(8,128)(2,1)} %bitcast.208, bf16[11,1024,256]{1,2,0:T(8,128)(2,1)} %bitcast.207), kind=kLoop, calls=%fused_computation.36 | loop fusion | flops 23068672 | bytes 23068672
  455.0 27.7 %copy.59 = bf16[19,1024,512]{2,1,0:T(8,128)(2,1)} copy(bf16[19,1024,512]{1,2,0:T(8,128)(2,1)} %constant_dynamic-update-slice_fusion) | data formatting | bytes 39845888 | tf_op jit(solution)/shard_map/concatenate | solution.py:1204
  482.7 7.9 %convolution_convert_fusion.4 = bf16[2816,1024]{0,1:T(8,128)(2,1)} fusion(bf16[512,2816]{1,0:T(8,128)(2,1)} %get-tuple-element.127, bf16[512,1024]{1,0:T(8,128)(2,1)} %param.35, pred[512]{0:T(512)(128)(4,1)S(1)} %copy-done.15), kind=kOutput, calls=%fused_computation.41 | convolution fusion | flops 2957246464 | bytes 9699840 | tf_op jit(solution)/shard_map/dot_general | solution.py:42
  490.6 8.3 %copy.56 = bf16[2816,4,256]{2,0,1:T(8,128)(2,1)} copy(bf16[2816,4,256]{0,2,1:T(8,128)(2,1)} %bitcast.210) | data formatting | bytes 11534336 | tf_op jit(solution)/shard_map/reshape | solution.py:1199
  498.9 144.5 %shard_map.256 = (f32[4,88,256]{2,1,0:T(8,128)}, f32[19,32,512]{2,1,0:T(8,128)}, f32[8,128]{1,0:T(8,128)}, bf16[4,4,352,256]{3,2,1,0:T(8,128)(2,1)}, bf16[19,4,128,512]{3,2,1,0:T(8,128)(2,1)}) custom-call(bf16[4,4,2,352,256]{4,3,2,1,0:T(8,128)(2,1)} %bitcast.206, bf16[19,4,2,128,512]{4,3,2,1,0:T(8,128)(2,1)} %bitcast.204, f32[4,2,32,128]{3,2,1,0:T(8,128)} %bitcast.218), custom_call_target="tpu_custom_call" | custom-call | tf_op jit(solution)/shard_map/pallas_call | solution.py:1017
  (142 shorter events, 122.9 us)
Async XLA Ops:
  162.5 22.0 %copy-start.14 = (pred[512]{0:T(512)(128)(4,1)}, pred[512]{0:T(512)(128)(4,1)S(1)}, u32[]{:S(2)}) copy-start(pred[512]{0:T(512)(128)(4,1)S(1)} %iota_compare_fusion.4) | copy-start | bytes 1540
  162.6 6.3 copy-start.16
  162.6 6.3 copy-start.17
  168.9 4.5 copy-start.26
  168.9 4.5 copy-start.2
  175.2 9.3 %copy-start.10 = (bf16[512,1024]{1,0:T(8,128)(2,1)S(1)}, bf16[512,1024]{1,0:T(8,128)(2,1)}, u32[]{:S(2)}) copy-start(bf16[512,1024]{1,0:T(8,128)(2,1)} %param.35) | copy-start | bytes 3145732
  184.5 2.0 copy-start.20
  188.4 7.0 %copy-start.6 = (s32[512,512]{1,0:T(8,128)S(1)}, s32[512,512]{1,0:T(8,128)}, u32[]{:S(2)}) copy-start(s32[512,512]{1,0:T(8,128)} %refs_2_.1) | copy-start | bytes 3145732
  188.4 7.0 %copy-start.7 = (s32[512,512]{1,0:T(8,128)S(1)}, s32[512,512]{1,0:T(8,128)}, u32[]{:S(2)}) copy-start(s32[512,512]{1,0:T(8,128)} %refs_3_.1) | copy-start | bytes 3145732
  276.3 1.9 copy-start
  311.9 1.9 copy-start
  377.3 4.7 copy-start.19
  377.3 4.7 copy-start.23
  382.0 2.6 copy-start.12
  382.0 2.7 copy-start.1
  385.0 7.4 %copy-start.4 = (f32[512,1024]{1,0:T(8,128)S(1)}, f32[512,1024]{1,0:T(8,128)}, u32[]{:S(2)}) copy-start(f32[512,1024]{1,0:T(8,128)} %copy-done.3) | copy-start | bytes 6291460
  392.4 4.0 copy-start.18
  392.4 4.0 copy-start.22
  430.2 13.0 %copy-start.8 = (bf16[1024,1024]{0,1:T(8,128)(2,1)S(1)}, bf16[1024,1024]{0,1:T(8,128)(2,1)}, u32[]{:S(2)}) copy-start(bf16[1024,1024]{0,1:T(8,128)(2,1)} %convolution_convert_fusion.8) | copy-start | bytes 6291460
  443.1 2.3 copy-start.24
  455.0 27.7 %copy-start.15 = (pred[512]{0:T(512)(128)(4,1)S(1)}, pred[512]{0:T(512)(128)(4,1)}, u32[]{:S(2)}) copy-start(pred[512]{0:T(512)(128)(4,1)} %copy-done.14) | copy-start | bytes 1540
  643.4 6.7 %copy-start.11 = (f32[4,88,256]{2,1,0:T(8,128)S(1)}, f32[4,88,256]{2,1,0:T(8,128)}, u32[]{:S(2)}) copy-start(f32[4,88,256]{2,1,0:T(8,128)} %get-tuple-element.133) | copy-start | bytes 1081348
  643.5 7.4 %copy-start.13 = (f32[8,128]{1,0:T(8,128)S(1)}, f32[8,128]{1,0:T(8,128)}, u32[]{:S(2)}) copy-start(f32[8,128]{1,0:T(8,128)} %get-tuple-element.134) | copy-start | bytes 12292
  643.5 8.6 %copy-start.5 = (f32[512,1024]{1,0:T(8,128)S(1)}, f32[512,1024]{1,0:T(8,128)}, u32[]{:S(2)}) copy-start(f32[512,1024]{1,0:T(8,128)} %get-tuple-element.200) | copy-start | bytes 6291460
  (6 other events, 10.1 us)

commit v3 on v2

--- a/solution.py
+++ b/solution.py
@@ -13,6 +13,9 @@
 IMG = 196
 RING = 6
 SCATTER_COPIES = 10
+LAGS = 4
+FFN_LAG = 8
+BACK_QB = 16
 TILE = 256
 QB = 8
 GELU_SCALE = 0.7978845608028654
@@ -427,7 +430,7 @@
     refs = refs[4 + count :]
     fulls, refs = refs[:count], refs[count:]
     saved, refs = refs[:10], refs[10:]
-    (out_h, na_h, q_h, k_h, v_h, att_h, hid_h, nf_h, mix_h, probs_h) = saved
+    (out_h, na_t, q_t, k_h, v_h, att_t, hid_h, nf_t, mix_t, probs_h) = saved
     (slope_h, act_h), refs = refs[:2], refs[2:]
     (
         line,
@@ -454,6 +457,8 @@
         w_wide,
         w_down,
         gains,
+        turned,
+        mixed_t,
         send_sem,
         recv_sem,
         gather_sem,
@@ -498,6 +503,20 @@
     g[Q].spread()
     g[V].start()
     leaving = []
+    turning = {}
+
+    def turn_out(slot, source, target):
+        if slot in turning:
+            turning[slot].wait()
+
+        def one(tile, carry):
+            at = pl.ds(pl.multiple_of(tile * TILE, TILE), TILE)
+            turned[slot, at, :] = source[:, at].T
+            return carry
+
+        lax.fori_loop(0, width // TILE, one, 0)
+        turning[slot] = move(turned.at[slot], target)
+
     for copy in arriving:
         copy.wait()
     small_in.wait()
@@ -515,7 +534,7 @@
         return carry
 
     lax.fori_loop(0, slots // 64, normalise, 0)
-    leaving.append(move(na, na_h))
+    turn_out(0, na, na_t)
     valid = iota((1, slots), 1) < occupied[0] + IMG
 
     def bias_block(block, carry):
@@ -552,7 +571,7 @@
         lax.fori_loop(0, width // TILE, one, 0)
 
     project(0, q)
-    leaving.append(move(q, q_h))
+    turn_out(1, q, q_t)
     g[GATE].spread()
     g[UP].start()
     g[O].forward()
@@ -606,7 +625,7 @@
     lax.fori_loop(2, 5, attend, 0)
     g[GATE].last()
     lax.fori_loop(5, pairs, attend, 0)
-    leaving.append(move(att, att_h))
+    turn_out(0, att, att_t)
     g[DOWN].spread()
     g[UP].forward()
     g[GATE].done()
@@ -629,7 +648,7 @@
         return carry
 
     lax.fori_loop(0, slots // 64, normalise_two, 0)
-    leaving.append(move(nf, nf_h))
+    turn_out(1, nf, nf_t)
     g[UP].last()
     g[DOWN].forward()
     g[UP].done()
@@ -643,6 +662,7 @@
         return (
             pltpu.make_async_copy(slope.at[turn], slope_h.at[:, at], ring_sem.at[2 + turn]),
             pltpu.make_async_copy(act.at[turn], act_h.at[:, at], ring_sem.at[4 + turn]),
+            pltpu.make_async_copy(mixed_t.at[turn], mix_t.at[at], ring_sem.at[6 + turn]),
         )
 
     def ffn_tile(tile, carry):
@@ -661,7 +681,9 @@
         half = 0.5 * (1.0 + bend)
         active = gate * half
         rise = half + 0.5 * gate * (1.0 - bend * bend) * GELU_SCALE * (1.0 + 3.0 * GELU_CUBE * square)
-        mix[:, at] = (active * up).astype(BF)
+        mixed = (active * up).astype(BF)
+        mix[:, at] = mixed
+        mixed_t[turn] = mixed.T
         act[turn] = active.astype(BF)
         slope[turn] = (up * rise).astype(BF)
         for copy in ffn_out(tile):
@@ -672,7 +694,6 @@
     lax.fori_loop(0, tiles // 2, ffn_tile, 0)
     g[DOWN].last()
     lax.fori_loop(tiles // 2, tiles, ffn_tile, 0)
-    leaving.append(move(mix, mix_h))
     g[DOWN].done()
     move(fulls[DOWN], w_down).wait()
     valid_rows = iota((slots, 1), 0) < occupied[0] + IMG
@@ -683,10 +704,9 @@
         na[:, at] = jnp.where(valid_rows, result, 0.0).astype(BF)
         return carry
 
-    leaving[0].wait()
     lax.fori_loop(0, width // TILE, down_tile, 0)
     move(na, out_h).wait()
-    for copy in leaving[1:]:
+    for copy in leaving + list(turning.values()):
         copy.wait()
     for pair in (pairs - 2, pairs - 1):
         probs_out(pair).wait()
@@ -712,7 +732,9 @@
         jax.ShapeDtypeStruct((rows * devices, columns), shard.dtype)
         for (rows, columns), shard in zip(shapes, shards)
     ]
-    out_shape += [low] * 6 + [full, low, wide]
+    low_t = jax.ShapeDtypeStruct((width, slots), BF)
+    wide_t = jax.ShapeDtypeStruct((ffn, slots), BF)
+    out_shape += [low, low_t, low_t, low, low, low_t, full, low_t, wide_t]
     out_shape += [jax.ShapeDtypeStruct((H, slots, slots), BF), wide, wide]
     hbm = pl.BlockSpec(memory_space=pl.ANY)
     page = pltpu.VMEM((slots, width), BF)
@@ -746,11 +768,13 @@
             pltpu.VMEM((2, width, ffn), BF),
             pltpu.VMEM((ffn, width), BF),
             pltpu.VMEM((8, width), F32),
+            pltpu.VMEM((2, width, slots), BF),
+            pltpu.VMEM((2, TILE, slots), BF),
             pltpu.SemaphoreType.DMA((copies,)),
             pltpu.SemaphoreType.DMA((copies,)),
             pltpu.SemaphoreType.DMA((len(shards),)),
             pltpu.SemaphoreType.DMA((64,)),
-            pltpu.SemaphoreType.DMA((6,)),
+            pltpu.SemaphoreType.DMA((8,)),
         ],
         compiler_params=pltpu.CompilerParams(
             collective_id=0, has_side_effects=True, vmem_limit_bytes=63 * 2**20
@@ -882,6 +906,24 @@
             total = total + self.in_line[slot, step - 1, : self.rows].astype(F32)
         return total
 
+    def pump(self, index, out, made=None):
+        index = jnp.int32(index)
+        made = self.chunks if made is None else made
+        idle = index >= made if made < self.chunks else False
+        for lag, action in enumerate((self.fetch, self.add_core, self.add_corner, self.add_square, self.finish)):
+            chunk = index - lag
+            ready = jnp.logical_and(chunk >= 0, chunk < self.chunks)
+            if made < self.chunks:
+                ready = jnp.logical_and(ready, jnp.logical_not(idle))
+
+            @pl.when(ready)
+            def _(chunk=chunk, action=action):
+                action(chunk, out) if action == self.finish else action(chunk)
+
+    def finish(self, chunk, out):
+        out[chunk] = self.total(chunk)
+        self.wait_sent(chunk)
+
     def wait_sent(self, chunk):
         self.core_copy(chunk).wait_send()
         for p, part in enumerate(self.parts):
@@ -889,57 +931,6 @@
                 self.hop(chunk, p, mask).wait_send()
         for step in range(1, self.links.nn):
             self.line_copy(chunk, step).wait_send()
-
-
-def scatter_kernel(nn, few, many, few_ref, many_ref, small_ref, few_out, many_out, small_out, few_came, many_came, *refs):
-    few_slots, many_slots = refs[:6], refs[6:12]
-    small_came, small_round, small_line, small_mine, send_sem, recv_sem = refs[12:]
-    links = Links(nn, send_sem, recv_sem)
-    links.greet()
-    sets = []
-    base = 0
-    for (chunks, rows, columns), grads, came, slots in (
-        (few, few_ref, few_came, few_slots),
-        (many, many_ref, many_came, many_slots),
-    ):
-        sets.append(Scatter(links, chunks, rows, columns, grads, came, slots, base))
-        base += chunks * SCATTER_COPIES
-    links.used = base
-
-    def run(scatter, out):
-        chunks = scatter.chunks
-
-        def each(chunk, carry):
-            scatter.trade(chunk)
-            return carry
-
-        lax.fori_loop(0, chunks, each, 0)
-
-        def step(index, carry):
-            for lag, action in enumerate(
-                (scatter.fetch, scatter.add_core, scatter.add_corner, scatter.add_square)
-            ):
-                chunk = index - lag
-
-                @pl.when(jnp.logical_and(chunk >= 0, chunk < chunks))
-                def _(chunk=chunk, action=action):
-                    action(chunk)
-
-            chunk = index - 4
-
-            @pl.when(chunk >= 0)
-            def _(chunk=chunk):
-                out[chunk] = scatter.total(chunk)
-                scatter.wait_sent(chunk)
-
-            return carry
-
-        lax.fori_loop(0, chunks + 4, step, 0)
-
-    run(sets[0], few_out)
-    run(sets[1], many_out)
-    scatter_small(links, small_ref, small_out, small_came, small_round, small_line, small_mine)
-    links.finish()
 
 
 def scatter_small(links, grads, out, came, round_in, line_in, mine):
@@ -982,57 +973,526 @@
     return (rows + 15) // 16 * 16
 
 
-def scatter_slots(squares, nn, rows, columns):
+def scatter_slots(squares, nn, rows, columns, ring):
     half = columns // 2
     return [
-        pltpu.VMEM((RING, squares, nn * rows, columns), BF),
+        pltpu.VMEM((ring, squares, nn * rows, columns), BF),
         pltpu.VMEM((2, squares, nn * rows, columns), BF),
-        pltpu.VMEM((RING, 6, nn * rows, half), BF),
-        pltpu.VMEM((RING, nn, padded(rows), columns), BF),
-        pltpu.VMEM((RING, nn - 1, padded(rows), columns), BF),
+        pltpu.VMEM((ring, 6, nn * rows, half), BF),
+        pltpu.VMEM((ring, nn, padded(rows), columns), BF),
+        pltpu.VMEM((ring, nn - 1, padded(rows), columns), BF),
         pltpu.SemaphoreType.DMA((2, 2)),
     ]
 
 
-def scatter_all(nw, nn, few_grads, many_grads, small):
+def norm_pull(values, gain, grad):
+    scale = lax.rsqrt(jnp.mean(values * values, axis=-1, keepdims=True) + RMS_EPSILON)
+    scaled = grad * gain
+    along = jnp.mean(scaled * values, axis=-1, keepdims=True)
+    share = grad * values * scale
+    return scale * scaled - values * (scale * scale * scale * along), share
+
+
+def fold_rows(values):
+    return jnp.sum(values.reshape(values.shape[0] // 8, 8, values.shape[1]), axis=0)
+
+
+def pack_row(row, first, each, devices):
+    total = row.shape[1]
+    shape = (128, total)
+    pick = jnp.where(iota(shape, 0) == first + lax.rem(iota(shape, 1), each), 1.0, 0.0)
+    shape = (devices, total)
+    mine = jnp.where(iota(shape, 1) // each == iota(shape, 0), row, 0.0)
+    return lax.dot_general(
+        mine,
+        pick,
+        (((1,), (1,)), ((), ())),
+        preferred_element_type=F32,
+        precision=lax.Precision.HIGHEST,
+    )
+
+
+def backward_kernel(nn, few_facts, many_facts, *refs):
+    occupied, refs = refs[0], refs[1:]
+    (
+        tokens,
+        rel_hbm,
+        lay_hbm,
+        cotangent,
+        small_h,
+        query_h,
+        key_h,
+        value_h,
+        output_h,
+        gate_h,
+        up_h,
+        down_h,
+        na_t,
+        q_t,
+        k_h,
+        v_h,
+        att_t,
+        hid_h,
+        nf_t,
+        mix_t,
+        probs_h,
+        slope_h,
+        act_h,
+    ) = refs[:23]
+    refs = refs[23:]
+    (rows_out, few_out, many_out, small_out, few_grads, many_grads, few_came, many_came) = refs[:8]
+    few_slots, many_slots, refs = refs[8:14], refs[14:20], refs[20:]
+    (
+        x,
+        rel,
+        lay,
+        small,
+        gains,
+        grad,
+        left,
+        left_att,
+        acc,
+        hid,
+        wd_s,
+        wg_s,
+        wu_s,
+        slope_s,
+        act_s,
+        few_stage,
+        many_stage,
+        branch,
+        w_one,
+        pull,
+        pull_t,
+        qt,
+        k,
+        v,
+        probs,
+        pieces,
+        dq,
+        dkt,
+        dvt,
+        onehot,
+        table,
+        sums,
+        small_grads,
+        small_came,
+        small_round,
+        small_line,
+        small_mine,
+        send_sem,
+        recv_sem,
+        local_sem,
+        tile_sem,
+        stage_sem,
+        probs_sem,
+    ) = refs
+    slots, width = x.shape
+    links = Links(nn, send_sem, recv_sem)
+    numbers = iter(range(64))
+
+    def move(src, dst):
+        copy = pltpu.make_async_copy(src, dst, local_sem.at[next(numbers)])
+        copy.start()
+        return copy
+
+    ffn = mix_t.shape[0]
+    tiles = ffn // TILE
+    mix_in = move(mix_t, pieces.at[pl.ds(0, ffn)])
+    grad_in = move(cotangent, grad)
+    nf_in = move(nf_t, left)
+
+    def tile_copies(tile):
+        turn = lax.rem(tile, 2)
+        at = pl.ds(pl.multiple_of(tile * TILE, TILE), TILE)
+        return [
+            pltpu.make_async_copy(src, dst.at[turn], tile_sem.at[turn, index])
+            for index, (src, dst) in enumerate(
+                (
+                    (down_h.at[at], wd_s),
+                    (gate_h.at[:, at], wg_s),
+                    (up_h.at[:, at], wu_s),
+                    (slope_h.at[:, at], slope_s),
+                    (act_h.at[:, at], act_s),
+                )
+            )
+        ]
+
+    for copy in tile_copies(0):
+        copy.start()
+    later = [move(hid_h, hid), move(small_h, small), move(att_t, left_att), move(output_h, w_one.at[0])]
+    later += [move(q_t, qt), move(k_h, k), move(v_h, v)]
+    last = [move(tokens, x), move(rel_hbm, rel), move(lay_hbm, lay), move(value_h, w_one.at[1])]
+    links.greet()
+    few = Scatter(links, *few_facts, few_grads, few_came, few_slots, 0)
+    base = few_facts[0] * SCATTER_COPIES
+    many = Scatter(links, *many_facts, many_grads, many_came, many_slots, base)
+    links.used = base + many_facts[0] * SCATTER_COPIES
+
+    def stage_copy(scatter, stage, chunk, first):
+        turn = lax.rem(chunk, 2)
+        return pltpu.make_async_copy(
+            stage.at[turn], scatter.grads.at[chunk], stage_sem.at[first + turn]
+        )
+
+    def few_copy(chunk):
+        return stage_copy(few, few_stage, chunk, 0)
+
+    def many_copy(chunk):
+        return stage_copy(many, many_stage, chunk, 2)
+
+    grad_in.wait()
+    valid_rows = iota((slots, 1), 0) < occupied[0] + IMG
+
+    def keep_valid(tile, carry):
+        at = pl.ds(pl.multiple_of(tile * TILE, TILE), TILE)
+        grad[:, at] = jnp.where(valid_rows, grad[:, at].astype(F32), 0.0).astype(BF)
+        return carry
+
+    lax.fori_loop(0, width // TILE, keep_valid, 0)
+    mix_in.wait()
+    block = few.block
+
+    def down_chunk(chunk, carry):
+        at = pl.ds(pl.multiple_of(chunk * few.columns, few.columns), few.columns)
+        turn = lax.rem(chunk, 2)
+
+        def one(index, carry):
+            rows = pl.ds(pl.multiple_of(index * block, 16), block)
+            few_stage[turn, index // 2, lax.rem(index, 2)] = dot(pieces[rows, :], grad[:, at]).astype(BF)
+            return carry
+
+        lax.fori_loop(0, ffn // block, one, 0)
+        few_copy(chunk).start()
+
+        @pl.when(chunk >= 1)
+        def _():
+            few_copy(chunk - 1).wait()
+            few.trade(chunk - 1)
+
+        return carry
+
+    lax.fori_loop(0, few.chunks, down_chunk, 0)
+    few_copy(few.chunks - 1).wait()
+    few.trade(few.chunks - 1)
+    nf_in.wait()
+
+    def put(chunk, low, value):
+        shape = many_stage.shape[1:4]
+        many_stage[lax.rem(chunk, 2), :, :, :, low : low + value.shape[1]] = value.astype(BF).reshape(
+            shape + (value.shape[1],)
+        )
+
+    def ffn_tile(tile, carry):
+        turn = lax.rem(tile, 2)
+
+        @pl.when(tile + 1 < tiles)
+        def _():
+            for copy in tile_copies(tile + 1):
+                copy.start()
+
+        for copy in tile_copies(tile):
+            copy.wait()
+        grad_mixed = dot_nt(grad[...], wd_s[turn])
+        gate_low = (grad_mixed * slope_s[turn].astype(F32)).astype(BF)
+        up_low = (grad_mixed * act_s[turn].astype(F32)).astype(BF)
+        put(tile, 0, dot(left[...], gate_low))
+        put(tile, TILE, dot(left[...], up_low))
+        many_copy(tile).start()
+
+        @pl.when(tile >= 1)
+        def _():
+            many_copy(tile - 1).wait()
+            many.trade(tile - 1)
+
+        for part in range(width // TILE):
+            at = slice(part * TILE, (part + 1) * TILE)
+            more = dot_nt(gate_low, wg_s[turn, at, :]) + dot_nt(up_low, wu_s[turn, at, :])
+            acc[:, at] = jnp.where(tile == 0, 0.0, acc[:, at]) + more
+        few.pump(tile, few_out)
+        many.pump(tile - FFN_LAG, many_out)
+        return carry
+
+    lax.fori_loop(0, tiles, ffn_tile, 0)
+    many_copy(tiles - 1).wait()
+    many.trade(tiles - 1)
+    done = tiles - FFN_LAG
+    for copy in later:
+        copy.wait()
+    na_in = move(na_t, left)
+    rows = small.reshape(small.shape[0] // 8, 8, 128)[:, 0, :]
+    devices = rows.shape[0]
+    each = width // devices
+    gains[0:1, :] = unpack_row(rows, 0, each, width)
+    gains[1:2, :] = unpack_row(rows, each, each, width)
+
+    def norm_two(index, total):
+        at = pl.ds(pl.multiple_of(index * 64, 64), 64)
+        part, share = norm_pull(hid[at, :], gains[1:2, :], acc[at, :])
+        whole = grad[at, :].astype(F32) + part
+        hid[at, :] = whole
+        branch[at, :] = whole.astype(BF)
+        return total + fold_rows(share)
+
+    zero = jnp.zeros((8, width), F32)
+    sums[0] = lax.fori_loop(0, slots // 64, norm_two, zero)
+
+    def emit(chunk, value):
+        put(chunk, 0, value)
+        many_copy(chunk).start()
+
+    def flush(chunk):
+        many_copy(chunk).wait()
+        many.trade(chunk)
+
+    wide = many.columns
+    for part in range(width // wide):
+        emit(tiles + part, dot(left_att[...], branch[:, part * wide : (part + 1) * wide]))
+    many.pump(done, many_out)
+    done += 1
+
+    def pull_tile(tile, carry):
+        at = pl.ds(pl.multiple_of(tile * TILE, TILE), TILE)
+        found = dot_nt(branch[...], w_one[0, at, :]).astype(BF)
+        pull[:, at] = found
+        pull_t[at, :] = found.T
+        return carry
+
+    lax.fori_loop(0, width // TILE, pull_tile, 0)
+    for part in range(width // wide):
+        flush(tiles + part)
+    made = tiles + width // wide
+    query_in = move(query_h, w_one.at[0])
+
+    def probs_copy(pair):
+        turn = lax.rem(pair, 2)
+        return pltpu.make_async_copy(probs_h.at[pl.ds(pair * 2, 2)], probs.at[turn], probs_sem.at[turn])
+
+    pairs = H // 2
+    probs_copy(0).start()
+
+    def attend_back(pair, carry):
+        @pl.when(pair + 1 < pairs)
+        def _():
+            probs_copy(pair + 1).start()
+
+        probs_copy(pair).wait()
+        turn = lax.rem(pair, 2)
+        at = pl.ds(pl.multiple_of(pair * 128, 128), 128)
+        low = iota((slots, 128), 1) < HD
+        keys, pulls, values = k[:, at], pull[:, at], v[:, at]
+        found = []
+        for side in range(2):
+            head = pair * 2 + side
+            mine = jnp.where(low if side == 0 else jnp.logical_not(low), pulls, 0)
+            share = probs[turn, side]
+            wanted = dot_nt(mine, values)
+            share_f = share.astype(F32)
+            joint = share_f * wanted
+            piece = (joint - share_f * jnp.sum(joint, axis=-1, keepdims=True)).astype(BF)
+            pieces[pl.ds(pl.multiple_of(head * slots, slots), slots), :] = piece
+            found.append(dot(piece, keys))
+            rows = pl.ds(pl.multiple_of(head * HD, HD), HD)
+            dkt[rows, :] = dot(qt[rows, :], piece).astype(BF)
+            dvt[rows, :] = dot(pull_t[rows, :], share).astype(BF)
+        dq[:, at] = jnp.where(low, found[0], found[1]).astype(BF)
+        many.pump(done + pair, many_out, made)
+        return carry
+
+    lax.fori_loop(0, pairs, attend_back, 0)
+    done = min(done + pairs, made)
+    for copy in last:
+        copy.wait()
+    na_in.wait()
+    for index, (grads, turned) in enumerate(((dvt, True), (dq, False), (dkt, True))):
+        for part in range(width // wide):
+            at = slice(part * wide, (part + 1) * wide)
+            chunk = made + index * (width // wide) + part
+            if index or part:
+                flush(chunk - 1)
+            if turned:
+                emit(chunk, dot_nt(left[...], grads[at, :]))
+            else:
+                emit(chunk, dot(left[...], grads[:, at]))
+        many.pump(done, many_out, made)
+        done = min(done + 1, made)
+    flush(many.chunks - 1)
+    table[...] = jnp.zeros_like(table)
+
+    def table_block_back(index, carry):
+        for query in range(BACK_QB):
+            for which, bucket in enumerate((rel, lay)):
+                row = bucket[pl.ds(index * BACK_QB + query, 1), :]
+                first = (query * 2 + which) * NB
+                onehot[first : first + NB, :] = ones_where(
+                    jnp.broadcast_to(row, (NB, slots)) == iota((NB, slots), 0)
+                )
+        heads = [
+            pieces[pl.ds(pl.multiple_of(head * slots + index * BACK_QB, BACK_QB), BACK_QB), :]
+            for head in range(H)
+        ]
+        table[...] += dot_nt(onehot[...], jnp.concatenate(heads, axis=0))
+        return carry
+
+    blocks = slots // BACK_QB
+    groups = 8
+
+    def table_group(group, carry):
+        lax.fori_loop(group * (blocks // groups), (group + 1) * (blocks // groups), table_block_back, 0)
+        many.pump(done + group, many_out)
+        return carry
+
+    lax.fori_loop(0, groups, table_group, 0)
+    done += groups
+    query_in.wait()
+
+    def turn_back(tile, carry):
+        at = pl.ds(pl.multiple_of(tile * TILE, TILE), TILE)
+        pull[:, at] = dvt[at, :].T
+        branch[:, at] = dkt[at, :].T
+        return carry
+
+    lax.fori_loop(0, width // TILE, turn_back, 0)
+
+    def first_two(tile, carry):
+        at = pl.ds(pl.multiple_of(tile * TILE, TILE), TILE)
+        acc[:, at] = dot_nt(pull[...], w_one[1, at, :]) + dot_nt(dq[...], w_one[0, at, :])
+        return carry
+
+    lax.fori_loop(0, width // TILE, first_two, 0)
+    key_in = move(key_h, w_one.at[0])
+    many.pump(done, many_out)
+    done += 1
+    key_in.wait()
+
+    def third(tile, carry):
+        at = pl.ds(pl.multiple_of(tile * TILE, TILE), TILE)
+        acc[:, at] += dot_nt(branch[...], w_one[0, at, :])
+        return carry
+
+    lax.fori_loop(0, width // TILE, third, 0)
+    many.pump(done, many_out)
+    done += 1
+
+    def norm_one(index, total):
+        at = pl.ds(pl.multiple_of(index * 64, 64), 64)
+        part, share = norm_pull(x[at, :].astype(F32), gains[0:1, :], acc[at, :])
+        hid[at, :] += part
+        return total + fold_rows(share)
+
+    sums[1] = lax.fori_loop(0, slots // 64, norm_one, zero)
+    rows_copy = move(hid, rows_out)
+    total = table[...]
+    mine = iota(total.shape, 0) // (2 * NB) == lax.rem(iota(total.shape, 1), BACK_QB)
+    folded = jnp.sum(
+        jnp.where(mine, total, 0.0).reshape(BACK_QB, 2 * NB, H * BACK_QB), axis=0
+    )
+    packed = pack_row(jnp.sum(sums[1], axis=0, keepdims=True), 0, each, devices)
+    packed += pack_row(jnp.sum(sums[0], axis=0, keepdims=True), each, each, devices)
+    for index in range(2):
+        shape = (H * BACK_QB, 128)
+        lane = 2 * each + H * index + iota(shape, 0) // BACK_QB
+        pick = jnp.where(iota(shape, 1) == lane, 1.0, 0.0)
+        packed += jnp.dot(
+            folded[index * NB : (index + 1) * NB],
+            pick,
+            preferred_element_type=F32,
+            precision=lax.Precision.HIGHEST,
+        )
+    small_grads[...] = jnp.zeros_like(small_grads)
+    for device in range(devices):
+        wide_at, z = divmod(device, nn)
+        small_grads[wide_at // 2, wide_at % 2, z * 8 : z * 8 + 1, :] = packed[device : device + 1]
+    scatter_small(links, small_grads, small_out, small_came, small_round, small_line, small_mine)
+
+    def rest(index, carry):
+        many.pump(index, many_out)
+        return carry
+
+    lax.fori_loop(done, many.chunks + LAGS, rest, 0)
+    rows_copy.wait()
+    links.finish()
+
+
+def backward_all(nw, nn, counts, page, weights, saved):
     squares = nw // 2
-
-    def facts(grads):
-        return (grads.shape[0], grads.shape[1] // (nw * nn), grads.shape[2])
-
-    few, many = facts(few_grads), facts(many_grads)
-    outs = []
+    devices = nw * nn
+    slots, width = page[0].shape
+    ffn = weights[5].shape[1]
+    few = (width // 256, ffn // devices, 256)
+    many = (ffn // TILE + 8, width // devices, 2 * TILE)
+    outs = [jax.ShapeDtypeStruct((slots, width), F32)]
     for chunks, rows, columns in (few, many):
         outs.append(jax.ShapeDtypeStruct((chunks, rows, columns), F32))
     outs.append(jax.ShapeDtypeStruct((8, 128), F32))
+    for chunks, rows, columns in (few, many):
+        outs.append(jax.ShapeDtypeStruct((chunks, squares, 2, nn * rows, columns), BF))
     for chunks, rows, columns in (few, many):
         outs.append(jax.ShapeDtypeStruct((chunks, squares, nn * rows, columns), BF))
     copies = (few[0] + many[0]) * SCATTER_COPIES + 16
     vmem = pl.BlockSpec(memory_space=pltpu.VMEM)
     hbm = pl.BlockSpec(memory_space=pl.ANY)
-    given = [
-        grads.reshape(grads.shape[0], squares, 2, -1, grads.shape[2])
-        for grads in (few_grads, many_grads)
-    ]
+    low = pltpu.VMEM((slots, width), BF)
+    turned = pltpu.VMEM((width, slots), BF)
+    full = pltpu.VMEM((slots, width), F32)
+    inputs = (counts,) + tuple(page) + tuple(weights) + tuple(saved)
     return pl.pallas_call(
-        functools.partial(scatter_kernel, nn, few, many),
+        functools.partial(backward_kernel, nn, few, many),
         out_shape=outs,
-        in_specs=[hbm, hbm, vmem],
-        out_specs=[vmem, vmem, vmem, hbm, hbm],
-        scratch_shapes=scatter_slots(squares, nn, few[1], few[2])
-        + scatter_slots(squares, nn, many[1], many[2])
+        in_specs=[pl.BlockSpec(memory_space=pltpu.SMEM)] + [hbm] * (len(inputs) - 1),
+        out_specs=[hbm, vmem, vmem, vmem, hbm, hbm, hbm, hbm],
+        scratch_shapes=scatter_slots(squares, nn, few[1], few[2], few[0])
+        + scatter_slots(squares, nn, many[1], many[2], RING)
         + [
+            low,
+            pltpu.VMEM((slots, slots), jnp.int32),
+            pltpu.VMEM((slots, slots), jnp.int32),
+            pltpu.VMEM((devices * 8, 128), F32),
+            pltpu.VMEM((8, width), F32),
+            low,
+            turned,
+            turned,
+            full,
+            full,
+            pltpu.VMEM((2, TILE, width), BF),
+            pltpu.VMEM((2, width, TILE), BF),
+            pltpu.VMEM((2, width, TILE), BF),
+            pltpu.VMEM((2, slots, TILE), BF),
+            pltpu.VMEM((2, slots, TILE), BF),
+            pltpu.VMEM((2, squares, 2, nn * few[1], few[2]), BF),
+            pltpu.VMEM((2, squares, 2, nn * many[1], many[2]), BF),
+            low,
+            pltpu.VMEM((2, width, width), BF),
+            low,
+            turned,
+            turned,
+            low,
+            low,
+            pltpu.VMEM((2, 2, slots, slots), BF),
+            pltpu.VMEM((H * slots, slots), BF),
+            low,
+            turned,
+            turned,
+            pltpu.VMEM((BACK_QB * 2 * NB, slots), BF),
+            pltpu.VMEM((BACK_QB * 2 * NB, H * BACK_QB), F32),
+            pltpu.VMEM((2, 8, width), F32),
+            pltpu.VMEM((squares, 2, nn * 8, 128), F32),
             pltpu.VMEM((squares, nn * 8, 128), F32),
             pltpu.VMEM((3, nn * 8, 128), F32),
             pltpu.VMEM((nn - 1, 8, 128), F32),
             pltpu.VMEM((squares, nn * 8, 128), F32),
             pltpu.SemaphoreType.DMA((copies,)),
             pltpu.SemaphoreType.DMA((copies,)),
+            pltpu.SemaphoreType.DMA((64,)),
+            pltpu.SemaphoreType.DMA((2, 5)),
+            pltpu.SemaphoreType.DMA((4,)),
+            pltpu.SemaphoreType.DMA((2,)),
         ],
         compiler_params=pltpu.CompilerParams(
-            collective_id=1, has_side_effects=True, vmem_limit_bytes=60 * 2**20
+            collective_id=1, has_side_effects=True, vmem_limit_bytes=63 * 2**20
         ),
-    )(*given, small.reshape(squares, 2, nn * 8, 128))[:3]
+    )(*inputs)[:4]
+
 
 def local_fast(
     nw,
@@ -1057,174 +1517,28 @@
     small = jnp.concatenate([gain_attn, gain_ffn, rel_table, lay_table]).astype(F32)
     small = jnp.pad(small[None], ((0, 7), (0, 128 - small.shape[0])))
     down = jnp.pad(w_down, ((0, padded(w_down.shape[0]) - w_down.shape[0]), (0, 0)))
-    (
-        full_small,
-        full_query,
-        full_key,
-        full_value,
-        full_output,
-        full_gate,
-        full_up,
-        full_down,
-        output,
-        normed_attn,
-        queries,
-        keys_all,
-        values_all,
-        attended,
-        hidden_one,
-        normed_ffn,
-        mixed,
-        probs,
-        slope,
-        active,
-    ) = forward_all(
-        nw,
-        nn,
-        ocr_counts,
-        tokens,
-        rel_bucket,
-        lay_bucket,
-        [small, w_query, w_key, w_value, w_output, w_gate, w_up, down],
-        w_down.shape[0],
-    )
-    rows = full_small.reshape(nw * nn, 8, 128)[:, 0]
-    each = gain_attn.shape[0]
-    full_gain_attn = rows[:, :each].reshape(-1)
-    full_gain_ffn = rows[:, each : 2 * each].reshape(-1)
-    slot = tokens.shape[0]
-    valid = jnp.arange(slot) < ocr_counts[0] + IMG
-    buckets = jnp.arange(NB)
-    onehot = jnp.concatenate(
-        [
-            (rel_bucket[:, :, None] == buckets).astype(jnp.bfloat16),
-            (lay_bucket[:, :, None] == buckets).astype(jnp.bfloat16),
-        ],
-        axis=2,
-    )
-    tokens_f = tokens.astype(F32)
-    grad_result = jnp.where(valid[:, None], cotangent.astype(jnp.float32), 0.0)
-    grad_low = grad_result.astype(jnp.bfloat16)
-    grad_down = contract_rows(mixed, grad_low)
-    grad_mixed = contract_cols(grad_low, full_down)
-    gate_low = (grad_mixed * slope.astype(F32)).astype(BF)
-    up_low = (grad_mixed * active.astype(F32)).astype(BF)
-    grad_gate = contract_rows(normed_ffn, gate_low)
-    grad_up = contract_rows(normed_ffn, up_low)
-    grad_normed_ffn = contract_cols(gate_low, full_gate) + contract_cols(up_low, full_up)
-    norm_value, norm_pull = jax.vjp(rms_scale, hidden_one, full_gain_ffn)
-    grad_hidden_part, grad_gain_ffn = norm_pull(grad_normed_ffn)
-    grad_hidden = grad_result + grad_hidden_part
-    branch_low = grad_hidden.astype(jnp.bfloat16)
-    grad_output = contract_rows(attended, branch_low)
-    grad_attended = contract_cols(branch_low, full_output).astype(jnp.bfloat16)
-
-    def one_group(operands):
-        query_group, key_group, value_group, grad_group, probs_low = operands
-        part = functools.partial(jnp.einsum, preferred_element_type=F32)
-        grad_values = part("hij,ihd->jhd", probs_low, grad_group)
-        grad_probs = part("ihd,jhd->hij", grad_group, value_group)
-        share = probs_low.astype(F32)
-        grad_scores = (
-            share * (grad_probs - jnp.sum(share * grad_probs, axis=-1, keepdims=True))
-        ).astype(BF)
-        return (
-            part("hij,jhd->ihd", grad_scores, key_group).astype(BF),
-            part("hij,ihd->jhd", grad_scores, query_group).astype(BF),
-            grad_values.astype(BF),
-            part("hij,ijb->bh", grad_scores, onehot),
-        )
-
-    grad_q, grad_k, grad_v, grad_tables = lax.map(
-        one_group,
-        (
-            split_heads(queries),
-            split_heads(keys_all),
-            split_heads(values_all),
-            split_heads(grad_attended),
-            probs.reshape(H // HEAD_GROUP, HEAD_GROUP, slot, slot),
-        ),
-    )
-    grad_table_all = jnp.moveaxis(grad_tables, 0, 1).reshape(2 * NB, H)
-    grad_queries, grad_keys, grad_values = join_heads(grad_q), join_heads(grad_k), join_heads(grad_v)
-    grad_rel = grad_table_all[:NB].reshape(NB * H)
-    grad_lay = grad_table_all[NB:].reshape(NB * H)
-    grad_query = contract_rows(normed_attn, grad_queries)
-    grad_key = contract_rows(normed_attn, grad_keys)
-    grad_value = contract_rows(normed_attn, grad_values)
-    grad_normed_attn = (
-        contract_cols(grad_queries, full_query)
-        + contract_cols(grad_keys, full_key)
-        + contract_cols(grad_values, full_value)
-    )
-    input_value, input_pull = jax.vjp(rms_scale, tokens_f, full_gain_attn)
-    grad_input_part, grad_gain_attn = input_pull(grad_normed_attn)
-    grad_tokens = grad_hidden + grad_input_part
-    return (output, grad_tokens) + scatter_fast(
-        nw,
-        nn,
-        grad_query,
-        grad_key,
-        grad_value,
-        grad_output,
-        grad_gate,
-        grad_up,
-        grad_down,
-        grad_gain_attn,
-        grad_gain_ffn,
-        grad_rel,
-        grad_lay,
-    )
-
-
-def scatter_fast(
-    nw,
-    nn,
-    grad_query,
-    grad_key,
-    grad_value,
-    grad_output,
-    grad_gate,
-    grad_up,
-    grad_down,
-    grad_gain_attn,
-    grad_gain_ffn,
-    grad_rel,
-    grad_lay,
-):
-    devices = nw * nn
-
-    def columns(grad, width):
-        return jnp.moveaxis(
-            grad.astype(BF).reshape(grad.shape[0], grad.shape[1] // width, width), 1, 0
-        )
-
-    few = columns(grad_down, 256)
-    pairs = jnp.concatenate([columns(grad_gate, 256), columns(grad_up, 256)], axis=2)
-    many = jnp.concatenate(
-        [pairs] + [columns(grad, 512) for grad in (grad_output, grad_query, grad_key, grad_value)]
-    )
-    parts = [
-        part.reshape(devices, -1) for part in (grad_gain_attn, grad_gain_ffn, grad_rel, grad_lay)
-    ]
-    small = jnp.concatenate(parts, axis=1)
-    small = jnp.zeros((devices, 8, 128), F32).at[:, 0, : small.shape[1]].set(small)
-    few_sum, many_sum, small_sum = scatter_all(nw, nn, few, many, small)
+    page = (tokens, rel_bucket, lay_bucket)
+    shards = [small, w_query, w_key, w_value, w_output, w_gate, w_up, down]
+    found = forward_all(nw, nn, ocr_counts, *page, shards, w_down.shape[0])
+    weights, output, saved = found[: len(shards)], found[len(shards)], found[len(shards) + 1 :]
+    grad_tokens, few, many, small = backward_all(
+        nw, nn, ocr_counts, page + (cotangent,), weights, saved
+    )
 
     def join(stack):
         return jnp.moveaxis(stack, 0, 1).reshape(stack.shape[1], -1)
 
-    tiles = pairs.shape[0]
-    owned = []
-    for index in range(4):
-        at = tiles + 2 * index
-        owned.append(join(many_sum[at : at + 2]))
-    gate, up = join(many_sum[:tiles, :, :256]), join(many_sum[:tiles, :, 256:])
-    at, cuts = 0, []
-    for part in parts:
-        cuts.append(small_sum[0, at : at + part.shape[1]])
-        at += part.shape[1]
-    return (owned[1], owned[2], owned[3], owned[0], gate, up, join(few_sum)) + tuple(cuts)
+    tiles = w_gate.shape[1] // TILE
+    grad_output, grad_value, grad_query, grad_key = (
+        join(many[tiles + 2 * index : tiles + 2 * index + 2]) for index in range(4)
+    )
+    gate, up = join(many[:tiles, :, :TILE]), join(many[:tiles, :, TILE:])
+    cuts, at = [], 0
+    for part in (gain_attn, gain_ffn, rel_table, lay_table):
+        cuts.append(small[0, at : at + part.shape[0]])
+        at += part.shape[0]
+    grads = (grad_query, grad_key, grad_value, grad_output, gate, up, join(few))
+    return (output, grad_tokens) + grads + tuple(cuts)
 
 
 def local(

time: 665 us -> 352 us (0.53); the launches traced: 655 us -> 351 us
  matrix products: 165 us -> 0 us
  local copies, waits for them, and re-layouts: 118 us -> 15 us
  other arithmetic: 66.7 us -> 1.38 us
  Pallas kernels: 303 us -> 333 us
    dot_general x34 -> x0, matrix products: 165 us -> none  [the longest x4 59.5 us: one_group(): part('hij,ijb->bh', grad_scores, onehot)]
    pallas_call x1, Pallas kernels: 145 us -> 176 us  [backward_all(): pl.pallas_call(functools.partial(backward_kernel, nn, few, many), out_sha...]
    convert_element_type x7 -> x0, local copies, waits for them, and re-layouts: 29.6 us -> none  [the longest x2 16.5 us: columns(): grad.astype(BF).reshape(grad.shape[0], grad.shape[1] // width, width)]
    concatenate x2 -> x0, local copies, waits for them, and re-layouts: 29.2 us -> none  [scatter_fast(): jnp.concatenate([pairs] + [columns(grad, 512) for grad in (grad_output, g...]
    dynamic_slice x8 -> x0, local copies, waits for them, and re-layouts: 23.6 us -> none  [local_fast(): lax.map(one_group, (split_heads(queries), split_heads(keys_all), split_he...]
    eq x1 -> x0, other arithmetic: 23.3 us -> none  [local_fast(): lay_bucket[:, :, None] == buckets]
    concatenate x2 -> x0, other arithmetic: 16 us -> none  [the longest x1 15.9 us: local_fast(): jnp.concatenate([(rel_bucket[:, :, None] == buckets).astype(jnp.bfloat16)...]
    unnamed x1 -> x0, other arithmetic: 13 us -> none
where the time goes in v3:
time: 352 us; the launch traced here: 351 us
  Pallas kernels  333 us (95%)
  local copies, waits for them, and re-layouts  15 us (4%)
    pallas_call x1, Pallas kernels, backward_all(): pl.pallas_call(functools.partial(backward_kernel, nn, few, many), out_sha...  176 us
    pallas_call x1, Pallas kernels, forward_all(): pl.pallas_call(functools.partial(forward_kernel, nn, shapes), out_shape=o...  158 us

profile of v3, /device:TPU:0, one launch (start us, length us, event | category | flops | bytes accessed | tf_op | source)
XLA Modules:
  0.0 351.2 jit_solution(11787040400081097742)
XLA Ops:
  1.3 1.4 fusion.9.refs_4_
  2.7 1.6 pad.12.refs_11_
  4.3 157.8 %shard_map.255 = (f32[256,128]{1,0:T(8,128)}, bf16[1024,1024]{1,0:T(8,128)(2,1)}, bf16[1024,1024]{1,0:T(8,128)(2,1)}, bf16[1024,1024]{1,0:T(8,128)(2,1)}, bf16[1...) custom-call(s32[1]{0:T(128)S(6)} %copy.45.refs_0_, ...), custom_call_target="tpu_custom_call" | custom-call | tf_op jit(solution)/shard_map/pallas_call | solution.py:741
  162.1 175.7 %shard_map.256 = (f32[512,1024]{1,0:T(8,128)}, f32[4,88,256]{2,1,0:T(8,128)}, f32[19,32,512]{2,1,0:T(8,128)}, f32[8,128]{1,0:T(8,128)}, bf16[4,4,2,352,256]{4,3,...) custom-call(s32[1]{0:T(128)S(6)} %copy.45.refs_0_, ...), custom_call_target="tpu_custom_call" | custom-call | tf_op jit(solution)/shard_map/pallas_call | solution.py:1439
  337.8 0.0 copy-start.1
  337.8 1.8 copy.42
  339.6 1.3 slice_bitcast_fusion.8
  341.0 1.3 slice_bitcast_fusion.6
  342.3 1.1 slice_bitcast_fusion.2
  343.5 0.0 copy-start
  343.5 1.3 slice_bitcast_fusion
  344.8 0.8 copy.41
  345.5 0.7 copy.39
  346.2 0.7 copy.38
  346.9 0.7 copy.37
  347.5 0.7 copy.36
  348.2 0.8 copy.40
  348.9 0.0 copy-done.1
  348.9 1.0 copy.46
  349.9 0.0 copy-done
  349.9 1.3 copy.47
Async XLA Ops:
  337.8 11.2 %copy-start.1 = (bf16[512,1024]{1,0:T(8,128)(2,1)S(1)}, bf16[512,1024]{1,0:T(8,128)(2,1)}, u32[]{:S(2)}) copy-start(bf16[512,1024]{1,0:T(8,128)(2,1)} %get-tuple-element.84) | copy-start | bytes 3145732
  343.5 6.5 %copy-start = (f32[512,1024]{1,0:T(8,128)S(1)}, f32[512,1024]{1,0:T(8,128)}, u32[]{:S(2)}) copy-start(f32[512,1024]{1,0:T(8,128)} %get-tuple-element.85) | copy-start | bytes 6291460

commit v4 on v3

--- a/solution.py
+++ b/solution.py
@@ -13,9 +13,11 @@
 IMG = 196
 RING = 6
 SCATTER_COPIES = 10
-LAGS = 4
-FFN_LAG = 8
+LAG = (0, 1, 2, 4, 6)
+LAGS = LAG[-1]
+FFN_LAG = 4
 BACK_QB = 16
+DOWN_PIECE = 256
 TILE = 256
 QB = 8
 GELU_SCALE = 0.7978845608028654
@@ -276,8 +278,9 @@
 
 
 class Gather:
-    def __init__(self, links, shard, full, rows, parts, local_sem, line=None, merged=None):
+    def __init__(self, links, shard, full, rows, window, parts, local_sem, line=None, merged=None):
         self.links, self.shard, self.full, self.rows, self.parts = links, shard, full, rows, parts
+        self.window = window
         self.local_sem, self.line, self.merged = local_sem, line, merged
         nn = links.nn
         self.block = rows * nn
@@ -292,13 +295,11 @@
     def place(self, w, z):
         if self.line is not None:
             return self.line.at[z]
-        return self.full.at[pl.ds((w * self.links.nn + z) * self.rows, self.rows)]
+        return self.full.at[pl.ds((w * self.links.nn + z) * self.rows, self.rows), pl.ds(*self.window)]
 
     def span(self, mask, part=None):
         rows = pl.ds(jnp.bitwise_xor(self.links.w, mask) * self.block, self.block)
-        if part is None:
-            return self.full.at[rows]
-        low, size = self.parts[part][:2]
+        low, size = self.window if part is None else self.parts[part][:2]
         return self.full.at[rows, pl.ds(low, size)]
 
     def own(self):
@@ -365,9 +366,101 @@
             k.copy(place, place, number, k.wide(1)).wait_recv()
 
 
-def halves(columns):
+def halves(columns, first=0):
     low = columns // 256 * 128
-    return ((0, low, PARTS[0]), (low, columns - low, PARTS[1]))
+    return ((first, low, PARTS[0]), (first + low, columns - low, PARTS[1]))
+
+
+class GatherSquare:
+    def __init__(self, links, shard, full, rows, window, local_sem, square, lines, merged):
+        self.links, self.shard, self.full, self.rows, self.window = links, shard, full, rows, window
+        self.square, self.lines, self.merged, self.local_sem = square, lines, merged, local_sem
+        self.parts = halves(window[1])
+        self.block = rows * links.nn
+        self.part_ids = {
+            (p, mask): links.fresh()
+            for p in range(len(self.parts))
+            for mask in (X_BIT, Y_BIT, X_BIT | Y_BIT)
+        }
+        self.line_ids = [links.fresh() for _ in range(1, links.nn)]
+        self.core_ids = [links.fresh() for _ in range(square.shape[0])]
+
+    def spot(self, mask, p):
+        low, size = self.parts[p][:2]
+        return self.square.at[jnp.bitwise_xor(self.links.w, mask) // 2, :, pl.ds(low, size)]
+
+    def own(self):
+        return pltpu.make_async_copy(
+            self.shard, self.square.at[self.links.w // 2], self.local_sem.at[0]
+        )
+
+    def start(self):
+        k = self.links
+        self.own().start()
+        for p, (low, size, order) in enumerate(self.parts):
+            for bit in order:
+                k.send(self.shard.at[:, pl.ds(low, size)], self.spot(0, p), self.part_ids[p, bit], k.wide(bit))
+
+    def arrive(self, p, mask):
+        k = self.links
+        k.copy(self.spot(mask, p), self.spot(mask, p), self.part_ids[p, mask], k.wide(X_BIT)).wait_recv()
+
+    def forward(self):
+        k = self.links
+        for p, (low, size, (first, second)) in enumerate(self.parts):
+            self.arrive(p, first)
+            k.send(self.spot(first, p), self.spot(first, p), self.part_ids[p, first | second], k.wide(second))
+        for p, (low, size, (first, second)) in enumerate(self.parts):
+            self.arrive(p, second)
+
+    def keep(self):
+        return pltpu.make_async_copy(self.square, self.lines.at[self.links.z], self.local_sem.at[0])
+
+    def line(self):
+        k = self.links
+        self.own().wait()
+        for p in range(len(self.parts)):
+            self.arrive(p, X_BIT | Y_BIT)
+        self.keep().start()
+        for step in range(1, k.nn):
+            k.send(self.square, self.lines.at[k.z], self.line_ids[step - 1], k.along(step))
+
+    def rows_of(self, square, core):
+        rows = pl.ds((square * 2 + core) * self.block, self.block)
+        return self.full.at[rows, pl.ds(*self.window)]
+
+    def out(self, square):
+        core = lax.rem(self.links.w, 2)
+        return pltpu.make_async_copy(
+            self.merged.at[square], self.rows_of(square, core), self.local_sem.at[1 + square]
+        )
+
+    def join(self):
+        k = self.links
+        self.keep().wait()
+        for step in range(1, k.nn):
+            came = lax.rem(k.z - step + k.nn, k.nn)
+            k.copy(self.square, self.lines.at[came], self.line_ids[step - 1], k.along(step)).wait_recv()
+
+        def one(square, carry):
+            whole = jnp.concatenate(
+                [self.lines[z, square, : self.rows].astype(F32) for z in range(k.nn)], axis=0
+            )
+            self.merged[square] = whole.astype(BF)
+            return carry
+
+        lax.fori_loop(0, self.merged.shape[0], one, 0)
+        core = lax.rem(k.w, 2)
+        for square, number in enumerate(self.core_ids):
+            self.out(square).start()
+            k.send(self.merged.at[square], self.rows_of(square, core), number, k.wide(1))
+
+    def done(self):
+        k = self.links
+        core = lax.rem(k.w, 2)
+        for square, number in enumerate(self.core_ids):
+            self.out(square).wait()
+            k.copy(self.merged.at[square], self.rows_of(square, 1 - core), number, k.wide(1)).wait_recv()
 
 
 def dot(left, right):
@@ -425,13 +518,12 @@
 
 def forward_kernel(nn, shapes, *refs):
     count = len(shapes)
-    occupied, tokens, rel_hbm, lay_hbm = refs[:4]
-    shards = refs[4 : 4 + count]
-    refs = refs[4 + count :]
+    occupied, tokens, rel_hbm, lay_hbm, cotangent = refs[:5]
+    shards = refs[5 : 5 + count]
+    refs = refs[5 + count :]
     fulls, refs = refs[:count], refs[count:]
-    saved, refs = refs[:10], refs[10:]
-    (out_h, na_t, q_t, k_h, v_h, att_t, hid_h, nf_t, mix_t, probs_h) = saved
-    (slope_h, act_h), refs = refs[:2], refs[2:]
+    (grad_h, na_t, q_t, k_h, v_h, att_t, hid_h, nf_t, mix_h, probs_h, slope_h, act_h) = refs[:12]
+    down_grads, down_came, refs = refs[12], refs[13], refs[14:]
     (
         line,
         merged,
@@ -455,7 +547,8 @@
         probs,
         w_one,
         w_wide,
-        w_down,
+        grad,
+        down_stage,
         gains,
         turned,
         mixed_t,
@@ -464,6 +557,10 @@
         gather_sem,
         local_sem,
         ring_sem,
+        rest_square,
+        rest_lines,
+        rest_merged,
+        rest_sem,
     ) = refs
     slots, width = x.shape
     links = Links(nn, send_sem, recv_sem)
@@ -475,33 +572,51 @@
         return copy
 
     arriving = [move(tokens, x), move(rel_hbm, rel), move(lay_hbm, lay)]
+    grad_in = move(cotangent, grad)
     links.greet()
     g = []
     for index, (rows, columns) in enumerate(shapes):
         odd = rows % 16 != 0 and columns > 128
+        columns = columns // 2 if odd else columns
         g.append(
             Gather(
                 links,
-                shards[index],
+                shards[index].at[:, pl.ds(0, columns)] if odd else shards[index],
                 fulls[index],
                 rows,
+                (0, columns),
                 halves(columns) if columns > 128 else ((0, columns, PARTS[0]),),
                 gather_sem.at[index],
                 line if odd else None,
                 merged if odd else None,
             )
         )
+    rows, columns = shapes[-1]
+    rest = GatherSquare(
+        links,
+        shards[-1].at[:, pl.ds(columns // 2, columns // 2)],
+        fulls[-1],
+        rows,
+        (columns // 2, columns // 2),
+        rest_sem,
+        rest_square,
+        rest_lines,
+        rest_merged,
+    )
+    down_ids = [links.fresh() for _ in range(down_grads.shape[0])]
     SMALL, Q, K, V, O, GATE, UP, DOWN = range(8)
     g[SMALL].start()
     g[Q].start()
-    g[K].start()
+    rest.start()
     g[SMALL].spread()
     g[SMALL].forward()
+    g[K].start()
+    g[Q].spread()
+    g[V].start()
     g[SMALL].last()
     g[SMALL].done()
+    rest.forward()
     small_in = move(fulls[SMALL], small)
-    g[Q].spread()
-    g[V].start()
     leaving = []
     turning = {}
 
@@ -544,22 +659,22 @@
         return carry
 
     blocks = slots // QB
-    lax.fori_loop(0, blocks // 4, bias_block, 0)
     g[K].spread()
     g[O].start()
+    g[GATE].start()
     g[Q].forward()
-    lax.fori_loop(blocks // 4, blocks // 2, bias_block, 0)
+    lax.fori_loop(0, blocks // 3, bias_block, 0)
     g[V].spread()
-    g[GATE].start()
     g[K].forward()
     g[Q].last()
-    lax.fori_loop(blocks // 2, 3 * blocks // 4, bias_block, 0)
+    lax.fori_loop(blocks // 3, 2 * blocks // 3, bias_block, 0)
     g[O].spread()
+    g[UP].start()
     g[V].forward()
     g[K].last()
     g[Q].done()
     fetch = move(fulls[Q], w_one.at[0])
-    lax.fori_loop(3 * blocks // 4, blocks, bias_block, 0)
+    lax.fori_loop(2 * blocks // 3, blocks, bias_block, 0)
     fetch.wait()
 
     def project(slot, target):
@@ -573,7 +688,7 @@
     project(0, q)
     turn_out(1, q, q_t)
     g[GATE].spread()
-    g[UP].start()
+    g[DOWN].start()
     g[O].forward()
     g[V].last()
     g[K].done()
@@ -581,12 +696,12 @@
     fetch.wait()
     project(1, k)
     leaving.append(move(k, k_h))
-    g[O].last()
     g[V].done()
     fetch = move(fulls[V], w_one.at[0])
     fetch.wait()
     project(0, v)
     leaving.append(move(v, v_h))
+    g[O].last()
 
     def probs_out(pair):
         turn = lax.rem(pair, 2)
@@ -616,20 +731,14 @@
         return carry
 
     pairs = H // 2
-    lax.fori_loop(0, 2, attend, 0)
+    lax.fori_loop(0, 4, attend, 0)
     g[UP].spread()
-    g[DOWN].start()
+    rest.line()
     g[GATE].forward()
     g[O].done()
     fetch_o = move(fulls[O], w_one.at[1])
-    lax.fori_loop(2, 5, attend, 0)
-    g[GATE].last()
-    lax.fori_loop(5, pairs, attend, 0)
+    lax.fori_loop(4, pairs, attend, 0)
     turn_out(0, att, att_t)
-    g[DOWN].spread()
-    g[UP].forward()
-    g[GATE].done()
-    fetch_gate = move(fulls[GATE], w_wide.at[0])
     fetch_o.wait()
 
     def output_tile(tile, carry):
@@ -649,11 +758,47 @@
 
     lax.fori_loop(0, slots // 64, normalise_two, 0)
     turn_out(1, nf, nf_t)
+    g[UP].forward()
+    g[DOWN].spread()
+    g[GATE].last()
+    g[GATE].done()
+    fetch_gate = move(fulls[GATE], w_wide.at[0])
+    grad_in.wait()
+    valid_rows = iota((slots, 1), 0) < occupied[0] + IMG
+
+    def keep_valid(tile, carry):
+        at = pl.ds(pl.multiple_of(tile * TILE, TILE), TILE)
+        grad[:, at] = jnp.where(valid_rows, grad[:, at].astype(F32), 0.0).astype(BF)
+        return carry
+
+    lax.fori_loop(0, width // TILE, keep_valid, 0)
+    leaving.append(move(grad, grad_h))
+    fetch_gate.wait()
+    ffn = mixed_t.shape[0]
+    tiles = ffn // TILE
+    across = slots // TILE
+
+    def gate_spot(tile, second):
+        at = pl.ds(pl.multiple_of(lax.rem(tile, across) * TILE, TILE), TILE)
+        return bias.at[tile // across + second * (-(-tiles // across)), :, at]
+
+    def gate_tile(tile, carry):
+        at = pl.ds(pl.multiple_of(tile * TILE, TILE), TILE)
+        gate = dot(nf[...], w_wide[0, :, at])
+        square = gate * gate
+        inner = GELU_SCALE * gate * (1.0 + GELU_CUBE * square)
+        bend = jnp.tanh(inner)
+        half = 0.5 * (1.0 + bend)
+        gate_spot(tile, 0)[...] = gate * half
+        gate_spot(tile, 1)[...] = half + 0.5 * gate * (1.0 - bend * bend) * GELU_SCALE * (
+            1.0 + 3.0 * GELU_CUBE * square
+        )
+        return carry
+
+    lax.fori_loop(0, tiles, gate_tile, 0)
     g[UP].last()
-    g[DOWN].forward()
     g[UP].done()
     fetch_up = move(fulls[UP], w_wide.at[1])
-    fetch_gate.wait()
     fetch_up.wait()
 
     def ffn_out(tile):
@@ -662,7 +807,7 @@
         return (
             pltpu.make_async_copy(slope.at[turn], slope_h.at[:, at], ring_sem.at[2 + turn]),
             pltpu.make_async_copy(act.at[turn], act_h.at[:, at], ring_sem.at[4 + turn]),
-            pltpu.make_async_copy(mixed_t.at[turn], mix_t.at[at], ring_sem.at[6 + turn]),
+            pltpu.make_async_copy(mix.at[turn], mix_h.at[:, at], ring_sem.at[6 + turn]),
         )
 
     def ffn_tile(tile, carry):
@@ -673,39 +818,62 @@
 
         at = pl.ds(pl.multiple_of(tile * TILE, TILE), TILE)
         turn = lax.rem(tile, 2)
-        gate = dot(nf[...], w_wide[0, :, at])
         up = dot(nf[...], w_wide[1, :, at])
-        square = gate * gate
-        inner = GELU_SCALE * gate * (1.0 + GELU_CUBE * square)
-        bend = jnp.tanh(inner)
-        half = 0.5 * (1.0 + bend)
-        active = gate * half
-        rise = half + 0.5 * gate * (1.0 - bend * bend) * GELU_SCALE * (1.0 + 3.0 * GELU_CUBE * square)
+        active = gate_spot(tile, 0)[...]
+        rise = gate_spot(tile, 1)[...]
         mixed = (active * up).astype(BF)
-        mix[:, at] = mixed
-        mixed_t[turn] = mixed.T
+        mix[turn] = mixed
+        mixed_t[at, :] = mixed.T
         act[turn] = active.astype(BF)
         slope[turn] = (up * rise).astype(BF)
         for copy in ffn_out(tile):
             copy.start()
         return carry
 
-    tiles = mix.shape[1] // TILE
-    lax.fori_loop(0, tiles // 2, ffn_tile, 0)
+    lax.fori_loop(0, tiles, ffn_tile, 0)
+    g[DOWN].forward()
+    block = down_stage.shape[3]
+    piece = down_stage.shape[4]
+
+    def down_copy(chunk):
+        turn = lax.rem(chunk, 2)
+        return pltpu.make_async_copy(down_stage.at[turn], down_grads.at[chunk], ring_sem.at[8 + turn])
+
+    def down_chunk(chunk, carry):
+        at = pl.ds(pl.multiple_of(chunk * piece, piece), piece)
+
+        def one(index, carry):
+            rows = pl.ds(pl.multiple_of(index * block, 16), block)
+            down_stage[lax.rem(chunk, 2), index // 2, lax.rem(index, 2)] = dot(
+                mixed_t[rows, :], grad[:, at]
+            ).astype(BF)
+            return carry
+
+        lax.fori_loop(0, ffn // block, one, 0)
+        down_copy(chunk).start()
+        return carry
+
+    def down_trade(chunk):
+        core = lax.rem(links.w, 2)
+        return links.copy(
+            down_grads.at[chunk, :, 1 - core], down_came.at[chunk], down_ids[chunk], links.wide(1)
+        )
+
+    chunks = width // piece
+    for chunk in range(chunks):
+        down_chunk(jnp.int32(chunk), 0)
+        if chunk == 1:
+            rest.join()
+        if chunk >= 1:
+            down_copy(chunk - 1).wait()
+            down_trade(chunk - 1).start()
     g[DOWN].last()
-    lax.fori_loop(tiles // 2, tiles, ffn_tile, 0)
+    down_copy(chunks - 1).wait()
+    down_trade(chunks - 1).start()
     g[DOWN].done()
-    move(fulls[DOWN], w_down).wait()
-    valid_rows = iota((slots, 1), 0) < occupied[0] + IMG
-
-    def down_tile(tile, carry):
-        at = pl.ds(pl.multiple_of(tile * TILE, TILE), TILE)
-        result = hid[:, at] + dot(mix[...], w_down[:, at])
-        na[:, at] = jnp.where(valid_rows, result, 0.0).astype(BF)
-        return carry
-
-    lax.fori_loop(0, width // TILE, down_tile, 0)
-    move(na, out_h).wait()
+    rest.done()
+    for chunk in range(chunks):
+        down_trade(chunk).wait()
     for copy in leaving + list(turning.values()):
         copy.wait()
     for pair in (pairs - 2, pairs - 1):
@@ -716,14 +884,14 @@
     links.finish()
 
 
-def forward_all(nw, nn, counts, tokens, rel, lay, shards, odd_rows):
+def forward_all(nw, nn, counts, tokens, rel, lay, cotangent, shards, odd_rows):
     devices = nw * nn
     shapes = []
     for index, shard in enumerate(shards):
         rows = odd_rows if index == len(shards) - 1 else shard.shape[0]
         shapes.append((rows, shard.shape[1]))
-    copies = len(shards) * (nn - 1 + 6 + 4)
     slots, width = tokens.shape
+    copies = (len(shards) + 1) * (nn - 1 + 6 + nw // 2) + width // DOWN_PIECE
     ffn = shapes[5][1]
     low = jax.ShapeDtypeStruct((slots, width), BF)
     wide = jax.ShapeDtypeStruct((slots, ffn), BF)
@@ -733,19 +901,22 @@
         for (rows, columns), shard in zip(shapes, shards)
     ]
     low_t = jax.ShapeDtypeStruct((width, slots), BF)
-    wide_t = jax.ShapeDtypeStruct((ffn, slots), BF)
-    out_shape += [low, low_t, low_t, low, low, low_t, full, low_t, wide_t]
+    out_shape += [low, low_t, low_t, low, low, low_t, full, low_t, wide]
     out_shape += [jax.ShapeDtypeStruct((H, slots, slots), BF), wide, wide]
+    down = (nw // 2, 2, nn * odd_rows, DOWN_PIECE)
+    out_shape += [jax.ShapeDtypeStruct((width // DOWN_PIECE,) + down, BF)]
+    out_shape += [jax.ShapeDtypeStruct((width // DOWN_PIECE, nw // 2, nn * odd_rows, DOWN_PIECE), BF)]
+    half = (shards[-1].shape[0], shards[-1].shape[1] // 2)
     hbm = pl.BlockSpec(memory_space=pl.ANY)
     page = pltpu.VMEM((slots, width), BF)
     return pl.pallas_call(
         functools.partial(forward_kernel, nn, shapes),
         out_shape=out_shape,
-        in_specs=[pl.BlockSpec(memory_space=pltpu.SMEM)] + [hbm] * (3 + len(shards)),
+        in_specs=[pl.BlockSpec(memory_space=pltpu.SMEM)] + [hbm] * (4 + len(shards)),
         out_specs=[hbm] * len(out_shape),
         scratch_shapes=[
-            pltpu.VMEM((nn,) + shards[-1].shape, BF),
-            pltpu.VMEM((nn * odd_rows, shards[-1].shape[1]), BF),
+            pltpu.VMEM((nn,) + half, BF),
+            pltpu.VMEM((nn * odd_rows, half[1]), BF),
             page,
             pltpu.VMEM((slots, slots), jnp.int32),
             pltpu.VMEM((slots, slots), jnp.int32),
@@ -760,34 +931,40 @@
             page,
             pltpu.VMEM((slots, width), F32),
             page,
-            pltpu.VMEM((slots, ffn), BF),
+            pltpu.VMEM((2, slots, TILE), BF),
             pltpu.VMEM((2, slots, TILE), BF),
             pltpu.VMEM((2, slots, TILE), BF),
             pltpu.VMEM((2, 2, slots, slots), BF),
             pltpu.VMEM((2, width, width), BF),
             pltpu.VMEM((2, width, ffn), BF),
-            pltpu.VMEM((ffn, width), BF),
+            page,
+            pltpu.VMEM((2,) + down, BF),
             pltpu.VMEM((8, width), F32),
             pltpu.VMEM((2, width, slots), BF),
-            pltpu.VMEM((2, TILE, slots), BF),
+            pltpu.VMEM((ffn, slots), BF),
             pltpu.SemaphoreType.DMA((copies,)),
             pltpu.SemaphoreType.DMA((copies,)),
             pltpu.SemaphoreType.DMA((len(shards),)),
             pltpu.SemaphoreType.DMA((64,)),
-            pltpu.SemaphoreType.DMA((8,)),
+            pltpu.SemaphoreType.DMA((10,)),
+            pltpu.VMEM((nw // 2,) + half, BF),
+            pltpu.VMEM((nn, nw // 2) + half, BF),
+            pltpu.VMEM((nw // 2, nn * odd_rows, half[1]), BF),
+            pltpu.SemaphoreType.DMA((1 + nw // 2,)),
         ],
         compiler_params=pltpu.CompilerParams(
             collective_id=0, has_side_effects=True, vmem_limit_bytes=63 * 2**20
         ),
-    )(counts, tokens, rel, lay, *shards)
+    )(counts, tokens, rel, lay, cotangent, *shards)
 
 
 class Scatter:
-    def __init__(self, links, chunks, rows, columns, grads, came, slots, base):
+    def __init__(self, links, chunks, rows, columns, grads, came, slots, base, traded=False):
         self.links, self.chunks, self.rows, self.columns = links, chunks, rows, columns
         self.grads, self.came = grads, came
         (self.held, self.other, self.round, self.out_line, self.in_line, self.load_sem) = slots
         self.base = base
+        self.traded = traded
         self.block = rows * links.nn
         self.parts = halves(columns)
         self.core = lax.rem(links.w, 2)
@@ -819,7 +996,8 @@
         )
 
     def fetch(self, chunk):
-        self.core_copy(chunk).wait_recv()
+        if not self.traded:
+            self.core_copy(chunk).wait_recv()
         for load in self.loads(chunk):
             load.start()
 
@@ -897,6 +1075,11 @@
                 ].astype(BF)
         for step in range(1, self.links.nn):
             self.line_copy(chunk, step).start()
+        if not self.traded:
+            self.core_copy(chunk).wait_send()
+        for p in range(len(self.parts)):
+            for mask in (X_BIT, Y_BIT, X_BIT | Y_BIT):
+                self.hop(chunk, p, mask).wait_send()
 
     def total(self, chunk):
         slot = lax.rem(chunk, self.ring)
@@ -910,7 +1093,8 @@
         index = jnp.int32(index)
         made = self.chunks if made is None else made
         idle = index >= made if made < self.chunks else False
-        for lag, action in enumerate((self.fetch, self.add_core, self.add_corner, self.add_square, self.finish)):
+        steps = (self.fetch, self.add_core, self.add_corner, self.add_square, self.finish)
+        for lag, action in zip(LAG, steps):
             chunk = index - lag
             ready = jnp.logical_and(chunk >= 0, chunk < self.chunks)
             if made < self.chunks:
@@ -922,13 +1106,6 @@
 
     def finish(self, chunk, out):
         out[chunk] = self.total(chunk)
-        self.wait_sent(chunk)
-
-    def wait_sent(self, chunk):
-        self.core_copy(chunk).wait_send()
-        for p, part in enumerate(self.parts):
-            for mask in (X_BIT, Y_BIT, X_BIT | Y_BIT):
-                self.hop(chunk, p, mask).wait_send()
         for step in range(1, self.links.nn):
             self.line_copy(chunk, step).wait_send()
 
@@ -1018,7 +1195,7 @@
         tokens,
         rel_hbm,
         lay_hbm,
-        cotangent,
+        grad_h,
         small_h,
         query_h,
         key_h,
@@ -1034,14 +1211,16 @@
         att_t,
         hid_h,
         nf_t,
-        mix_t,
+        mix_h,
         probs_h,
         slope_h,
         act_h,
-    ) = refs[:23]
-    refs = refs[23:]
-    (rows_out, few_out, many_out, small_out, few_grads, many_grads, few_came, many_came) = refs[:8]
-    few_slots, many_slots, refs = refs[8:14], refs[14:20], refs[20:]
+        few_grads,
+        few_came,
+    ) = refs[:25]
+    refs = refs[25:]
+    (out_h, rows_out, few_out, many_out, small_out, many_grads, many_came) = refs[:7]
+    few_slots, many_slots, refs = refs[7:13], refs[13:19], refs[19:]
     (
         x,
         rel,
@@ -1050,7 +1229,6 @@
         gains,
         grad,
         left,
-        left_att,
         acc,
         hid,
         wd_s,
@@ -1058,7 +1236,6 @@
         wu_s,
         slope_s,
         act_s,
-        few_stage,
         many_stage,
         branch,
         w_one,
@@ -1069,9 +1246,6 @@
         v,
         probs,
         pieces,
-        dq,
-        dkt,
-        dvt,
         onehot,
         table,
         sums,
@@ -1096,10 +1270,9 @@
         copy.start()
         return copy
 
-    ffn = mix_t.shape[0]
+    ffn = mix_h.shape[1]
     tiles = ffn // TILE
-    mix_in = move(mix_t, pieces.at[pl.ds(0, ffn)])
-    grad_in = move(cotangent, grad)
+    grad_in = move(grad_h, grad)
     nf_in = move(nf_t, left)
 
     def tile_copies(tile):
@@ -1120,61 +1293,20 @@
 
     for copy in tile_copies(0):
         copy.start()
-    later = [move(hid_h, hid), move(small_h, small), move(att_t, left_att), move(output_h, w_one.at[0])]
+    later = [move(hid_h, hid), move(small_h, small), move(att_t, pull_t), move(output_h, w_one.at[0])]
     later += [move(q_t, qt), move(k_h, k), move(v_h, v)]
     last = [move(tokens, x), move(rel_hbm, rel), move(lay_hbm, lay), move(value_h, w_one.at[1])]
     links.greet()
-    few = Scatter(links, *few_facts, few_grads, few_came, few_slots, 0)
+    few = Scatter(links, *few_facts, few_grads, few_came, few_slots, 0, traded=True)
     base = few_facts[0] * SCATTER_COPIES
     many = Scatter(links, *many_facts, many_grads, many_came, many_slots, base)
     links.used = base + many_facts[0] * SCATTER_COPIES
 
-    def stage_copy(scatter, stage, chunk, first):
+    def many_copy(chunk):
         turn = lax.rem(chunk, 2)
-        return pltpu.make_async_copy(
-            stage.at[turn], scatter.grads.at[chunk], stage_sem.at[first + turn]
-        )
-
-    def few_copy(chunk):
-        return stage_copy(few, few_stage, chunk, 0)
-
-    def many_copy(chunk):
-        return stage_copy(many, many_stage, chunk, 2)
+        return pltpu.make_async_copy(many_stage.at[turn], many.grads.at[chunk], stage_sem.at[turn])
 
     grad_in.wait()
-    valid_rows = iota((slots, 1), 0) < occupied[0] + IMG
-
-    def keep_valid(tile, carry):
-        at = pl.ds(pl.multiple_of(tile * TILE, TILE), TILE)
-        grad[:, at] = jnp.where(valid_rows, grad[:, at].astype(F32), 0.0).astype(BF)
-        return carry
-
-    lax.fori_loop(0, width // TILE, keep_valid, 0)
-    mix_in.wait()
-    block = few.block
-
-    def down_chunk(chunk, carry):
-        at = pl.ds(pl.multiple_of(chunk * few.columns, few.columns), few.columns)
-        turn = lax.rem(chunk, 2)
-
-        def one(index, carry):
-            rows = pl.ds(pl.multiple_of(index * block, 16), block)
-            few_stage[turn, index // 2, lax.rem(index, 2)] = dot(pieces[rows, :], grad[:, at]).astype(BF)
-            return carry
-
-        lax.fori_loop(0, ffn // block, one, 0)
-        few_copy(chunk).start()
-
-        @pl.when(chunk >= 1)
-        def _():
-            few_copy(chunk - 1).wait()
-            few.trade(chunk - 1)
-
-        return carry
-
-    lax.fori_loop(0, few.chunks, down_chunk, 0)
-    few_copy(few.chunks - 1).wait()
-    few.trade(few.chunks - 1)
     nf_in.wait()
 
     def put(chunk, low, value):
@@ -1247,7 +1379,7 @@
 
     wide = many.columns
     for part in range(width // wide):
-        emit(tiles + part, dot(left_att[...], branch[:, part * wide : (part + 1) * wide]))
+        emit(tiles + part, dot(pull_t[...], branch[:, part * wide : (part + 1) * wide]))
     many.pump(done, many_out)
     done += 1
 
@@ -1293,30 +1425,39 @@
             pieces[pl.ds(pl.multiple_of(head * slots, slots), slots), :] = piece
             found.append(dot(piece, keys))
             rows = pl.ds(pl.multiple_of(head * HD, HD), HD)
-            dkt[rows, :] = dot(qt[rows, :], piece).astype(BF)
-            dvt[rows, :] = dot(pull_t[rows, :], share).astype(BF)
-        dq[:, at] = jnp.where(low, found[0], found[1]).astype(BF)
-        many.pump(done + pair, many_out, made)
+            qt[rows, :] = dot(qt[rows, :], piece).astype(BF)
+            pull_t[rows, :] = dot(pull_t[rows, :], share).astype(BF)
+        pull[:, at] = jnp.where(low, found[0], found[1]).astype(BF)
         return carry
 
-    lax.fori_loop(0, pairs, attend_back, 0)
-    done = min(done + pairs, made)
-    for copy in last:
-        copy.wait()
-    na_in.wait()
-    for index, (grads, turned) in enumerate(((dvt, True), (dq, False), (dkt, True))):
-        for part in range(width // wide):
-            at = slice(part * wide, (part + 1) * wide)
-            chunk = made + index * (width // wide) + part
-            if index or part:
+    for half in range(width // wide):
+        heads = pairs * wide // width
+        first = done - half * heads
+
+        def attend_pump(pair, carry, first=first, made=made):
+            attend_back(pair, 0)
+            many.pump(first + pair, many_out, made)
+            return carry
+
+        lax.fori_loop(half * heads, (half + 1) * heads, attend_pump, 0)
+        done = done + heads if made == many.chunks else min(done + heads, made)
+        if half == 0:
+            for copy in last:
+                copy.wait()
+            na_in.wait()
+        at = slice(half * wide, (half + 1) * wide)
+        for part, (grads, turned) in enumerate(((pull_t, True), (pull, False), (qt, True))):
+            chunk = tiles + width // wide + half * 3 + part
+            if part:
                 flush(chunk - 1)
             if turned:
                 emit(chunk, dot_nt(left[...], grads[at, :]))
             else:
                 emit(chunk, dot(left[...], grads[:, at]))
+        flush(chunk)
         many.pump(done, many_out, made)
-        done = min(done + 1, made)
-    flush(many.chunks - 1)
+        done = done + 1 if made == many.chunks else min(done + 1, made)
+        made = min(made + 3, many.chunks)
     table[...] = jnp.zeros_like(table)
 
     def table_block_back(index, carry):
@@ -1335,8 +1476,7 @@
         return carry
 
     blocks = slots // BACK_QB
-    groups = 8
-
+    groups = 4
     def table_group(group, carry):
         lax.fori_loop(group * (blocks // groups), (group + 1) * (blocks // groups), table_block_back, 0)
         many.pump(done + group, many_out)
@@ -1344,19 +1484,30 @@
 
     lax.fori_loop(0, groups, table_group, 0)
     done += groups
+    whole = ffn // slots
+    output_in = [
+        move(down_h.at[:, pl.ds(part * slots, slots)], pieces.at[pl.ds(part * ffn, ffn)])
+        for part in range(width // slots)
+    ]
+    first_mix = width // slots * ffn
+    output_in += [
+        move(mix_h.at[:, pl.ds(part * slots, slots)], pieces.at[pl.ds(first_mix + part * slots, slots)])
+        for part in range(whole)
+    ]
+    output_in.append(move(mix_h.at[:, pl.ds(whole * slots, TILE)], slope_s.at[0]))
     query_in.wait()
 
     def turn_back(tile, carry):
         at = pl.ds(pl.multiple_of(tile * TILE, TILE), TILE)
-        pull[:, at] = dvt[at, :].T
-        branch[:, at] = dkt[at, :].T
+        v[:, at] = pull_t[at, :].T
+        branch[:, at] = qt[at, :].T
         return carry
 
     lax.fori_loop(0, width // TILE, turn_back, 0)
 
     def first_two(tile, carry):
         at = pl.ds(pl.multiple_of(tile * TILE, TILE), TILE)
-        acc[:, at] = dot_nt(pull[...], w_one[1, at, :]) + dot_nt(dq[...], w_one[0, at, :])
+        acc[:, at] = dot_nt(v[...], w_one[1, at, :]) + dot_nt(pull[...], w_one[0, at, :])
         return carry
 
     lax.fori_loop(0, width // TILE, first_two, 0)
@@ -1382,6 +1533,7 @@
 
     sums[1] = lax.fori_loop(0, slots // 64, norm_one, zero)
     rows_copy = move(hid, rows_out)
+    output_in.append(move(hid_h, acc))
     total = table[...]
     mine = iota(total.shape, 0) // (2 * NB) == lax.rem(iota(total.shape, 1), BACK_QB)
     folded = jnp.sum(
@@ -1405,12 +1557,36 @@
         small_grads[wide_at // 2, wide_at % 2, z * 8 : z * 8 + 1, :] = packed[device : device + 1]
     scatter_small(links, small_grads, small_out, small_came, small_round, small_line, small_mine)
 
+    for copy in output_in:
+        copy.wait()
+    valid_rows = iota((slots, 1), 0) < occupied[0] + IMG
+
+    def output_tile(tile, carry):
+        at = pl.ds(pl.multiple_of(tile * TILE, TILE), TILE)
+        part, column = tile // (slots // TILE), lax.rem(tile, slots // TILE) * TILE
+        column = pl.ds(pl.multiple_of(column, TILE), TILE)
+        total = acc[:, at]
+        for index in range(whole):
+            rows = pl.ds(pl.multiple_of(part * ffn + index * slots, TILE), slots)
+            mixed = pieces[first_mix + index * slots : first_mix + (index + 1) * slots, :]
+            total = total + dot(mixed, pieces[rows, column])
+        rows = pl.ds(pl.multiple_of(part * ffn + whole * slots, TILE), TILE)
+        total = total + dot(slope_s[0], pieces[rows, column])
+        x[:, at] = jnp.where(valid_rows, total, 0.0).astype(BF)
+        many.pump(done + tile, many_out)
+        return carry
+
+    lax.fori_loop(0, width // TILE, output_tile, 0)
+    done += width // TILE
+    out_copy = move(x, out_h)
+
     def rest(index, carry):
         many.pump(index, many_out)
         return carry
 
     lax.fori_loop(done, many.chunks + LAGS, rest, 0)
     rows_copy.wait()
+    out_copy.wait()
     links.finish()
 
 
@@ -1419,16 +1595,15 @@
     devices = nw * nn
     slots, width = page[0].shape
     ffn = weights[5].shape[1]
-    few = (width // 256, ffn // devices, 256)
+    few = (width // DOWN_PIECE, ffn // devices, DOWN_PIECE)
     many = (ffn // TILE + 8, width // devices, 2 * TILE)
-    outs = [jax.ShapeDtypeStruct((slots, width), F32)]
+    outs = [jax.ShapeDtypeStruct((slots, width), BF), jax.ShapeDtypeStruct((slots, width), F32)]
     for chunks, rows, columns in (few, many):
         outs.append(jax.ShapeDtypeStruct((chunks, rows, columns), F32))
     outs.append(jax.ShapeDtypeStruct((8, 128), F32))
-    for chunks, rows, columns in (few, many):
-        outs.append(jax.ShapeDtypeStruct((chunks, squares, 2, nn * rows, columns), BF))
-    for chunks, rows, columns in (few, many):
-        outs.append(jax.ShapeDtypeStruct((chunks, squares, nn * rows, columns), BF))
+    chunks, rows, columns = many
+    outs.append(jax.ShapeDtypeStruct((chunks, squares, 2, nn * rows, columns), BF))
+    outs.append(jax.ShapeDtypeStruct((chunks, squares, nn * rows, columns), BF))
     copies = (few[0] + many[0]) * SCATTER_COPIES + 16
     vmem = pl.BlockSpec(memory_space=pltpu.VMEM)
     hbm = pl.BlockSpec(memory_space=pl.ANY)
@@ -1440,7 +1615,7 @@
         functools.partial(backward_kernel, nn, few, many),
         out_shape=outs,
         in_specs=[pl.BlockSpec(memory_space=pltpu.SMEM)] + [hbm] * (len(inputs) - 1),
-        out_specs=[hbm, vmem, vmem, vmem, hbm, hbm, hbm, hbm],
+        out_specs=[hbm, hbm, vmem, vmem, vmem, hbm, hbm],
         scratch_shapes=scatter_slots(squares, nn, few[1], few[2], few[0])
         + scatter_slots(squares, nn, many[1], many[2], RING)
         + [
@@ -1451,7 +1626,6 @@
             pltpu.VMEM((8, width), F32),
             low,
             turned,
-            turned,
             full,
             full,
             pltpu.VMEM((2, TILE, width), BF),
@@ -1459,7 +1633,6 @@
             pltpu.VMEM((2, width, TILE), BF),
             pltpu.VMEM((2, slots, TILE), BF),
             pltpu.VMEM((2, slots, TILE), BF),
-            pltpu.VMEM((2, squares, 2, nn * few[1], few[2]), BF),
             pltpu.VMEM((2, squares, 2, nn * many[1], many[2]), BF),
             low,
             pltpu.VMEM((2, width, width), BF),
@@ -1470,9 +1643,6 @@
             low,
             pltpu.VMEM((2, 2, slots, slots), BF),
             pltpu.VMEM((H * slots, slots), BF),
-            low,
-            turned,
-            turned,
             pltpu.VMEM((BACK_QB * 2 * NB, slots), BF),
             pltpu.VMEM((BACK_QB * 2 * NB, H * BACK_QB), F32),
             pltpu.VMEM((2, 8, width), F32),
@@ -1485,13 +1655,13 @@
             pltpu.SemaphoreType.DMA((copies,)),
             pltpu.SemaphoreType.DMA((64,)),
             pltpu.SemaphoreType.DMA((2, 5)),
-            pltpu.SemaphoreType.DMA((4,)),
+            pltpu.SemaphoreType.DMA((2,)),
             pltpu.SemaphoreType.DMA((2,)),
         ],
         compiler_params=pltpu.CompilerParams(
             collective_id=1, has_side_effects=True, vmem_limit_bytes=63 * 2**20
         ),
-    )(*inputs)[:4]
+    )(*inputs)[:5]
 
 
 def local_fast(
@@ -1519,19 +1689,18 @@
     down = jnp.pad(w_down, ((0, padded(w_down.shape[0]) - w_down.shape[0]), (0, 0)))
     page = (tokens, rel_bucket, lay_bucket)
     shards = [small, w_query, w_key, w_value, w_output, w_gate, w_up, down]
-    found = forward_all(nw, nn, ocr_counts, *page, shards, w_down.shape[0])
-    weights, output, saved = found[: len(shards)], found[len(shards)], found[len(shards) + 1 :]
-    grad_tokens, few, many, small = backward_all(
-        nw, nn, ocr_counts, page + (cotangent,), weights, saved
+    found = forward_all(nw, nn, ocr_counts, *page, cotangent, shards, w_down.shape[0])
+    weights, grad, saved = found[: len(shards)], found[len(shards)], found[len(shards) + 1 :]
+    output, grad_tokens, few, many, small = backward_all(
+        nw, nn, ocr_counts, page + (grad,), weights, saved
     )
 
     def join(stack):
         return jnp.moveaxis(stack, 0, 1).reshape(stack.shape[1], -1)
 
     tiles = w_gate.shape[1] // TILE
-    grad_output, grad_value, grad_query, grad_key = (
-        join(many[tiles + 2 * index : tiles + 2 * index + 2]) for index in range(4)
-    )
+    grad_output = join(many[tiles : tiles + 2])
+    grad_value, grad_query, grad_key = (join(many[tiles + 2 + part :: 3]) for part in range(3))
     gate, up = join(many[:tiles, :, :TILE]), join(many[:tiles, :, TILE:])
     cuts, at = [], 0
     for part in (gain_attn, gain_ffn, rel_table, lay_table):

time: 352 us -> 314 us (0.89)
  Pallas kernels: 333 us -> 295 us
    pallas_call x1, Pallas kernels: 158 us -> 139 us  [forward_all(): pl.pallas_call(functools.partial(forward_kernel, nn, shapes), out_shape=o...]
    pallas_call x1, Pallas kernels: 176 us -> 157 us  [backward_all(): pl.pallas_call(functools.partial(backward_kernel, nn, few, many), out_sha...]
where the time goes in v4:
time: 314 us; the launch traced here: 313 us
  Pallas kernels  295 us (94%)
  local copies, waits for them, and re-layouts  15 us (5%)
    pallas_call x1, Pallas kernels, backward_all(): pl.pallas_call(functools.partial(backward_kernel, nn, few, many), out_sha...  157 us
    pallas_call x1, Pallas kernels, forward_all(): pl.pallas_call(functools.partial(forward_kernel, nn, shapes), out_shape=o...  139 us

profile of v4, /device:TPU:0, one launch (start us, length us, event | category | flops | bytes accessed | tf_op | source)
XLA Modules:
  0.0 313.0 jit_solution(5421182928706033828)
XLA Ops:
  1.3 1.4 fusion.9.refs_5_
  2.7 1.6 pad.12.refs_12_
  4.3 138.5 %shard_map.255 = (f32[256,128]{1,0:T(8,128)}, bf16[1024,1024]{1,0:T(8,128)(2,1)}, bf16[1024,1024]{1,0:T(8,128)(2,1)}, bf16[1024,1024]{1,0:T(8,128)(2,1)}, bf16[1...) custom-call(s32[1]{0:T(128)S(6)} %copy.45.refs_0_, ...), custom_call_target="tpu_custom_call" | custom-call | tf_op jit(solution)/shard_map/pallas_call | solution.py:912
  142.8 156.8 %shard_map.256 = (bf16[512,1024]{1,0:T(8,128)(2,1)}, f32[512,1024]{1,0:T(8,128)}, f32[4,88,256]{2,1,0:T(8,128)}, f32[19,32,512]{2,1,0:T(8,128)}, f32[8,128]{1,0:...) custom-call(s32[1]{0:T(128)S(6)} %copy.45.refs_0_, bf16[512,1024]{1,0:T(8,128)(2,1)} %refs_1_.3, ...), custom_call_target="tpu_custom_call" | custom-call | tf_op jit(solution)/shard_map/pallas_call | solution.py:1614
  299.6 0.0 copy-start.1
  299.7 1.4 slice_bitcast_fusion.8
  301.0 1.3 slice_bitcast_fusion.6
  302.4 1.8 copy.42
  304.1 1.1 slice_bitcast_fusion.2
  305.3 0.0 copy-start
  305.3 1.3 slice_bitcast_fusion
  306.6 0.8 copy.41
  307.3 0.7 copy.39
  308.0 0.7 copy.38
  308.7 0.7 copy.37
  309.3 0.7 copy.36
  310.0 0.8 copy.40
  310.7 0.0 copy-done.1
  310.7 1.0 copy.46
  311.7 0.0 copy-done
  311.7 1.3 copy.47
Async XLA Ops:
  299.6 11.1 %copy-start.1 = (bf16[512,1024]{1,0:T(8,128)(2,1)S(1)}, bf16[512,1024]{1,0:T(8,128)(2,1)}, u32[]{:S(2)}) copy-start(bf16[512,1024]{1,0:T(8,128)(2,1)} %get-tuple-element.90) | copy-start | bytes 3145732
  305.3 6.5 %copy-start = (f32[512,1024]{1,0:T(8,128)S(1)}, f32[512,1024]{1,0:T(8,128)}, u32[]{:S(2)}) copy-start(f32[512,1024]{1,0:T(8,128)} %get-tuple-element.91) | copy-start | bytes 6291460
